TPU v7x, 128 devices: a whole 4x4x4 slice. The times are simulated.
128 devices in a mesh: term: 8 (over x_hi, y), sector: 16 (over x_lo, z, core).
Axes of the slice: x: 4 (x_hi: 2, x_lo: 2; x = x_hi * 2 + x_lo), y: 4, z: 4, core: 2. Of those that a mesh axis runs over, the one named last changes fastest.
Arguments:
- wavefunction: bfloat16 [16, 512, 512], P('sector'), may hold values from -6 to 6
- left_ops: bfloat16 [256, 512, 512], P(('term', 'sector')), may hold values from -0.125 to 0.125
- right_ops: bfloat16 [256, 512, 512], P(('term', 'sector')), may hold values from -0.125 to 0.125
- sector_dims: int32 [16], replicated, may hold values from 128 to 512, as said below
- coupling_source: int32 [3072], P(('term', 'sector')), may hold values from 0 to 15
- coupling_target: int32 [3072], P(('term', 'sector')), may hold values from 0 to 15
- coupling_operator: int32 [3072], P(('term', 'sector')), may hold values from 0 to 1
Outputs:
- sigma_blocks: float32 [16, 512, 512], P('sector')
Inputs may be any that keep to these rules, and one draw needn't show every extreme that they name: `sector_dims`: multiples of 128; at least one sector has dimension 512.
All inputs are finite; a program needn't handle non-finite values.
Results may differ from a plain program's by a relative error of at most 0.0029.
Values may be sent and summed in bfloat16 or wider, within the bound.
No kernel may reach another device: no remote copies, remote signals or barrier semaphores. Data moves between devices by JAX's collectives and lax.ppermute only.
A program may use at most 128 MiB of HBM per device.

v0:
```python
import jax
import jax.numpy as jnp
from jax import lax
from jax.sharding import PartitionSpec as P


def block_mask(dims_part, block_width):
    positions = jnp.arange(block_width, dtype=jnp.int32)
    kept_rows = positions[None, :] < dims_part[:, None]
    return kept_rows[:, :, None] & kept_rows[:, None, :]


def body(
    wavefunction,
    left_ops,
    right_ops,
    sector_dims,
    coupling_source,
    coupling_target,
    coupling_operator,
):
    gathered = lax.all_gather(wavefunction, "sector", axis=0, tiled=True)
    block_width = gathered.shape[1]
    sector_total = gathered.shape[0]
    masked_wave = gathered * block_mask(sector_dims, block_width).astype(jnp.bfloat16)

    def advance(blocks, coupling):
        source, target, chosen = coupling
        halfway = jnp.dot(
            left_ops[chosen], masked_wave[source], preferred_element_type=jnp.float32
        ).astype(jnp.bfloat16)
        contribution = jnp.dot(halfway, right_ops[chosen], preferred_element_type=jnp.float32)
        return (blocks.at[target].add(contribution), None)

    start_blocks = jnp.zeros((sector_total, block_width, block_width), jnp.float32)
    partial_blocks = lax.scan(
        advance, start_blocks, (coupling_source, coupling_target, coupling_operator)
    )[0]
    own_part = lax.psum_scatter(partial_blocks, "sector", scatter_dimension=0, tiled=True)
    summed = lax.psum(own_part, "term")
    sector_count = summed.shape[0]
    first_sector = lax.axis_index("sector") * sector_count
    own_dims = lax.dynamic_slice_in_dim(sector_dims, first_sector, sector_count)
    return summed * block_mask(own_dims, block_width).astype(jnp.float32)


def solution(mesh):
    placed = (
        P("sector", None, None),
        P(("term", "sector"), None, None),
        P(("term", "sector"), None, None),
        P(),
        P(("term", "sector")),
        P(("term", "sector")),
        P(("term", "sector")),
    )
    return jax.shard_map(
        body, mesh=mesh, in_specs=placed, out_specs=P("sector", None, None), check_vma=False
    )
```

profile of v0, /device:TPU:1, one launch (start us, length us, event | category | flops | bytes accessed | tf_op | source)
XLA Modules:
  0.0 560.9 jit_solution(6861968593285508169)
XLA Ops:
  8.0 56.8 %all-gather.2.cloned.1.call-done = bf16[16,512,512]{2,1,0:T(8,128)(2,1)} async-done(((bf16[1,512,512]{2,1,0:T(8,128)(2,1)}), bf16[16,512,512]{2,1,0:T(8,128)(2,1)}) %all-gather.2.cloned.1.call-update) | async-done | bytes 8388624 | tf_op jit(solution)/shard_map/all_gather | solution.py:22
  64.9 8.2 %and_select_fusion = bf16[16,512,512]{2,1,0:T(8,128)(2,1)} fusion(bf16[16,512,512]{2,1,0:T(8,128)(2,1)} %all-gather.2.cloned.1.call-done, pred[16,512]{1,0:T(8,128)(4,1)S(1)} %iota_compare_fusion), kind=kLoop, calls=%fused_computation.12 | loop fusion | flops 8388608 | bytes 16785408 | tf_op jit(solution)/shard_map/mul | solution.py:25
  73.1 7.9 %broadcast_in_dim.2 = f32[16,512,512]{2,1,0:T(8,128)} broadcast(f32[]{:T(128)} %constant.44.clone.1), dimensions={} | broadcast | bytes 16777220 | tf_op jit(solution)/shard_map/broadcast_in_dim | solution.py:35
  81.0 287.9 %while.11 = (s32[]{:T(128)}, f32[16,512,512]{2,1,0:T(8,128)}, s32[24]{0:T(128)S(1)}, s32[24]{0:T(128)S(1)}, bf16[2,512,512]{2,1,0:T(8,128)(2,1)S(1)}, /*index=5*...) while((s32[]{:T(128)}, f32[16,512,512]{2,1,0:T(8,128)}, ...), condition=%wide.region_2.3_spmd, body=%wide.region_0.2_spmd.sunk | while | flops 537657344 | bytes 3672876 | solution.py:36
  89.3 3.7 fusion.20
  113.3 3.7 fusion.20
  125.2 3.7 fusion.20
  137.2 3.7 fusion.20
  149.2 3.8 fusion.20
  161.3 3.8 fusion.20
  173.3 3.7 fusion.20
  185.3 3.7 fusion.20
  197.3 3.8 fusion.20
  245.2 3.7 fusion.20
  257.2 3.7 fusion.20
  269.3 3.7 fusion.20
  293.2 3.7 fusion.20
  305.2 3.7 fusion.20
  329.2 3.7 fusion.20
  341.2 3.8 fusion.20
  353.2 3.8 fusion.20
  365.2 3.7 fusion.20
  369.0 97.6 %reduce-scatter.2.cloned.1.call-done = f32[1,512,512]{2,1,0:T(8,128)} async-done(((f32[16,512,512]{2,1,0:T(8,128)}), f32[1,512,512]{2,1,0:T(8,128)}) %reduce-scatter.2.cloned.1.call-update) | async-done | bytes 1048592 | tf_op jit(solution)/shard_map/reduce_scatter | solution.py:39
  467.8 84.2 %all-reduce.2.cloned.1.call-done = f32[1,512,512]{2,1,0:T(8,128)} async-done(((f32[1,512,512]{2,1,0:T(8,128)}), f32[1,512,512]{2,1,0:T(8,128)}) %all-reduce.2.cloned.1.call-update) | async-done | bytes 1048592 | tf_op jit(solution)/shard_map/psum | solution.py:40
  (126 shorter events, 91.8 us)
Async XLA Ops:
  6.5 58.4 %all-gather.2.cloned.1.call-start = ((), (), s32[]{:S(2)}) async-start(), calls=%async_computation.1 | async-start | bytes 8912896 | tf_op jit(solution)/shard_map/all_gather | solution.py:22
  7.3 459.3 %reduce-scatter.2.cloned.1.call-start = ((), (), s32[]{:S(2)}) async-start(), calls=%async_computation.2 | async-start | bytes 17825792 | tf_op jit(solution)/shard_map/reduce_scatter | solution.py:39
  73.0 7.9 %copy-start = (s32[3]{0:T(128)S(1)}, s32[3]{0:T(128)}, u32[]{:S(2)}) copy-start(s32[3]{0:T(128)} %constant.37.clone.1) | copy-start | bytes 40
  73.0 7.9 %copy-start.2 = (bf16[2,512,512]{2,1,0:T(8,128)(2,1)S(1)}, bf16[2,512,512]{2,1,0:T(8,128)(2,1)}, u32[]{:S(2)}) copy-start(bf16[2,512,512]{2,1,0:T(8,128)(2,1)} %param.12) | copy-start | bytes 3145732
  73.1 7.9 %copy-start.3 = (bf16[2,512,512]{2,1,0:T(8,128)(2,1)S(1)}, bf16[2,512,512]{2,1,0:T(8,128)(2,1)}, u32[]{:S(2)}) copy-start(bf16[2,512,512]{2,1,0:T(8,128)(2,1)} %param.13) | copy-start | bytes 3145732
  73.1 7.9 %copy-start.4 = (s32[24]{0:T(128)S(1)}, s32[24]{0:T(128)}, u32[]{:S(2)}) copy-start(s32[24]{0:T(128)} %param.16) | copy-start | bytes 292
  73.1 7.9 %copy-start.5 = (s32[24]{0:T(128)S(1)}, s32[24]{0:T(128)}, u32[]{:S(2)}) copy-start(s32[24]{0:T(128)} %param.17) | copy-start | bytes 292
  73.1 7.9 %copy-start.6 = (s32[24]{0:T(128)S(1)}, s32[24]{0:T(128)}, u32[]{:S(2)}) copy-start(s32[24]{0:T(128)} %param.15) | copy-start | bytes 292
  368.9 97.7 %copy-start.1 = (s32[16]{0:T(128)S(1)}, s32[16]{0:T(128)}, u32[]{:S(2)}) copy-start(s32[16]{0:T(128)} %param.14) | copy-start | bytes 196
  369.0 183.1 %all-reduce.2.cloned.1.call-start = ((), (), s32[]{:S(2)}) async-start(), calls=%async_computation.3 | async-start | bytes 2097152 | tf_op jit(solution)/shard_map/psum | solution.py:40
Sparse Core Ops, SparseCore 0:
  9.1 55.7 all-gather.1
  369.1 97.4 reduce-scatter.1
  469.1 82.9 all-reduce.1
where the time goes:
time: 568 us; the launch traced here: 561 us
  waiting for transfers between devices  239 us (42%)
  loops' own time  134 us (24%)
  matrix products  89.4 us (16%)
  local copies, waits for them, and re-layouts  54.6 us (10%)
  other arithmetic  30.3 us (5%)
  between operations  13.2 us (2%)
    another operation x1, loops' own time, body(): lax.scan(advance, start_blocks, (coupling_source, coupling_target, coupli...  134 us
    reduce_scatter x1, waiting for transfers between devices, body(): lax.psum_scatter(partial_blocks, 'sector', scatter_dimension=0, tiled=True)  97.6 us
    dot_general x24, matrix products, advance(): jnp.dot(halfway, right_ops[chosen], preferred_element_type=jnp.float32)  89.4 us
    psum x1, waiting for transfers between devices, body(): summed = lax.psum(own_part, 'term')  84.2 us
    all_gather x1, waiting for transfers between devices, body(): gathered = lax.all_gather(wavefunction, 'sector', axis=0, tiled=True)  56.8 us
    dynamic_slice x72, local copies, waits for them, and re-layouts, body(): lax.scan(advance, start_blocks, (coupling_source, coupling_target, coupli...  46.1 us
    another operation x24, other arithmetic  18.3 us
  transfers between devices with their start and end apart: 3, of which 3 were waited for; matrix products, arithmetic and copies ran while one was open for 0% of the time, Pallas kernels for 0%

commit v1 on v0

v1 whole, which is shorter than its diff:
```python
import jax
import jax.numpy as jnp
from jax import lax
from jax.experimental import pallas as pl
from jax.experimental.pallas import tpu as pltpu
from jax.sharding import Mesh, PartitionSpec as P

AXES = ("x_hi", "y", "x_lo", "z", "core")
SIZES = (2, 4, 2, 4, 2)
TERM = ("x_hi", "y")
SECTOR = ("x_lo", "z", "core")
LEVELS = 4
GRAIN = 128
STRIPE = 64
MIB = 1024 * 1024


def couplings_kernel(
    own_source, own_target, own_chosen, mate_meta, dims,
    own_left, mate_left, own_right, mate_right, wave,
    out_ref,
    left, right, waves, sums, sems,
):
    core = lax.axis_index("core")
    own_count = own_source.shape[0]
    ops = own_left.shape[0]
    sectors = wave.shape[0]
    copies = [
        pltpu.make_async_copy(own_left.at[:, :, core], left.at[pl.ds(0, ops)], sems.at[0]),
        pltpu.make_async_copy(mate_left, left.at[pl.ds(ops, ops)], sems.at[1]),
        pltpu.make_async_copy(own_right, right.at[pl.ds(0, ops)], sems.at[2]),
        pltpu.make_async_copy(mate_right, right.at[pl.ds(ops, ops)], sems.at[3]),
        pltpu.make_async_copy(wave, waves, sems.at[4]),
    ]
    for copy in copies:
        copy.start()
    sums[...] = jnp.zeros_like(sums)
    for copy in copies:
        copy.wait()

    def one(i, carry):
        is_own = i < own_count
        j = jnp.where(is_own, i, i - own_count)
        source = jnp.where(is_own, own_source[j], mate_meta[0, j])
        target = jnp.where(is_own, own_target[j], mate_meta[1, j])
        chosen = jnp.where(is_own, own_chosen[j], mate_meta[2, j] + ops)
        source_level = dims[source] // GRAIN
        target_level = dims[target] // GRAIN
        case = (source_level - 1) * LEVELS + target_level - 1
        for sl in range(1, LEVELS + 1):
            for tl in range(1, LEVELS + 1):

                @pl.when(case == (sl - 1) * LEVELS + tl - 1)
                def _(sl=sl, tl=tl):
                    inner, rows, cols = sl * GRAIN, tl * STRIPE, tl * GRAIN
                    block = left[chosen, :tl, :, :inner].reshape(rows, inner)
                    halfway = jnp.dot(
                        block, waves[source, :inner, :inner], preferred_element_type=jnp.float32
                    ).astype(jnp.bfloat16)
                    sums[target, :rows, :cols] += jnp.dot(
                        halfway, right[chosen, :inner, :cols], preferred_element_type=jnp.float32
                    )

        return carry

    lax.fori_loop(0, 2 * own_count, one, 0)
    parts = out_ref.shape[0]
    rows = out_ref.shape[2]
    for part in range(parts):
        out_ref[part] = sums[:, part * rows:(part + 1) * rows, :].astype(jnp.bfloat16)


def body(
    wavefunction,
    left_ops,
    right_ops,
    sector_dims,
    coupling_source,
    coupling_target,
    coupling_operator,
):
    ops, width, _ = left_ops.shape
    swap = [(0, 1), (1, 0)]
    core = lax.axis_index("core")
    striped = left_ops.reshape(ops, width // GRAIN, 2, STRIPE, width)
    other_half = lax.dynamic_index_in_dim(striped, 1 - core, 2, keepdims=False)
    meta = jnp.stack([coupling_source, coupling_target, coupling_operator])
    mate_left = lax.ppermute(other_half, "core", swap)
    mate_right = lax.ppermute(right_ops, "core", swap)
    mate_meta = lax.ppermute(meta, "core", swap)
    wave = lax.all_gather(wavefunction, SECTOR, axis=0, tiled=True)
    sectors = wave.shape[0]
    members = 8
    smem = pl.BlockSpec(memory_space=pltpu.SMEM)
    anywhere = pl.BlockSpec(memory_space=pl.ANY)
    partial = pl.pallas_call(
        couplings_kernel,
        out_shape=jax.ShapeDtypeStruct((members, sectors, width // 2 // members, width), jnp.bfloat16),
        in_specs=[smem] * 5 + [anywhere] * 5,
        out_specs=pl.BlockSpec(memory_space=pltpu.VMEM),
        scratch_shapes=[
            pltpu.VMEM((2 * ops, width // GRAIN, STRIPE, width), jnp.bfloat16),
            pltpu.VMEM((2 * ops, width, width), jnp.bfloat16),
            pltpu.VMEM((sectors, width, width), jnp.bfloat16),
            pltpu.VMEM((sectors, width // 2, width), jnp.float32),
            pltpu.SemaphoreType.DMA((5,)),
        ],
        compiler_params=pltpu.CompilerParams(vmem_limit_bytes=48 * MIB),
        name="couplings",
    )(
        coupling_source, coupling_target, coupling_operator, mate_meta, sector_dims,
        striped, mate_left, right_ops, mate_right, wave,
    )
    rows = partial.shape[2]
    sent = partial.reshape(members * sectors, rows, width)
    got = lax.all_to_all(sent, AXES, 0, 0, tiled=True)
    own = jnp.sum(got.reshape(-1, 2, rows, width).astype(jnp.float32), axis=0)
    own = own.astype(jnp.bfloat16)
    spread = jnp.broadcast_to(own[None], (members, 2, rows, width))
    whole = lax.all_to_all(spread, TERM, 0, 0, tiled=True)
    whole = whole.reshape(width // GRAIN, 2, 2, rows, width).transpose(0, 2, 1, 3, 4)
    return whole.reshape(1, width, width).astype(jnp.float32)


def solution(mesh):
    fine = Mesh(mesh.devices.reshape(SIZES), AXES)
    everyone = P(AXES)
    placed = (
        P(SECTOR, None, None),
        P(AXES, None, None),
        P(AXES, None, None),
        P(),
        everyone,
        everyone,
        everyone,
    )
    return jax.shard_map(
        body, mesh=fine, in_specs=placed, out_specs=P(SECTOR, None, None), check_vma=False
    )
```

time: 568 us -> 191 us (0.34)
  waiting for transfers between devices: 239 us -> 54.4 us
  loops' own time: 134 us -> 0 us
  matrix products: 89.4 us -> 0 us
  blocking collectives: 0 us -> 75.7 us
  local copies, waits for them, and re-layouts: 54.6 us -> 7.26 us
  Pallas kernels: 0 us -> 32 us
  other arithmetic: 30.3 us -> 3.67 us
    another operation x1 -> x0, loops' own time: 134 us -> none  [body(): lax.scan(advance, start_blocks, (coupling_source, coupling_target, coupli...]
    reduce_scatter x1 -> x0, waiting for transfers between devices: 97.6 us -> none  [body(): lax.psum_scatter(partial_blocks, 'sector', scatter_dimension=0, tiled=True)]
    dot_general x24 -> x0, matrix products: 89.4 us -> none  [advance(): jnp.dot(halfway, right_ops[chosen], preferred_element_type=jnp.float32)]
    psum x1 -> x0, waiting for transfers between devices: 84.2 us -> none  [body(): summed = lax.psum(own_part, 'term')]
    all_to_all x0 -> x2, blocking collectives: none -> 75.7 us  [the longest x1 61.1 us: body(): got = lax.all_to_all(sent, AXES, 0, 0, tiled=True)]
    dynamic_slice x73 -> x0, local copies, waits for them, and re-layouts: 46.7 us -> none  [the longest x72 46.1 us: body(): lax.scan(advance, start_blocks, (coupling_source, coupling_target, coupli...]
    pallas_call x0 -> x1, Pallas kernels: none -> 32 us  [body(): pl.pallas_call(couplings_kernel, out_shape=jax.ShapeDtypeStruct((members,...]
    another operation x24 -> x1, other arithmetic: 18.3 us -> 0.7 us  [body(): meta = jnp.stack([coupling_source, coupling_target, coupling_operator])]
  transfers between devices with their start and end apart: 3 -> 4, of which waited for: 3 -> 2; matrix products, arithmetic and copies ran while one was open for 0% -> 1% of each run, Pallas kernels for 0% -> 0%
where the time goes in v1:
time: 191 us; the launch traced here: 189 us
  blocking collectives  75.7 us (40%)
  waiting for transfers between devices  54.4 us (28%)
  Pallas kernels  32 us (17%)
  between operations  13.4 us (7%)
  local copies, waits for them, and re-layouts  7.26 us (4%)
  other arithmetic  3.67 us (2%)
  starting transfers between devices  2.16 us (1%)
    all_to_all x1, blocking collectives, body(): got = lax.all_to_all(sent, AXES, 0, 0, tiled=True)  61.1 us
    all_gather x1, waiting for transfers between devices, body(): wave = lax.all_gather(wavefunction, SECTOR, axis=0, tiled=True)  52.9 us
    pallas_call x1, Pallas kernels, body(): pl.pallas_call(couplings_kernel, out_shape=jax.ShapeDtypeStruct((members,...  32 us
    all_to_all x1, blocking collectives, body(): whole = lax.all_to_all(spread, TERM, 0, 0, tiled=True)  14.5 us
    unnamed x12, local copies, waits for them, and re-layouts  5.07 us
  transfers between devices with their start and end apart: 4, of which 2 were waited for; matrix products, arithmetic and copies ran while one was open for 1% of the time, Pallas kernels for 0%

profile of v1, /device:TPU:1, one launch (start us, length us, event | category | flops | bytes accessed | tf_op | source)
XLA Modules:
  0.0 188.5 jit_solution(8926393317714284860)
XLA Ops:
  6.5 0.0 all-gather.2.cloned.1.call-start
  6.5 0.7 all-gather.2.cloned.1.call-update
  7.3 1.5 collective-permute-start.2
  8.8 1.1 dynamic-slice_bitcast_fusion
  9.8 0.1 collective-permute-start.1
  9.9 0.7 pad_add_fusion
  10.6 0.5 collective-permute-start
  11.2 0.8 collective-permute-done.mate_meta
  12.0 0.0 collective-permute-done.1.mate_left
  12.0 0.0 collective-permute-done.2.mate_right
  12.0 52.9 %all-gather.2.cloned.1.call-done.wave = bf16[16,512,512]{2,1,0:T(8,128)(2,1)} async-done(((bf16[1,512,512]{2,1,0:T(8,128)(2,1)}), bf16[16,512,512]{2,1,0:T(8,128)(2,1)}) %all-gather.2.cloned.1.call-update) | async-done | bytes 8388624 | tf_op jit(solution)/shard_map/all_gather | solution.py:91
  64.9 0.0 copy-start
  64.9 1.2 copy-done
  66.1 1.2 copy-done.1
  67.3 0.7 copy-done.2
  68.0 0.7 copy-done.3
  68.6 0.7 copy-done.4
  69.3 0.7 copy-done.5
  70.0 32.0 %couplings.1 = bf16[8,16,32,512]{3,2,1,0:T(8,128)(2,1)} custom-call(s32[24]{0:T(128)S(1)} %copy-done.2, s32[24]{0:T(128)S(1)} %copy-done.3, s32[24]{0:T(128)S(1)} %copy-done.4, s32[3,24]{1,0:T(4,128)S(1)} %collective-permute-done.mate_meta, s32[16]{0:T(128)S(1)} %copy-done.5, bf16[2,4,2,64,512]{4,3,2,1,0:T(8,128)(2,1)S(1)} %bitcast.14, ...), custom_call_target="tpu_custom_call" | custom-call | tf_op jit(solution)/shard_map/couplings/pallas_call | solution.py:96
  101.9 61.1 %all_to_all.10 = bf16[128,32,512]{2,1,0:T(8,128)(2,1)} all-to-all(bf16[128,32,512]{2,1,0:T(8,128)(2,1)} %bitcast.18), channel_id=1, replica_groups=mesh['x_hi'=2,'y'=4,'x_lo'=2,'z'=4,'core'=2] {'x_hi','y','x_lo','z','core'}, dimensions={0} | all-to-all | bytes 8388608 | tf_op jit(solution)/shard_map/all_to_all | solution.py:116
  163.1 2.9 %reduce_sum.12 = bf16[2,32,512]{2,1,0:T(8,128)(2,1)S(1)} reduce(bf16[64,2,32,512]{3,2,1,0:T(8,128)(2,1)} %bitcast.19, bf16[]{:T(256)} %constant.15.clone.1), dimensions={0}, to_apply=%region_0.1 | reduce | flops 2064384 | bytes 4259842 | tf_op jit(solution)/shard_map/reduce_sum | solution.py:117
  166.0 14.5 %all_to_all.11 = bf16[8,2,32,512]{3,2,1,0:T(8,128)(2,1)S(1)} all-to-all(bf16[8,2,32,512]{3,2,1,0:T(8,128)(2,1)S(1)} %broadcast_in_dim.2), channel_id=1, replica_groups=mesh['x_hi'=2,'y'=4,'x_lo'=2,'z'=4,'core'=2] {'x_hi','y'}, dimensions={0} | all-to-all | bytes 1048576 | tf_op jit(solution)/shard_map/all_to_all | solution.py:120
  180.5 0.1 convert_bitcast_fusion
  180.6 1.1 copy.9
  (6 shorter events, 0.1 us)
Async XLA Ops:
  6.5 58.4 %all-gather.2.cloned.1.call-start = ((), (), s32[]{:S(2)}) async-start(), calls=%async_computation.2 | async-start | bytes 8912896 | tf_op jit(solution)/shard_map/all_gather | solution.py:91
  7.3 4.8 %collective-permute-start.2 = (bf16[2,512,512]{2,1,0:T(8,128)(2,1)}, bf16[2,512,512]{2,1,0:T(8,128)(2,1)S(1)}, u32[]{:S(2)}, u32[]{:S(2)}) collective-permute-start(bf16[2,512,512]{2,1,0:T(8,128)(2,1)} %own_right.1), channel_id=1, source_target_pairs={{0,1},{1,0},{2,3},{3,2},{4,5},{5,4},{6,7},{7,6},{8,9},{9,8},{10,11... | collective-permute-start | bytes 3145736 | tf_op jit(solution)/shard_map/ppermute | solution.py:89
  9.8 2.2 %collective-permute-start.1 = (bf16[2,4,64,512]{3,2,1,0:T(8,128)(2,1)S(1)}, bf16[2,4,64,512]{3,2,1,0:T(8,128)(2,1)S(1)}, u32[]{:S(2)}, u32[]{:S(2)}) collective-permute-start(bf16[2,4,64,512]{3,2,1,0:T(8,128)(2,1)S(1)} %dynamic-slice_bitcast_fusion), channel_id=1, source_target_pairs={{0,1},{1,0},{2,3},{3,2},{4,5},{5,4},{6,7},{7,6},{8,9},{9,8},{10,11... | collective-permute-start | bytes 1572872 | tf_op jit(solution)/shard_map/ppermute | solution.py:88
  10.6 1.4 collective-permute-start
  64.9 1.2 copy-start
  66.1 1.2 copy-start.1
  67.3 0.7 copy-start.2
  68.0 0.7 copy-start.3
  68.6 0.7 copy-start.4
  69.3 0.7 copy-start.5
Sparse Core Ops, SparseCore 0:
  9.1 55.7 all-gather.1

commit v2 on v1

--- a/solution.py
+++ b/solution.py
@@ -18,27 +18,55 @@
 def couplings_kernel(
     own_source, own_target, own_chosen, mate_meta, dims,
     own_left, mate_left, own_right, mate_right, wave,
-    out_ref,
-    left, right, waves, sums, sems,
+    out,
+    left, right, waves, halves, sums, rounded, op_sems, wave_sems, out_sems,
 ):
     core = lax.axis_index("core")
     own_count = own_source.shape[0]
     ops = own_left.shape[0]
     sectors = wave.shape[0]
-    copies = [
-        pltpu.make_async_copy(own_left.at[:, :, core], left.at[pl.ds(0, ops)], sems.at[0]),
-        pltpu.make_async_copy(mate_left, left.at[pl.ds(ops, ops)], sems.at[1]),
-        pltpu.make_async_copy(own_right, right.at[pl.ds(0, ops)], sems.at[2]),
-        pltpu.make_async_copy(mate_right, right.at[pl.ds(ops, ops)], sems.at[3]),
-        pltpu.make_async_copy(wave, waves, sems.at[4]),
+    parts, _, rows, width = out.shape
+    op_copies = [
+        pltpu.make_async_copy(own_left.at[:, :, core], left.at[pl.ds(0, ops)], op_sems.at[0]),
+        pltpu.make_async_copy(mate_left, left.at[pl.ds(ops, ops)], op_sems.at[1]),
+        pltpu.make_async_copy(own_right, right.at[pl.ds(0, ops)], op_sems.at[2]),
+        pltpu.make_async_copy(mate_right, right.at[pl.ds(ops, ops)], op_sems.at[3]),
     ]
-    for copy in copies:
-        copy.start()
+
+    def wave_copy(s):
+        return pltpu.make_async_copy(wave.at[s], waves.at[s], wave_sems.at[s])
+
+    op_copies[0].start()
+    op_copies[1].start()
+    for s in range(sectors):
+        wave_copy(s).start()
+    op_copies[2].start()
+    op_copies[3].start()
     sums[...] = jnp.zeros_like(sums)
-    for copy in copies:
-        copy.wait()
+    op_copies[0].wait()
+    op_copies[1].wait()
 
-    def one(i, carry):
+    def first_half(s, carry):
+        wave_copy(s).wait()
+        level = dims[s] // GRAIN
+        for sl in range(1, LEVELS + 1):
+
+            @pl.when(level == sl)
+            def _(sl=sl):
+                inner = sl * GRAIN
+                stacked = left[:, :, :, :inner].reshape(2 * ops * width // 2, inner)
+                product = jnp.dot(
+                    stacked, waves[s, :inner, :inner], preferred_element_type=jnp.float32
+                ).astype(jnp.bfloat16)
+                halves[s, :, :, :inner] = product.reshape(2 * ops, width // 2, inner)
+
+        return carry
+
+    lax.fori_loop(0, sectors, first_half, 0)
+    op_copies[2].wait()
+    op_copies[3].wait()
+
+    def second_half(i, carry):
         is_own = i < own_count
         j = jnp.where(is_own, i, i - own_count)
         source = jnp.where(is_own, own_source[j], mate_meta[0, j])
@@ -46,28 +74,32 @@
         chosen = jnp.where(is_own, own_chosen[j], mate_meta[2, j] + ops)
         source_level = dims[source] // GRAIN
         target_level = dims[target] // GRAIN
-        case = (source_level - 1) * LEVELS + target_level - 1
         for sl in range(1, LEVELS + 1):
-            for tl in range(1, LEVELS + 1):
 
-                @pl.when(case == (sl - 1) * LEVELS + tl - 1)
-                def _(sl=sl, tl=tl):
-                    inner, rows, cols = sl * GRAIN, tl * STRIPE, tl * GRAIN
-                    block = left[chosen, :tl, :, :inner].reshape(rows, inner)
-                    halfway = jnp.dot(
-                        block, waves[source, :inner, :inner], preferred_element_type=jnp.float32
-                    ).astype(jnp.bfloat16)
-                    sums[target, :rows, :cols] += jnp.dot(
-                        halfway, right[chosen, :inner, :cols], preferred_element_type=jnp.float32
-                    )
+            @pl.when(source_level == sl)
+            def _(sl=sl):
+                for tl in range(1, LEVELS + 1):
+
+                    @pl.when(target_level == tl)
+                    def _(tl=tl):
+                        inner, stripe, cols = sl * GRAIN, tl * STRIPE, tl * GRAIN
+                        sums[target, :stripe, :cols] += jnp.dot(
+                            halves[source, chosen, :stripe, :inner],
+                            right[chosen, :inner, :cols],
+                            preferred_element_type=jnp.float32,
+                        )
 
         return carry
 
-    lax.fori_loop(0, 2 * own_count, one, 0)
-    parts = out_ref.shape[0]
-    rows = out_ref.shape[2]
+    lax.fori_loop(0, 2 * own_count, second_half, 0)
+    out_copies = []
     for part in range(parts):
-        out_ref[part] = sums[:, part * rows:(part + 1) * rows, :].astype(jnp.bfloat16)
+        rounded[part] = sums[:, part * rows:(part + 1) * rows, :].astype(jnp.bfloat16)
+        copy = pltpu.make_async_copy(rounded.at[part], out.at[part], out_sems.at[part])
+        copy.start()
+        out_copies.append(copy)
+    for copy in out_copies:
+        copy.wait()
 
 
 def body(
@@ -92,20 +124,24 @@
     sectors = wave.shape[0]
     members = 8
     smem = pl.BlockSpec(memory_space=pltpu.SMEM)
-    anywhere = pl.BlockSpec(memory_space=pl.ANY)
+    anywhere = pl.BlockSpec(memory_space=pltpu.HBM)
     partial = pl.pallas_call(
         couplings_kernel,
         out_shape=jax.ShapeDtypeStruct((members, sectors, width // 2 // members, width), jnp.bfloat16),
         in_specs=[smem] * 5 + [anywhere] * 5,
-        out_specs=pl.BlockSpec(memory_space=pltpu.VMEM),
+        out_specs=anywhere,
         scratch_shapes=[
             pltpu.VMEM((2 * ops, width // GRAIN, STRIPE, width), jnp.bfloat16),
             pltpu.VMEM((2 * ops, width, width), jnp.bfloat16),
             pltpu.VMEM((sectors, width, width), jnp.bfloat16),
+            pltpu.VMEM((sectors, 2 * ops, width // 2, width), jnp.bfloat16),
             pltpu.VMEM((sectors, width // 2, width), jnp.float32),
-            pltpu.SemaphoreType.DMA((5,)),
+            pltpu.VMEM((members, sectors, width // 2 // members, width), jnp.bfloat16),
+            pltpu.SemaphoreType.DMA((4,)),
+            pltpu.SemaphoreType.DMA((sectors,)),
+            pltpu.SemaphoreType.DMA((members,)),
         ],
-        compiler_params=pltpu.CompilerParams(vmem_limit_bytes=48 * MIB),
+        compiler_params=pltpu.CompilerParams(vmem_limit_bytes=56 * MIB),
         name="couplings",
     )(
         coupling_source, coupling_target, coupling_operator, mate_meta, sector_dims,

time: 191 us -> 181 us (0.948); the launches traced: 189 us -> 182 us
  local copies, waits for them, and re-layouts: 7.26 us -> 2.21 us
  Pallas kernels: 32 us -> 29.4 us
    unnamed x12 -> x6, local copies, waits for them, and re-layouts: 5.07 us -> 0.01 us
    pallas_call x1, Pallas kernels: 32 us -> 29.4 us  [body(): pl.pallas_call(couplings_kernel, out_shape=jax.ShapeDtypeStruct((members,...]
where the time goes in v2:
time: 181 us; the launch traced here: 182 us
  blocking collectives  76.4 us (42%)
  waiting for transfers between devices  54.4 us (30%)
  Pallas kernels  29.4 us (16%)
  between operations  13.4 us (7%)
  other arithmetic  3.67 us (2%)
  local copies, waits for them, and re-layouts  2.21 us (1%)
  starting transfers between devices  2.16 us (1%)
    all_to_all x1, blocking collectives, body(): got = lax.all_to_all(sent, AXES, 0, 0, tiled=True)  61.9 us
    all_gather x1, waiting for transfers between devices, body(): wave = lax.all_gather(wavefunction, SECTOR, axis=0, tiled=True)  52.9 us
    pallas_call x1, Pallas kernels, body(): pl.pallas_call(couplings_kernel, out_shape=jax.ShapeDtypeStruct((members,...  29.4 us
    all_to_all x1, blocking collectives, body(): whole = lax.all_to_all(spread, TERM, 0, 0, tiled=True)  14.5 us
  transfers between devices with their start and end apart: 4, of which 2 were waited for; matrix products, arithmetic and copies ran while one was open for 1% of the time, Pallas kernels for 0%

profile of v2, /device:TPU:1, one launch (start us, length us, event | category | flops | bytes accessed | tf_op | source)
XLA Modules:
  0.0 181.6 jit_solution(4392345519258314507)
XLA Ops:
  6.5 0.0 all-gather.2.cloned.1.call-start
  6.5 0.7 all-gather.2.cloned.1.call-update
  7.3 1.5 collective-permute-start.2
  8.8 1.1 dynamic-slice_bitcast_fusion
  9.8 0.1 collective-permute-start.1
  9.9 0.7 pad_add_fusion
  10.6 0.5 collective-permute-start
  11.2 0.8 collective-permute-done.mate_meta
  12.0 0.0 copy-start.2
  12.0 0.0 collective-permute-done.1.mate_left
  12.0 0.0 copy-start.1
  12.0 0.0 collective-permute-done.2.mate_right
  12.0 0.0 copy-start
  12.0 52.9 %all-gather.2.cloned.1.call-done.wave = bf16[16,512,512]{2,1,0:T(8,128)(2,1)} async-done(((bf16[1,512,512]{2,1,0:T(8,128)(2,1)}), bf16[16,512,512]{2,1,0:T(8,128)(2,1)}) %all-gather.2.cloned.1.call-update) | async-done | bytes 8388624 | tf_op jit(solution)/shard_map/all_gather | solution.py:123
  64.9 0.0 copy-done.2
  64.9 0.0 copy-done.1
  64.9 0.0 copy-done
  64.9 29.4 %couplings.1 = bf16[8,16,32,512]{3,2,1,0:T(8,128)(2,1)} custom-call(s32[24]{0:T(128)} %own_source.1, s32[24]{0:T(128)} %own_target.1, s32[24]{0:T(128)} %own_chosen.1, s32[3,24]{1,0:T(4,128)} %copy-done.2, s32[16]{0:T(128)} %dims.1, bf16[2,4,2,64,512]{4,3,2,1,0:T(8,128)(2,1)} %bitcast.16, bf16[2,4,64,512]{3,2,1,0:T(8,128)(2,1)} %copy-done.1, ...), custom_call_target="tpu_custom_call" | custom-call | tf_op jit(solution)/shard_map/couplings/pallas_call | solution.py:128
  94.3 61.9 %all_to_all.10 = bf16[128,32,512]{2,1,0:T(8,128)(2,1)} all-to-all(bf16[128,32,512]{2,1,0:T(8,128)(2,1)} %bitcast.13), channel_id=1, replica_groups=mesh['x_hi'=2,'y'=4,'x_lo'=2,'z'=4,'core'=2] {'x_hi','y','x_lo','z','core'}, dimensions={0} | all-to-all | bytes 8388608 | tf_op jit(solution)/shard_map/all_to_all | solution.py:152
  156.1 2.9 %reduce_sum.12 = bf16[2,32,512]{2,1,0:T(8,128)(2,1)S(1)} reduce(bf16[64,2,32,512]{3,2,1,0:T(8,128)(2,1)} %bitcast.14, bf16[]{:T(256)} %constant.15.clone.1), dimensions={0}, to_apply=%region_0.1 | reduce | flops 2064384 | bytes 4259842 | tf_op jit(solution)/shard_map/reduce_sum | solution.py:153
  159.1 14.5 %all_to_all.11 = bf16[8,2,32,512]{3,2,1,0:T(8,128)(2,1)S(1)} all-to-all(bf16[8,2,32,512]{3,2,1,0:T(8,128)(2,1)S(1)} %broadcast_in_dim.2), channel_id=1, replica_groups=mesh['x_hi'=2,'y'=4,'x_lo'=2,'z'=4,'core'=2] {'x_hi','y'}, dimensions={0} | all-to-all | bytes 1048576 | tf_op jit(solution)/shard_map/all_to_all | solution.py:156
  173.6 0.1 convert_bitcast_fusion
  173.7 1.1 copy.9
  (1 shorter events, 0.0 us)
Async XLA Ops:
  6.5 58.4 %all-gather.2.cloned.1.call-start = ((), (), s32[]{:S(2)}) async-start(), calls=%async_computation.2 | async-start | bytes 8912896 | tf_op jit(solution)/shard_map/all_gather | solution.py:123
  7.3 4.8 %collective-permute-start.2 = (bf16[2,512,512]{2,1,0:T(8,128)(2,1)}, bf16[2,512,512]{2,1,0:T(8,128)(2,1)S(1)}, u32[]{:S(2)}, u32[]{:S(2)}) collective-permute-start(bf16[2,512,512]{2,1,0:T(8,128)(2,1)} %own_right.1), channel_id=1, source_target_pairs={{0,1},{1,0},{2,3},{3,2},{4,5},{5,4},{6,7},{7,6},{8,9},{9,8},{10,11... | collective-permute-start | bytes 3145736 | tf_op jit(solution)/shard_map/ppermute | solution.py:121
  9.8 2.2 %collective-permute-start.1 = (bf16[2,4,64,512]{3,2,1,0:T(8,128)(2,1)S(1)}, bf16[2,4,64,512]{3,2,1,0:T(8,128)(2,1)S(1)}, u32[]{:S(2)}, u32[]{:S(2)}) collective-permute-start(bf16[2,4,64,512]{3,2,1,0:T(8,128)(2,1)S(1)} %dynamic-slice_bitcast_fusion), channel_id=1, source_target_pairs={{0,1},{1,0},{2,3},{3,2},{4,5},{5,4},{6,7},{7,6},{8,9},{9,8},{10,11... | collective-permute-start | bytes 1572872 | tf_op jit(solution)/shard_map/ppermute | solution.py:120
  10.6 1.4 collective-permute-start
  12.0 52.9 %copy-start.2 = (s32[3,24]{1,0:T(4,128)}, s32[3,24]{1,0:T(4,128)S(1)}, u32[]{:S(2)}) copy-start(s32[3,24]{1,0:T(4,128)S(1)} %collective-permute-done.mate_meta) | copy-start | bytes 868
  12.0 52.9 %copy-start.1 = (bf16[2,4,64,512]{3,2,1,0:T(8,128)(2,1)}, bf16[2,4,64,512]{3,2,1,0:T(8,128)(2,1)S(1)}, u32[]{:S(2)}) copy-start(bf16[2,4,64,512]{3,2,1,0:T(8,128)(2,1)S(1)} %collective-permute-done.1.mate_left) | copy-start | bytes 1572868
  12.0 52.9 %copy-start = (bf16[2,512,512]{2,1,0:T(8,128)(2,1)}, bf16[2,512,512]{2,1,0:T(8,128)(2,1)S(1)}, u32[]{:S(2)}) copy-start(bf16[2,512,512]{2,1,0:T(8,128)(2,1)S(1)} %collective-permute-done.2.mate_right) | copy-start | bytes 3145732
Sparse Core Ops, SparseCore 0:
  9.1 55.7 all-gather.1

commit v3 on v0

v3 whole, which is shorter than its diff:
```python
import jax
import jax.numpy as jnp
from jax import lax
from jax.experimental import pallas as pl
from jax.experimental.pallas import tpu as pltpu
from jax.sharding import Mesh, PartitionSpec as P

AXES = ("x_hi", "y", "x_lo", "z", "core")
SIZES = (2, 4, 2, 4, 2)
SECTOR = ("x_lo", "z", "core")
SHARERS = ("y", "core")
REDUCE = ("x_hi", "x_lo", "z")
SPREAD = ("x_hi", "y", "core")
RING = 4
GROUP = 8
LEVELS = 4
GRAIN = 128
SLICE = GRAIN // GROUP
STACK = 4
UNROLL = 2
MIB = 1024 * 1024


def plan_couplings(source, target, chosen, operators, sectors):
    count = source.shape[0]
    stacks = -(-(count + operators * (STACK - 1)) // STACK)
    stacks = -(-stacks // UNROLL) * UNROLL
    is_op = chosen[:, None] == jnp.arange(operators, dtype=jnp.int32)[None, :]
    number = jnp.sum(is_op.astype(jnp.int32), axis=0)
    taken = (number + STACK - 1) // STACK
    op = jnp.arange(operators, dtype=jnp.int32)
    end = jnp.sum(jnp.where(op[:, None] <= op[None, :], taken[:, None], 0), axis=0)
    start = end - taken
    spot = jnp.arange(count, dtype=jnp.int32)
    earlier = (chosen[:, None] == chosen[None, :]) & (spot[:, None] < spot[None, :])
    rank = jnp.sum(earlier.astype(jnp.int32), axis=0)
    place = rank + STACK * jnp.sum(jnp.where(is_op, start[None, :], 0), axis=1)
    here = place[:, None] == jnp.arange(stacks * STACK, dtype=jnp.int32)[None, :]
    code = source * (2 * sectors) + target - sectors
    table = sectors + jnp.sum(jnp.where(here, code[:, None], 0), axis=0)
    stack = jnp.arange(stacks, dtype=jnp.int32)
    stack_op = jnp.sum((end[:, None] <= stack[None, :]).astype(jnp.int32), axis=0)
    return table, jnp.minimum(stack_op, operators - 1), jnp.max(end)[None]


def couplings_kernel(
    table, stack_op, stack_count, dims,
    left_rows, own, own_down, own_up, own_far_a, own_far_b,
    mate, mate_down, mate_up, mate_far_a, mate_far_b, wave,
    out,
    left, right, waves, halves, sums, op_sems, wave_sems,
):
    y, core = lax.axis_index("y"), lax.axis_index("core")
    sectors, width, _ = wave.shape
    rows = sums.shape[1]
    ops = own.shape[0]

    def wave_copy(s):
        return pltpu.make_async_copy(wave.at[s], waves.at[s], wave_sems.at[s])

    left_copy = pltpu.make_async_copy(left_rows, left, op_sems.at[0])
    left_copy.start()
    for s in range(sectors):
        wave_copy(s).start()
    right_copies = []
    for c, parts in (
        (core, (own, own_down, own_up, own_far_a, own_far_b)),
        (1 - core, (mate, mate_down, mate_up, mate_far_a, mate_far_b)),
    ):
        for part, (shift, first) in zip(parts, ((0, 0), (RING - 1, 0), (1, 0), (2, 0), (2, 1))):
            slot = (lax.rem(y + shift, RING) * 2 + c) * ops + first
            copy = pltpu.make_async_copy(
                part, right.at[pl.ds(slot, part.shape[0])], op_sems.at[1 + len(right_copies)]
            )
            copy.start()
            right_copies.append(copy)
    sums[...] = jnp.zeros_like(sums)
    left_copy.wait()

    def first_half(s, carry):
        wave_copy(s).wait()
        level = dims[s] // GRAIN
        for sl in range(1, LEVELS + 1):

            @pl.when(level == sl)
            def _(sl=sl):
                inner = sl * GRAIN
                halves[s, :, :inner] = jnp.dot(
                    left[:, :inner], waves[s, :inner, :inner], preferred_element_type=jnp.float32
                ).astype(jnp.bfloat16)
                if inner < width:
                    halves[s, :, inner:] = jnp.zeros((left.shape[0], width - inner), jnp.bfloat16)

        return carry

    lax.fori_loop(0, sectors, first_half, 0)
    for copy in right_copies:
        copy.wait()

    def second_half(i, carry):
        for u in range(UNROLL):
            j = i * UNROLL + u
            op = stack_op[j]
            first = pl.multiple_of(op * rows, rows)
            codes = [table[j * STACK + k] for k in range(STACK)]
            sources = [lax.div(code, 2 * sectors) for code in codes]
            stacked = jnp.concatenate([halves[s, pl.ds(first, rows), :] for s in sources], axis=0)
            product = jnp.dot(stacked, right[op], preferred_element_type=jnp.float32)
            for k in range(STACK):
                target = lax.rem(codes[k], 2 * sectors)
                sums[target] += product[k * rows:(k + 1) * rows]
        return carry

    lax.fori_loop(0, lax.div(stack_count[0] + UNROLL - 1, UNROLL), second_half, 0)
    parts = out.shape[0]
    size = rows // parts
    for part in range(parts):
        out[part] = sums[:sectors, part * size:(part + 1) * size, :].astype(jnp.bfloat16)


def share_operators(left_ops, right_ops, meta):
    ops, width, _ = left_ops.shape
    down = [(i, (i + 1) % RING) for i in range(RING)]
    up = [(i, (i - 1) % RING) for i in range(RING)]
    swap = [(0, 1), (1, 0)]
    from_down = lax.ppermute(right_ops, "y", down)
    from_up = lax.ppermute(right_ops, "y", up)
    far_a = lax.ppermute(from_down[:1], "y", down)
    far_b = lax.ppermute(from_up[1:], "y", up)
    own = (right_ops, from_down, from_up, far_a, far_b)
    mate = tuple(lax.ppermute(part, "core", swap) for part in own)
    metas = lax.all_to_all(jnp.broadcast_to(meta[None], (GROUP,) + meta.shape), SHARERS, 0, 0, tiled=True)
    rows = left_ops.reshape(ops, width // GRAIN, GROUP, SLICE, width).transpose(2, 0, 1, 3, 4)
    left_rows = lax.all_to_all(rows, SHARERS, 0, 0, tiled=True)
    return left_rows.reshape(ops * width, width), own + mate, metas


def body(
    wavefunction,
    left_ops,
    right_ops,
    sector_dims,
    coupling_source,
    coupling_target,
    coupling_operator,
):
    ops, width, _ = left_ops.shape
    wave = lax.all_gather(wavefunction, SECTOR, axis=0, tiled=True)
    sectors = wave.shape[0]
    meta = jnp.stack([coupling_source, coupling_target, coupling_operator])
    left_rows, rights, metas = share_operators(left_ops, right_ops, meta)
    first_op = ops * jnp.arange(GROUP, dtype=jnp.int32)[:, None]
    table, stack_op, stack_count = plan_couplings(
        metas[:, 0].reshape(-1), metas[:, 1].reshape(-1), (metas[:, 2] + first_op).reshape(-1),
        ops * GROUP, sectors,
    )
    smem = pl.BlockSpec(memory_space=pltpu.SMEM)
    hbm = pl.BlockSpec(memory_space=pltpu.HBM)
    vmem = pl.BlockSpec(memory_space=pltpu.VMEM)
    rows = width // GROUP
    partial = pl.pallas_call(
        couplings_kernel,
        out_shape=jax.ShapeDtypeStruct((2, sectors, rows // 2, width), jnp.bfloat16),
        in_specs=[smem] * 4 + [hbm] * 12,
        out_specs=vmem,
        scratch_shapes=[
            pltpu.VMEM((ops * width, width), jnp.bfloat16),
            pltpu.VMEM((ops * GROUP, width, width), jnp.bfloat16),
            pltpu.VMEM((sectors, width, width), jnp.bfloat16),
            pltpu.VMEM((sectors, ops * width, width), jnp.bfloat16),
            pltpu.VMEM((sectors + 1, rows, width), jnp.float32),
            pltpu.SemaphoreType.DMA((11,)),
            pltpu.SemaphoreType.DMA((sectors,)),
        ],
        compiler_params=pltpu.CompilerParams(vmem_limit_bytes=56 * MIB),
        name="couplings",
    )(table, stack_op, stack_count, sector_dims, left_rows, *rights, wave)
    got = lax.all_to_all(partial.reshape(sectors, 2, rows // 2, width), REDUCE, 0, 0, tiled=True)
    share = jnp.sum(got.astype(jnp.float32), axis=0)
    x_hi, y, core = (lax.axis_index(name) for name in SPREAD)
    place = jnp.arange(rows // 2, dtype=jnp.int32)
    row = (x_hi * 2 + place // SLICE) * GRAIN + (y * 2 + core) * SLICE + place % SLICE
    column = jnp.arange(width, dtype=jnp.int32)
    own_pair = lax.axis_index("x_lo") * RING + lax.axis_index("z")
    limit = lax.dynamic_slice_in_dim(sector_dims, 2 * own_pair, 2)[:, None, None]
    kept = (row[None, :, None] < limit) & (column[None, None, :] < limit)
    share = jnp.where(kept, share, 0.0).astype(jnp.bfloat16)
    spread = jnp.broadcast_to(share[None], (GROUP,) + share.shape).reshape((2 * GROUP,) + share.shape[1:])
    whole = lax.all_to_all(spread, SPREAD, 0, 0, tiled=True)
    whole = whole.reshape(2, GROUP, 2, SLICE, width).transpose(0, 2, 1, 3, 4)
    return whole.reshape(1, width, width).astype(jnp.float32)


def solution(mesh):
    fine = Mesh(mesh.devices.reshape(SIZES), AXES)
    everyone = P(AXES)
    placed = (
        P(SECTOR, None, None),
        P(AXES, None, None),
        P(AXES, None, None),
        P(),
        everyone,
        everyone,
        everyone,
    )
    return jax.shard_map(
        body, mesh=fine, in_specs=placed, out_specs=P(SECTOR, None, None), check_vma=False
    )
```

time: 568 us -> 144 us (0.25); the launches traced: 561 us -> 143 us
  waiting for transfers between devices: 239 us -> 53.3 us
  loops' own time: 134 us -> 0 us
  matrix products: 89.4 us -> 0 us
  local copies, waits for them, and re-layouts: 54.6 us -> 6.18 us
  other arithmetic: 30.3 us -> 3.72 us
  starting transfers between devices: 0.08 us -> 24.9 us
  Pallas kernels: 0 us -> 23.9 us
  blocking collectives: 0 us -> 17.5 us
    another operation x1 -> x0, loops' own time: 134 us -> none  [body(): lax.scan(advance, start_blocks, (coupling_source, coupling_target, coupli...]
    reduce_scatter x1 -> x0, waiting for transfers between devices: 97.6 us -> none  [body(): lax.psum_scatter(partial_blocks, 'sector', scatter_dimension=0, tiled=True)]
    dot_general x24 -> x0, matrix products: 89.4 us -> none  [advance(): jnp.dot(halfway, right_ops[chosen], preferred_element_type=jnp.float32)]
    psum x1 -> x0, waiting for transfers between devices: 84.2 us -> none  [body(): summed = lax.psum(own_part, 'term')]
    all_gather x1, waiting for transfers between devices: 56.8 us -> 0.01 us  [body(): wave = lax.all_gather(wavefunction, SECTOR, axis=0, tiled=True)]
    dynamic_slice x73 -> x1, local copies, waits for them, and re-layouts: 46.7 us -> 0.08 us  [body(): lax.dynamic_slice_in_dim(sector_dims, 2 * own_pair, 2)[:, None, None]]
    all_to_all x0 -> x3, waiting for transfers between devices: none -> 31.5 us  [the longest x1 16.7 us: share_operators(): lax.all_to_all(jnp.broadcast_to(meta[None], (GROUP,) + meta.shape), SHARE...]
    pallas_call x0 -> x1, Pallas kernels: none -> 23.9 us  [body(): pl.pallas_call(couplings_kernel, out_shape=jax.ShapeDtypeStruct((2, secto...]
  transfers between devices with their start and end apart: 3 -> 13, of which waited for: 3 -> 5; matrix products, arithmetic and copies ran while one was open for 0% -> 6% of each run, Pallas kernels for 0% -> 0%
where the time goes in v3:
time: 144 us; the launch traced here: 143 us
  waiting for transfers between devices  53.3 us (37%)
  starting transfers between devices  24.9 us (17%)
  Pallas kernels  23.9 us (17%)
  blocking collectives  17.5 us (12%)
  between operations  13.5 us (9%)
  local copies, waits for them, and re-layouts  6.18 us (4%)
  other arithmetic  3.72 us (3%)
    pallas_call x1, Pallas kernels, body(): pl.pallas_call(couplings_kernel, out_shape=jax.ShapeDtypeStruct((2, secto...  23.9 us
    ppermute x1, waiting for transfers between devices, share_operators(): far_a = lax.ppermute(from_down[:1], 'y', down)  19.7 us
    all_to_all x1, blocking collectives, body(): whole = lax.all_to_all(spread, SPREAD, 0, 0, tiled=True)  17.5 us
    all_to_all x1, waiting for transfers between devices, share_operators(): lax.all_to_all(jnp.broadcast_to(meta[None], (GROUP,) + meta.shape), SHARE...  16.7 us
    all_to_all x1, waiting for transfers between devices, body(): lax.all_to_all(partial.reshape(sectors, 2, rows // 2, width), REDUCE, 0,...  14.8 us
    all_to_all x1, starting transfers between devices, body(): lax.all_to_all(partial.reshape(sectors, 2, rows // 2, width), REDUCE, 0,...  8.49 us
    all_to_all x1, starting transfers between devices, share_operators(): left_rows = lax.all_to_all(rows, SHARERS, 0, 0, tiled=True)  4.17 us
    all_to_all x1, starting transfers between devices, share_operators(): lax.all_to_all(jnp.broadcast_to(meta[None], (GROUP,) + meta.shape), SHARE...  3.45 us
  transfers between devices with their start and end apart: 13, of which 5 were waited for; matrix products, arithmetic and copies ran while one was open for 6% of the time, Pallas kernels for 0%

profile of v3, /device:TPU:1, one launch (start us, length us, event | category | flops | bytes accessed | tf_op | source)
XLA Modules:
  0.0 143.1 jit_solution(6522120753889913569)
XLA Ops:
  6.5 0.7 all-gather.2.cloned.1.call-update
  7.3 2.2 %collective-permute-start = (bf16[2,512,512]{2,1,0:T(8,128)(2,1)}, bf16[2,512,512]{2,1,0:T(8,128)(2,1)S(1)}, u32[]{:S(2)}, u32[]{:S(2)}) collective-permute-start(bf16[2,512,512]{2,1,0:T(8,128)(2,1)} %own.1), channel_id=1, source_target_pairs={{0,16},{16,32},{32,48},{48,0},{1,17},{17,33},{33,49},{49,1},{2,18}... | collective-permute-start | bytes 3145736 | tf_op jit(solution)/shard_map/ppermute | solution.py:126
  9.5 1.5 %collective-permute-start.1 = (bf16[2,512,512]{2,1,0:T(8,128)(2,1)}, bf16[2,512,512]{2,1,0:T(8,128)(2,1)S(1)}, u32[]{:S(2)}, u32[]{:S(2)}) collective-permute-start(bf16[2,512,512]{2,1,0:T(8,128)(2,1)} %own.1), channel_id=1, source_target_pairs={{0,48},{16,0},{32,16},{48,32},{1,49},{17,1},{33,17},{49,33},{2,50}... | collective-permute-start | bytes 3145736 | tf_op jit(solution)/shard_map/ppermute | solution.py:127
  11.0 1.0 collective-permute-start.4
  12.0 0.7 pad_add_fusion
  13.3 3.5 %all-to-all-start = ((s32[8,3,24]{2,1,0:T(4,128)}), s32[8,3,24]{2,1,0:T(4,128)S(1)}, u32[]{:S(2)}, u32[]{:S(2)}) async-start(s32[8,3,24]{2,1,0:T(4,128)} %broadcast_in_dim.45), calls=%async_computation | async-start | bytes 32768 | tf_op jit(solution)/shard_map/all_to_all | solution.py:132
  16.9 2.3 %copy.17 = bf16[2,4,8,16,512]{4,3,1,0,2:T(8,128)(2,1)} copy(bf16[2,4,8,16,512]{4,3,2,1,0:T(8,128)(2,1)} %bitcast.20) | data formatting | bytes 2097152 | tf_op jit(solution)/shard_map/reshape | solution.py:133
  19.2 16.7 %all-to-all-done = s32[8,3,24]{2,1,0:T(4,128)S(1)} async-done(((s32[8,3,24]{2,1,0:T(4,128)}), s32[8,3,24]{2,1,0:T(4,128)S(1)}, u32[]{:S(2)}, u32[]{:S(2)}) %all-to-all-start) | async-done | bytes 2336 | tf_op jit(solution)/shard_map/all_to_all | solution.py:132
  35.9 4.2 %all-to-all-start.1 = ((bf16[8,2,4,16,512]{4,3,2,1,0:T(8,128)(2,1)}), bf16[8,2,4,16,512]{4,3,2,1,0:T(8,128)(2,1)S(1)}, u32[]{:S(2)}, u32[]{:S(2)}) async-start(bf16[8,2,4,16,512]{4,3,2,1,0:T(8,128)(2,1)} %bitcast.15), calls=%async_computation.1 | async-start | bytes 2097152 | tf_op jit(solution)/shard_map/all_to_all | solution.py:134
  40.4 0.7 fusion.7
  41.1 0.9 slice.23
  42.0 1.4 collective-permute-start.2
  43.4 0.9 slice.24
  44.3 1.3 collective-permute-start.3
  45.6 0.6 collective-permute-start.5
  46.6 19.7 %collective-permute-done.2.own_far_a = bf16[1,512,512]{2,1,0:T(8,128)(2,1)} collective-permute-done((bf16[1,512,512]{2,1,0:T(8,128)(2,1)}, bf16[1,512,512]{2,1,0:T(8,128)(2,1)}, u32[]{:S(2)}, u32[]{:S(2)}) %collective-permute-start.2) | collective-permute-done | bytes 524320 | tf_op jit(solution)/shard_map/ppermute | solution.py:128
  66.4 0.7 collective-permute-start.7
  68.3 0.6 collective-permute-done.7.mate_far_a
  69.0 0.7 collective-permute-done.8.mate_far_b
  69.8 23.9 %couplings.1 = bf16[2,16,32,512]{3,2,1,0:T(8,128)(2,1)} custom-call(s32[240]{0:T(256)} %broadcast_add_fusion.table, s32[60]{0:T(128)} %broadcast_minimum_fusion.stack_op, s32[1]{0:T(128)} %bitcast.3.stack_count, s32[16]{0:T(128)} %dims.1, bf16[1024,512]{1,0:T(8,128)(2,1)} %bitcast.16, bf16[2,512,512]{2,1,0:T(8,128)(2,1)} %own.1, ...), custom_call_target="tpu_custom_call" | custom-call | tf_op jit(solution)/shard_map/couplings/pallas_call | solution.py:161
  93.7 8.5 %all-to-all-start.2 = ((bf16[16,2,32,512]{3,2,1,0:T(8,128)(2,1)}), bf16[16,2,32,512]{3,2,1,0:T(8,128)(2,1)S(1)}, u32[]{:S(2)}, u32[]{:S(2)}) async-start(bf16[16,2,32,512]{3,2,1,0:T(8,128)(2,1)} %bitcast.17), calls=%async_computation.2 | async-start | bytes 2097152 | tf_op jit(solution)/shard_map/all_to_all | solution.py:178
  102.4 14.8 %all-to-all-done.2 = bf16[16,2,32,512]{3,2,1,0:T(8,128)(2,1)S(1)} async-done(((bf16[16,2,32,512]{3,2,1,0:T(8,128)(2,1)}), bf16[16,2,32,512]{3,2,1,0:T(8,128)(2,1)S(1)}, u32[]{:S(2)}, u32[]{:S(2)}) %all-to-all-start.2) | async-done | bytes 1048608 | tf_op jit(solution)/shard_map/all_to_all | solution.py:178
  117.5 17.5 %all_to_all.20 = bf16[16,32,512]{2,1,0:T(8,128)(2,1)S(1)} all-to-all(bf16[16,32,512]{2,1,0:T(8,128)(2,1)S(1)} %bitcast.19), channel_id=1, replica_groups=mesh['x_hi'=2,'y'=4,'x_lo'=2,'z'=4,'core'=2] {'x_hi','y','core'}, dimensions={0} | all-to-all | bytes 1048576 | tf_op jit(solution)/shard_map/all_to_all | solution.py:189
  135.2 1.1 copy.15
  (45 shorter events, 3.4 us)
Async XLA Ops:
  6.5 63.2 %all-gather.2.cloned.1.call-start = ((), (), s32[]{:S(2)}) async-start(), calls=%async_computation.4 | async-start | bytes 8912896 | tf_op jit(solution)/shard_map/all_gather | solution.py:148
  7.3 33.8 %collective-permute-start = (bf16[2,512,512]{2,1,0:T(8,128)(2,1)}, bf16[2,512,512]{2,1,0:T(8,128)(2,1)S(1)}, u32[]{:S(2)}, u32[]{:S(2)}) collective-permute-start(bf16[2,512,512]{2,1,0:T(8,128)(2,1)} %own.1), channel_id=1, source_target_pairs={{0,16},{16,32},{32,48},{48,0},{1,17},{17,33},{33,49},{49,1},{2,18}... | collective-permute-start | bytes 3145736 | tf_op jit(solution)/shard_map/ppermute | solution.py:126
  9.5 33.9 %collective-permute-start.1 = (bf16[2,512,512]{2,1,0:T(8,128)(2,1)}, bf16[2,512,512]{2,1,0:T(8,128)(2,1)S(1)}, u32[]{:S(2)}, u32[]{:S(2)}) collective-permute-start(bf16[2,512,512]{2,1,0:T(8,128)(2,1)} %own.1), channel_id=1, source_target_pairs={{0,48},{16,0},{32,16},{48,32},{1,49},{17,1},{33,17},{49,33},{2,50}... | collective-permute-start | bytes 3145736 | tf_op jit(solution)/shard_map/ppermute | solution.py:127
  11.0 57.3 %collective-permute-start.4 = (bf16[2,512,512]{2,1,0:T(8,128)(2,1)}, bf16[2,512,512]{2,1,0:T(8,128)(2,1)}, u32[]{:S(2)}, u32[]{:S(2)}) collective-permute-start(bf16[2,512,512]{2,1,0:T(8,128)(2,1)} %own.1), channel_id=1, source_target_pairs={{0,1},{1,0},{2,3},{3,2},{4,5},{5,4},{6,7},{7,6},{8,9},{9,8},{10,11... | collective-permute-start | bytes 3145736 | tf_op jit(solution)/shard_map/ppermute | solution.py:131
  13.3 22.6 %all-to-all-start = ((s32[8,3,24]{2,1,0:T(4,128)}), s32[8,3,24]{2,1,0:T(4,128)S(1)}, u32[]{:S(2)}, u32[]{:S(2)}) async-start(s32[8,3,24]{2,1,0:T(4,128)} %broadcast_in_dim.45), calls=%async_computation | async-start | bytes 32768 | tf_op jit(solution)/shard_map/all_to_all | solution.py:132
  35.9 32.4 %all-to-all-start.1 = ((bf16[8,2,4,16,512]{4,3,2,1,0:T(8,128)(2,1)}), bf16[8,2,4,16,512]{4,3,2,1,0:T(8,128)(2,1)S(1)}, u32[]{:S(2)}, u32[]{:S(2)}) async-start(bf16[8,2,4,16,512]{4,3,2,1,0:T(8,128)(2,1)} %bitcast.15), calls=%async_computation.1 | async-start | bytes 2097152 | tf_op jit(solution)/shard_map/all_to_all | solution.py:134
  41.1 28.6 %copy-start.1 = (bf16[2,512,512]{2,1,0:T(8,128)(2,1)}, bf16[2,512,512]{2,1,0:T(8,128)(2,1)S(1)}, u32[]{:S(2)}) copy-start(bf16[2,512,512]{2,1,0:T(8,128)(2,1)S(1)} %collective-permute-done.own_down) | copy-start | bytes 3145732
  42.0 24.4 %collective-permute-start.2 = (bf16[1,512,512]{2,1,0:T(8,128)(2,1)}, bf16[1,512,512]{2,1,0:T(8,128)(2,1)}, u32[]{:S(2)}, u32[]{:S(2)}) collective-permute-start(bf16[1,512,512]{2,1,0:T(8,128)(2,1)} %slice.23), channel_id=1, source_target_pairs={{0,16},{16,32},{32,48},{48,0},{1,17},{17,33},{33,49},{49,1},{2,18}... | collective-permute-start | bytes 1572872 | tf_op jit(solution)/shard_map/ppermute | solution.py:128
  43.4 26.4 %copy-start.2 = (bf16[2,512,512]{2,1,0:T(8,128)(2,1)}, bf16[2,512,512]{2,1,0:T(8,128)(2,1)S(1)}, u32[]{:S(2)}) copy-start(bf16[2,512,512]{2,1,0:T(8,128)(2,1)S(1)} %collective-permute-done.1.own_up) | copy-start | bytes 3145732
  44.3 22.8 %collective-permute-start.3 = (bf16[1,512,512]{2,1,0:T(8,128)(2,1)}, bf16[1,512,512]{2,1,0:T(8,128)(2,1)}, u32[]{:S(2)}, u32[]{:S(2)}) collective-permute-start(bf16[1,512,512]{2,1,0:T(8,128)(2,1)} %slice.24), channel_id=1, source_target_pairs={{0,48},{16,0},{32,16},{48,32},{1,49},{17,1},{33,17},{49,33},{2,50}... | collective-permute-start | bytes 1572872 | tf_op jit(solution)/shard_map/ppermute | solution.py:129
  45.6 24.1 %collective-permute-start.5 = (bf16[2,512,512]{2,1,0:T(8,128)(2,1)S(1)}, bf16[2,512,512]{2,1,0:T(8,128)(2,1)}, u32[]{:S(2)}, u32[]{:S(2)}) collective-permute-start(bf16[2,512,512]{2,1,0:T(8,128)(2,1)S(1)} %collective-permute-done.own_down), channel_id=1, source_target_pairs={{0,1},{1,0},{2,3},{3,2},{4,5},{5,4},{6,7},{7,6},{8,9},{9,8},{10,11... | collective-permute-start | bytes 3145736 | tf_op jit(solution)/shard_map/ppermute | solution.py:131
  46.2 23.5 %collective-permute-start.6 = (bf16[2,512,512]{2,1,0:T(8,128)(2,1)S(1)}, bf16[2,512,512]{2,1,0:T(8,128)(2,1)}, u32[]{:S(2)}, u32[]{:S(2)}) collective-permute-start(bf16[2,512,512]{2,1,0:T(8,128)(2,1)S(1)} %collective-permute-done.1.own_up), channel_id=1, source_target_pairs={{0,1},{1,0},{2,3},{3,2},{4,5},{5,4},{6,7},{7,6},{8,9},{9,8},{10,11... | collective-permute-start | bytes 3145736 | tf_op jit(solution)/shard_map/ppermute | solution.py:131
  66.4 2.6 %collective-permute-start.7 = (bf16[1,512,512]{2,1,0:T(8,128)(2,1)}, bf16[1,512,512]{2,1,0:T(8,128)(2,1)}, u32[]{:S(2)}, u32[]{:S(2)}) collective-permute-start(bf16[1,512,512]{2,1,0:T(8,128)(2,1)} %collective-permute-done.2.own_far_a), channel_id=1, source_target_pairs={{0,1},{1,0},{2,3},{3,2},{4,5},{5,4},{6,7},{7,6},{8,9},{9,8},{10,11... | collective-permute-start | bytes 1572872 | tf_op jit(solution)/shard_map/ppermute | solution.py:131
  67.1 2.6 %collective-permute-start.8 = (bf16[1,512,512]{2,1,0:T(8,128)(2,1)}, bf16[1,512,512]{2,1,0:T(8,128)(2,1)}, u32[]{:S(2)}, u32[]{:S(2)}) collective-permute-start(bf16[1,512,512]{2,1,0:T(8,128)(2,1)} %collective-permute-done.3.own_far_b), channel_id=1, source_target_pairs={{0,1},{1,0},{2,3},{3,2},{4,5},{5,4},{6,7},{7,6},{8,9},{9,8},{10,11... | collective-permute-start | bytes 1572872 | tf_op jit(solution)/shard_map/ppermute | solution.py:131
  68.3 1.4 %copy-start = (bf16[8,2,4,16,512]{4,3,2,1,0:T(8,128)(2,1)}, bf16[8,2,4,16,512]{4,3,2,1,0:T(8,128)(2,1)S(1)}, u32[]{:S(2)}) copy-start(bf16[8,2,4,16,512]{4,3,2,1,0:T(8,128)(2,1)S(1)} %all-to-all-done.1) | copy-start | bytes 3145732
  69.7 32.4 %copy-start.3 = (s32[16]{0:T(128)S(1)}, s32[16]{0:T(128)}, u32[]{:S(2)}) copy-start(s32[16]{0:T(128)} %dims.1) | copy-start | bytes 196
  93.7 23.5 %all-to-all-start.2 = ((bf16[16,2,32,512]{3,2,1,0:T(8,128)(2,1)}), bf16[16,2,32,512]{3,2,1,0:T(8,128)(2,1)S(1)}, u32[]{:S(2)}, u32[]{:S(2)}) async-start(bf16[16,2,32,512]{3,2,1,0:T(8,128)(2,1)} %bitcast.17), calls=%async_computation.2 | async-start | bytes 2097152 | tf_op jit(solution)/shard_map/all_to_all | solution.py:178
Sparse Core Ops, SparseCore 0:
  9.1 55.7 all-gather.1

commit v4 on v3

v4 whole, which is shorter than its diff:
```python
import jax
import jax.numpy as jnp
from jax import lax
from jax.experimental import pallas as pl
from jax.experimental.pallas import tpu as pltpu
from jax.sharding import Mesh, PartitionSpec as P

AXES = ("x_hi", "y_hi", "y_lo", "x_lo", "z", "core")
SIZES = (2, 2, 2, 2, 4, 2)
SECTOR = ("x_lo", "z", "core")
SHARERS = ("y_lo", "core")
REDUCE = ("x_hi", "y_hi", "x_lo", "z")
SPREAD = ("x_hi", "y_hi", "y_lo", "core")
RING = 4
GROUP = 4
LEVELS = 4
GRAIN = 128
SLICE = GRAIN // GROUP
STACK = 4
UNROLL = 2
MIB = 1024 * 1024
SWAP = [(0, 1), (1, 0)]
UP = [(i, (i + 1) % RING) for i in range(RING)]
DOWN = [(i, (i - 1) % RING) for i in range(RING)]
SHIFTS = (0, RING - 1, 1, 2)


def plan_couplings(source, target, chosen, operators, sectors):
    count = source.shape[0]
    stacks = -(-(count + operators * (STACK - 1)) // STACK)
    stacks = -(-stacks // UNROLL) * UNROLL
    is_op = chosen[:, None] == jnp.arange(operators, dtype=jnp.int32)[None, :]
    number = jnp.sum(is_op.astype(jnp.int32), axis=0)
    taken = (number + STACK - 1) // STACK
    op = jnp.arange(operators, dtype=jnp.int32)
    end = jnp.sum(jnp.where(op[:, None] <= op[None, :], taken[:, None], 0), axis=0)
    start = end - taken
    spot = jnp.arange(count, dtype=jnp.int32)
    earlier = (chosen[:, None] == chosen[None, :]) & (spot[:, None] < spot[None, :])
    rank = jnp.sum(earlier.astype(jnp.int32), axis=0)
    place = rank + STACK * jnp.sum(jnp.where(is_op, start[None, :], 0), axis=1)
    here = place[:, None] == jnp.arange(stacks * STACK, dtype=jnp.int32)[None, :]
    code = source * (2 * sectors) + target - sectors
    table = sectors + jnp.sum(jnp.where(here, code[:, None], 0), axis=0)
    stack = jnp.arange(stacks, dtype=jnp.int32)
    stack_op = jnp.sum((end[:, None] <= stack[None, :]).astype(jnp.int32), axis=0)
    return table, jnp.minimum(stack_op, operators - 1), jnp.max(end)[None]


def couplings_kernel(table, stack_op, stack_count, dims, *refs):
    own_waves, mate_waves = refs[:11], refs[11:22]
    own_right, own_left, mate_right, mate_left, far_right, far_left, far_mate_right, far_mate_left = refs[22:30]
    out, left, right, waves, halves, sums, op_sems, wave_sems = refs[30:]
    y, x, z, core = (lax.axis_index(name) for name in ("y_lo", "x_lo", "z", "core"))
    sectors, width, _ = waves.shape
    rows = sums.shape[1]
    ops = own_right.shape[0]
    half = width // 2
    left_copies, right_copies = [], []
    for n, (pair, c, left_rows, right_ops) in enumerate((
        (y, core, own_left, own_right),
        (y, 1 - core, mate_left, mate_right),
        (1 - y, core, far_left, far_right),
        (1 - y, 1 - core, far_mate_left, far_mate_right),
    )):
        first = (pair * 2 + c) * ops
        size = ops * rows
        to = left.at[pl.ds(pl.multiple_of(first * rows, size), size)]
        left_copies.append(pltpu.make_async_copy(left_rows.at[core], to, op_sems.at[2 * n]))
        right_copies.append(
            pltpu.make_async_copy(right_ops, right.at[pl.ds(first, ops)], op_sems.at[2 * n + 1])
        )
    for copy in left_copies:
        copy.start()
    whole, low, high = (pl.ds(0, width), pl.ds(0, half), pl.ds(half, half))
    places = (
        (0, whole), (1, whole), (2, whole), (3, low), (3, high),
        (4, low), (4, high), (5, whole), (6, whole), (7, low), (7, high),
    )
    for c, pieces in ((0, own_waves), (1, mate_waves)):
        for piece, (place, part) in zip(pieces, places):
            slot = c * (sectors // 2) + place
            pltpu.make_async_copy(piece, waves.at[slot, part], wave_sems.at[slot]).start()
    for copy in right_copies:
        copy.start()
    sums[...] = jnp.zeros_like(sums)
    for copy in left_copies:
        copy.wait()

    def first_half(slot, carry):
        pltpu.make_async_copy(waves.at[slot], waves.at[slot], wave_sems.at[slot]).wait()
        other_core = lax.div(slot, sectors // 2)
        other_x = lax.rem(lax.div(slot, RING), 2)
        step = lax.rem(slot, RING)
        shift = jnp.where(step == 1, RING - 1, jnp.where(step == 2, 1, jnp.where(step == 3, 2, 0)))
        x_at = lax.rem(x + other_x, 2)
        core_at = lax.rem(core + other_core, 2)
        s = (x_at * RING + lax.rem(z + shift, RING)) * 2 + core_at
        level = dims[s] // GRAIN
        for sl in range(1, LEVELS + 1):

            @pl.when(level == sl)
            def _(sl=sl):
                inner = sl * GRAIN
                halves[s, :, :inner] = jnp.dot(
                    left[:, :inner], waves[slot, :inner, :inner], preferred_element_type=jnp.float32
                ).astype(jnp.bfloat16)
                if inner < width:
                    halves[s, :, inner:] = jnp.zeros((left.shape[0], width - inner), jnp.bfloat16)

        return carry

    lax.fori_loop(0, sectors, first_half, 0)
    for copy in right_copies:
        copy.wait()

    def second_half(i, carry):
        for u in range(UNROLL):
            j = i * UNROLL + u
            op = stack_op[j]
            first = pl.multiple_of(op * rows, rows)
            codes = [table[j * STACK + k] for k in range(STACK)]
            sources = [lax.div(code, 2 * sectors) for code in codes]
            stacked = jnp.concatenate([halves[s, pl.ds(first, rows), :] for s in sources], axis=0)
            product = jnp.dot(stacked, right[op], preferred_element_type=jnp.float32)
            for k in range(STACK):
                target = lax.rem(codes[k], 2 * sectors)
                sums[target] += product[k * rows:(k + 1) * rows]
        return carry

    lax.fori_loop(0, lax.div(stack_count[0] + UNROLL - 1, UNROLL), second_half, 0)
    parts = out.shape[0]
    size = rows // parts
    for part in range(parts):
        out[part] = sums[:sectors, part * size:(part + 1) * size, :].astype(jnp.bfloat16)


def along_x(part, steps):
    return lax.ppermute(part, ("x_hi", "x_lo"), steps)


def to_mate(part):
    return lax.ppermute(part, "core", SWAP)


def share(block, left_ops, right_ops, meta):
    ops, width, _ = left_ops.shape
    half = width // 2
    rows = left_ops.reshape(ops, LEVELS, 2, 2, SLICE, width).transpose(2, 3, 0, 1, 4, 5)
    rows = rows.reshape(2, 2, ops * LEVELS * SLICE, width)
    y = lax.axis_index("y_lo")
    near_rows = lax.dynamic_index_in_dim(rows, y, 0, keepdims=False)
    sent_rows = lax.dynamic_index_in_dim(rows, 1 - y, 0, keepdims=False)
    far_right = lax.ppermute(right_ops, "y_lo", SWAP)
    far_rows = lax.ppermute(sent_rows, "y_lo", SWAP)
    before = lax.ppermute(block, "z", UP)
    after = lax.ppermute(block, "z", DOWN)
    side_low = along_x(block[:half], UP)
    side_high = along_x(block[half:], DOWN)
    across_low = lax.ppermute(before[:half], "z", UP)
    across_high = lax.ppermute(after[half:], "z", DOWN)
    side_before = along_x(before, UP)
    side_after = along_x(after, DOWN)
    corner_low = along_x(across_low, UP)
    corner_high = along_x(across_high, DOWN)
    metas = lax.all_to_all(jnp.broadcast_to(meta[None], (GROUP,) + meta.shape), SHARERS, 0, 0, tiled=True)
    early = (
        block, before, after, across_low, across_high, side_low, side_high, side_before, side_after,
    )
    own_waves = early + (corner_low, corner_high)
    held = lax.optimization_barrier(early + (right_ops, near_rows, metas))
    metas = held[-1]
    mate_early = [to_mate(part) for part in held[:-1]]
    mate_late = [to_mate(part) for part in lax.optimization_barrier((corner_low, corner_high, far_right, far_rows))]
    mate_waves = tuple(mate_early[:9] + mate_late[:2])
    operators = (right_ops, near_rows, mate_early[9], mate_early[10], far_right, far_rows, mate_late[2], mate_late[3])
    return own_waves + mate_waves + operators, metas


def body(
    wavefunction,
    left_ops,
    right_ops,
    sector_dims,
    coupling_source,
    coupling_target,
    coupling_operator,
):
    ops, width, _ = left_ops.shape
    sectors = 4 * RING
    meta = jnp.stack([coupling_source, coupling_target, coupling_operator])
    shared, metas = share(wavefunction[0], left_ops, right_ops, meta)
    first_op = ops * jnp.arange(GROUP, dtype=jnp.int32)[:, None]
    table, stack_op, stack_count = plan_couplings(
        metas[:, 0].reshape(-1), metas[:, 1].reshape(-1), (metas[:, 2] + first_op).reshape(-1),
        ops * GROUP, sectors,
    )
    smem = pl.BlockSpec(memory_space=pltpu.SMEM)
    hbm = pl.BlockSpec(memory_space=pltpu.HBM)
    vmem = pl.BlockSpec(memory_space=pltpu.VMEM)
    rows = width // GROUP
    partial = pl.pallas_call(
        couplings_kernel,
        out_shape=jax.ShapeDtypeStruct((LEVELS, sectors, SLICE, width), jnp.bfloat16),
        in_specs=[smem] * 4 + [hbm] * len(shared),
        out_specs=vmem,
        scratch_shapes=[
            pltpu.VMEM((ops * width, width), jnp.bfloat16),
            pltpu.VMEM((ops * GROUP, width, width), jnp.bfloat16),
            pltpu.VMEM((sectors, width, width), jnp.bfloat16),
            pltpu.VMEM((sectors, ops * width, width), jnp.bfloat16),
            pltpu.VMEM((sectors + 1, rows, width), jnp.float32),
            pltpu.SemaphoreType.DMA((8,)),
            pltpu.SemaphoreType.DMA((sectors,)),
        ],
        compiler_params=pltpu.CompilerParams(vmem_limit_bytes=56 * MIB),
        name="couplings",
    )(table, stack_op, stack_count, sector_dims, *shared)
    got = lax.all_to_all(partial.reshape(-1, 2, SLICE, width), REDUCE, 0, 0, tiled=True)
    total = jnp.sum(got.astype(jnp.float32), axis=0)
    x_hi, y_hi, y_lo, core = (lax.axis_index(name) for name in SPREAD)
    row = (((x_hi * 2 + y_hi) * 2 + y_lo) * 2 + core) * SLICE + jnp.arange(SLICE, dtype=jnp.int32)
    column = jnp.arange(width, dtype=jnp.int32)
    own_pair = lax.axis_index("x_lo") * RING + lax.axis_index("z")
    limit = lax.dynamic_slice_in_dim(sector_dims, 2 * own_pair, 2)[:, None, None]
    kept = (row[None, :, None] < limit) & (column[None, None, :] < limit)
    total = jnp.where(kept, total, 0.0).astype(jnp.bfloat16)
    spread = jnp.broadcast_to(total[None], (8,) + total.shape).reshape((16,) + total.shape[1:])
    whole = lax.all_to_all(spread, SPREAD, 0, 0, tiled=True)
    return whole.reshape(1, width, width).astype(jnp.float32)


def solution(mesh):
    fine = Mesh(mesh.devices.reshape(SIZES), AXES)
    everyone = P(AXES)
    placed = (
        P(SECTOR, None, None),
        P(AXES, None, None),
        P(AXES, None, None),
        P(),
        everyone,
        everyone,
        everyone,
    )
    return jax.shard_map(
        body, mesh=fine, in_specs=placed, out_specs=P(SECTOR, None, None), check_vma=False
    )
```

time: 144 us -> 139 us (0.965)
  between operations: 13.5 us -> 0.22 us
  starting transfers between devices: 24.9 us -> 34.7 us
  waiting for transfers between devices: 53.3 us -> 48.6 us
  Pallas kernels: 23.9 us -> 25.6 us
  local copies, waits for them, and re-layouts: 6.18 us -> 7.82 us
    ppermute x9 -> x27, starting transfers between devices: 8.79 us -> 20.9 us  [the longest x6 8.17 us: along_x(): return lax.ppermute(part, ('x_hi', 'x_lo'), steps)]
    ppermute x9 -> x27, waiting for transfers between devices: 21.2 us -> 12.4 us  [the longest x1 6.1 us: share(): before = lax.ppermute(block, 'z', UP)]
    all_to_all x3 -> x2, waiting for transfers between devices: 31.5 us -> 36.2 us  [the longest x1 27.6 us: body(): lax.all_to_all(partial.reshape(-1, 2, SLICE, width), REDUCE, 0, 0, tiled=...]
    all_to_all x3 -> x2, starting transfers between devices: 16.1 us -> 13.8 us  [the longest x1 7.96 us: body(): lax.all_to_all(partial.reshape(-1, 2, SLICE, width), REDUCE, 0, 0, tiled=...]
    reshape x1 -> x0, local copies, waits for them, and re-layouts: 2.29 us -> none  [share_operators(): left_ops.reshape(ops, width // GRAIN, GROUP, SLICE, width)]
    unnamed x8 -> x44, local copies, waits for them, and re-layouts: 0.02 us -> 1.96 us
    pallas_call x1, Pallas kernels: 23.9 us -> 25.6 us  [body(): pl.pallas_call(couplings_kernel, out_shape=jax.ShapeDtypeStruct((LEVELS,...]
  transfers between devices with their start and end apart: 13 -> 29, of which waited for: 5 -> 9; matrix products, arithmetic and copies ran while one was open for 6% -> 6% of each run, Pallas kernels for 0% -> 0%
where the time goes in v4:
time: 139 us
  waiting for transfers between devices  48.6 us (35%)
  starting transfers between devices  34.7 us (25%)
  Pallas kernels  25.6 us (18%)
  blocking collectives  18.2 us (13%)
  local copies, waits for them, and re-layouts  7.82 us (6%)
  other arithmetic  4.02 us (3%)
    all_to_all x1, waiting for transfers between devices, body(): lax.all_to_all(partial.reshape(-1, 2, SLICE, width), REDUCE, 0, 0, tiled=...  27.6 us
    pallas_call x1, Pallas kernels, body(): pl.pallas_call(couplings_kernel, out_shape=jax.ShapeDtypeStruct((LEVELS,...  25.6 us
    all_to_all x1, blocking collectives, body(): whole = lax.all_to_all(spread, SPREAD, 0, 0, tiled=True)  18.2 us
    all_to_all x1, waiting for transfers between devices, share(): lax.all_to_all(jnp.broadcast_to(meta[None], (GROUP,) + meta.shape), SHARE...  8.62 us
    ppermute x6, starting transfers between devices, along_x(): return lax.ppermute(part, ('x_hi', 'x_lo'), steps)  8.17 us
    all_to_all x1, starting transfers between devices, body(): lax.all_to_all(partial.reshape(-1, 2, SLICE, width), REDUCE, 0, 0, tiled=...  7.96 us
    ppermute x1, waiting for transfers between devices, share(): before = lax.ppermute(block, 'z', UP)  6.1 us
    all_to_all x1, starting transfers between devices, share(): lax.all_to_all(jnp.broadcast_to(meta[None], (GROUP,) + meta.shape), SHARE...  5.82 us
  transfers between devices with their start and end apart: 29, of which 9 were waited for; matrix products, arithmetic and copies ran while one was open for 6% of the time, Pallas kernels for 0%

profile of v4, /device:TPU:1, one launch (start us, length us, event | category | flops | bytes accessed | tf_op | source)
XLA Modules:
  0.0 139.1 jit_solution(5639402640790559665)
XLA Ops:
  0.0 2.5 %collective-permute-start = (bf16[512,512]{1,0:T(8,128)(2,1)}, bf16[512,512]{1,0:T(8,128)(2,1)S(1)}, u32[]{:S(2)}, u32[]{:S(2)}) collective-permute-start(bf16[512,512]{1,0:T(8,128)(2,1)} %bitcast.25), channel_id=1, source_target_pairs={{0,2},{2,4},{4,6},{6,0},{1,3},{3,5},{5,7},{7,1},{8,10},{10,12},{12... | collective-permute-start | bytes 1572872 | tf_op jit(solution)/shard_map/ppermute | solution.py:156
  2.5 2.1 %collective-permute-start.1 = (bf16[512,512]{1,0:T(8,128)(2,1)}, bf16[512,512]{1,0:T(8,128)(2,1)S(1)}, u32[]{:S(2)}, u32[]{:S(2)}) collective-permute-start(bf16[512,512]{1,0:T(8,128)(2,1)} %bitcast.26), channel_id=1, source_target_pairs={{0,6},{2,0},{4,2},{6,4},{1,7},{3,1},{5,3},{7,5},{8,14},{10,8},{12,... | collective-permute-start | bytes 1572872 | tf_op jit(solution)/shard_map/ppermute | solution.py:157
  4.6 1.8 %slice_bitcast_fusion = (bf16[256,512]{1,0:T(8,128)(2,1)}, bf16[256,512]{1,0:T(8,128)(2,1)S(1)}) fusion(bf16[1,512,512]{2,1,0:T(8,128)(2,1)} %param.7), kind=kLoop, calls=%fused_computation.4 | loop fusion | bytes 1048576 | tf_op jit(solution)/shard_map/slice | solution.py:159
  6.4 1.2 collective-permute-start.4
  7.6 1.3 collective-permute-start.19
  8.9 1.5 %collective-permute-start.5 = (bf16[256,512]{1,0:T(8,128)(2,1)}, bf16[256,512]{1,0:T(8,128)(2,1)}, u32[]{:S(2)}, u32[]{:S(2)}) collective-permute-start(bf16[256,512]{1,0:T(8,128)(2,1)} %get-tuple-element.41), channel_id=1, source_target_pairs={{0,72},{8,0},{64,8},{72,64},{1,73},{9,1},{65,9},{73,65},{2,74},{10... | collective-permute-start | bytes 786440 | tf_op jit(solution)/shard_map/ppermute | solution.py:139
  10.3 6.1 %collective-permute-done.refs_1_ = bf16[512,512]{1,0:T(8,128)(2,1)S(1)} collective-permute-done((bf16[512,512]{1,0:T(8,128)(2,1)}, bf16[512,512]{1,0:T(8,128)(2,1)S(1)}, u32[]{:S(2)}, u32[]{:S(2)}) %collective-permute-start) | collective-permute-done | bytes 524320 | tf_op jit(solution)/shard_map/ppermute | solution.py:156
  17.2 1.3 collective-permute-start.6
  18.5 1.4 copy.10
  19.9 1.5 %collective-permute-start.7 = (bf16[512,512]{1,0:T(8,128)(2,1)S(1)}, bf16[512,512]{1,0:T(8,128)(2,1)}, u32[]{:S(2)}, u32[]{:S(2)}) collective-permute-start(bf16[512,512]{1,0:T(8,128)(2,1)S(1)} %collective-permute-done.1.refs_2_), channel_id=1, source_target_pairs={{0,72},{8,0},{64,8},{72,64},{1,73},{9,1},{65,9},{73,65},{2,74},{10... | collective-permute-start | bytes 1572872 | tf_op jit(solution)/shard_map/ppermute | solution.py:139
  22.3 1.3 collective-permute-start.20
  23.7 1.7 %collective-permute-done.2.refs_3_ = bf16[256,512]{1,0:T(8,128)(2,1)} collective-permute-done((bf16[256,512]{1,0:T(8,128)(2,1)}, bf16[256,512]{1,0:T(8,128)(2,1)}, u32[]{:S(2)}, u32[]{:S(2)}) %collective-permute-start.2) | collective-permute-done | bytes 262176 | tf_op jit(solution)/shard_map/ppermute | solution.py:160
  25.3 1.0 collective-permute-start.3
  27.0 5.8 %all-to-all-start = ((s32[4,3,24]{2,1,0:T(4,128)}), s32[4,3,24]{2,1,0:T(4,128)S(1)}, u32[]{:S(2)}, u32[]{:S(2)}) async-start(s32[4,3,24]{2,1,0:T(4,128)} %broadcast_in_dim.45), calls=%async_computation | async-start | bytes 16384 | tf_op jit(solution)/shard_map/all_to_all | solution.py:166
  32.8 2.6 %collective-permute-start.9 = (bf16[256,512]{1,0:T(8,128)(2,1)S(1)}, bf16[256,512]{1,0:T(8,128)(2,1)}, u32[]{:S(2)}, u32[]{:S(2)}) collective-permute-start(bf16[256,512]{1,0:T(8,128)(2,1)S(1)} %collective-permute-done.3.refs_4_), channel_id=1, source_target_pairs={{0,72},{8,0},{64,8},{72,64},{1,73},{9,1},{65,9},{73,65},{2,74},{10... | collective-permute-start | bytes 786440 | tf_op jit(solution)/shard_map/ppermute | solution.py:139
  35.6 8.6 %all-to-all-done = s32[4,3,24]{2,1,0:T(4,128)S(1)} async-done(((s32[4,3,24]{2,1,0:T(4,128)}), s32[4,3,24]{2,1,0:T(4,128)S(1)}, u32[]{:S(2)}, u32[]{:S(2)}) %all-to-all-start) | async-done | bytes 1184 | tf_op jit(solution)/shard_map/all_to_all | solution.py:166
  50.6 1.6 %collective-permute-done.11.refs_12_ = bf16[512,512]{1,0:T(8,128)(2,1)} collective-permute-done((bf16[512,512]{1,0:T(8,128)(2,1)S(1)}, bf16[512,512]{1,0:T(8,128)(2,1)}, u32[]{:S(2)}, u32[]{:S(2)}) %collective-permute-start.11) | collective-permute-done | bytes 524320 | tf_op jit(solution)/shard_map/ppermute | solution.py:143
  52.6 1.2 collective-permute-done.12.refs_13_
  55.4 1.1 collective-permute-done.24.refs_25_
  58.0 25.6 %couplings.1 = bf16[4,16,32,512]{3,2,1,0:T(8,128)(2,1)} custom-call(s32[120]{0:T(128)} %broadcast_add_fusion.table, s32[30]{0:T(128)} %broadcast_minimum_fusion.stack_op, s32[1]{0:T(128)} %bitcast.10.stack_count, s32[16]{0:T(128)} %dims.1, bf16[512,512]{1,0:T(8,128)(2,1)} %bitcast.27, bf16[512,512]{1,0:T(8,128)(2,1)} %copy-done.2, ...), custom_call_target="tpu_custom_call" | custom-call | tf_op jit(solution)/shard_map/couplings/pallas_call | solution.py:202
  83.5 8.0 %all-to-all-start.1 = ((bf16[32,2,32,512]{3,2,1,0:T(8,128)(2,1)}), bf16[32,2,32,512]{3,2,1,0:T(8,128)(2,1)S(1)}, u32[]{:S(2)}, u32[]{:S(2)}) async-start(bf16[32,2,32,512]{3,2,1,0:T(8,128)(2,1)} %bitcast.23), calls=%async_computation.1 | async-start | bytes 4194304 | tf_op jit(solution)/shard_map/all_to_all | solution.py:219
  91.7 27.6 %all-to-all-done.1 = bf16[32,2,32,512]{3,2,1,0:T(8,128)(2,1)S(1)} async-done(((bf16[32,2,32,512]{3,2,1,0:T(8,128)(2,1)}), bf16[32,2,32,512]{3,2,1,0:T(8,128)(2,1)S(1)}, u32[]{:S(2)}, u32[]{:S(2)}) %all-to-all-start.1) | async-done | bytes 2097184 | tf_op jit(solution)/shard_map/all_to_all | solution.py:219
  119.7 18.2 %all_to_all.15 = bf16[16,32,512]{2,1,0:T(8,128)(2,1)S(1)} all-to-all(bf16[16,32,512]{2,1,0:T(8,128)(2,1)S(1)} %bitcast.30), channel_id=1, replica_groups=mesh['x_hi'=2,'y_hi'=2,'y_lo'=2,'x_lo'=2,'z'=4,'core'=2] {'x_hi','y_hi',..., dimensions={0} | all-to-all | bytes 1048576 | tf_op jit(solution)/shard_map/all_to_all | solution.py:229
  137.9 1.1 bitcast_convert_fusion
  (113 shorter events, 12.9 us)
Async XLA Ops:
  0.0 16.4 %collective-permute-start = (bf16[512,512]{1,0:T(8,128)(2,1)}, bf16[512,512]{1,0:T(8,128)(2,1)S(1)}, u32[]{:S(2)}, u32[]{:S(2)}) collective-permute-start(bf16[512,512]{1,0:T(8,128)(2,1)} %bitcast.25), channel_id=1, source_target_pairs={{0,2},{2,4},{4,6},{6,0},{1,3},{3,5},{5,7},{7,1},{8,10},{10,12},{12... | collective-permute-start | bytes 1572872 | tf_op jit(solution)/shard_map/ppermute | solution.py:156
  2.5 17.4 %collective-permute-start.1 = (bf16[512,512]{1,0:T(8,128)(2,1)}, bf16[512,512]{1,0:T(8,128)(2,1)S(1)}, u32[]{:S(2)}, u32[]{:S(2)}) collective-permute-start(bf16[512,512]{1,0:T(8,128)(2,1)} %bitcast.26), channel_id=1, source_target_pairs={{0,6},{2,0},{4,2},{6,4},{1,7},{3,1},{5,3},{7,5},{8,14},{10,8},{12,... | collective-permute-start | bytes 1572872 | tf_op jit(solution)/shard_map/ppermute | solution.py:157
  6.4 10.9 %collective-permute-start.4 = (bf16[256,512]{1,0:T(8,128)(2,1)S(1)}, bf16[256,512]{1,0:T(8,128)(2,1)S(1)}, u32[]{:S(2)}, u32[]{:S(2)}) collective-permute-start(bf16[256,512]{1,0:T(8,128)(2,1)S(1)} %get-tuple-element.42), channel_id=1, source_target_pairs={{0,8},{8,64},{64,72},{72,0},{1,9},{9,65},{65,73},{73,1},{2,10},{10... | collective-permute-start | bytes 786440 | tf_op jit(solution)/shard_map/ppermute | solution.py:139
  7.6 38.2 %collective-permute-start.19 = (bf16[2,512,512]{2,1,0:T(8,128)(2,1)}, bf16[2,512,512]{2,1,0:T(8,128)(2,1)}, u32[]{:S(2)}, u32[]{:S(2)}) collective-permute-start(bf16[2,512,512]{2,1,0:T(8,128)(2,1)} %refs_22_.1), channel_id=1, source_target_pairs={{0,16},{16,0},{1,17},{17,1},{2,18},{18,2},{3,19},{19,3},{4,20},{20... | collective-permute-start | bytes 3145736 | tf_op jit(solution)/shard_map/ppermute | solution.py:154
  8.9 13.5 %collective-permute-start.5 = (bf16[256,512]{1,0:T(8,128)(2,1)}, bf16[256,512]{1,0:T(8,128)(2,1)}, u32[]{:S(2)}, u32[]{:S(2)}) collective-permute-start(bf16[256,512]{1,0:T(8,128)(2,1)} %get-tuple-element.41), channel_id=1, source_target_pairs={{0,72},{8,0},{64,8},{72,64},{1,73},{9,1},{65,9},{73,65},{2,74},{10... | collective-permute-start | bytes 786440 | tf_op jit(solution)/shard_map/ppermute | solution.py:139
  17.2 8.1 %collective-permute-start.2 = (bf16[256,512]{1,0:T(8,128)(2,1)}, bf16[256,512]{1,0:T(8,128)(2,1)}, u32[]{:S(2)}, u32[]{:S(2)}) collective-permute-start(bf16[256,512]{1,0:T(8,128)(2,1)} %slice.36), channel_id=1, source_target_pairs={{0,2},{2,4},{4,6},{6,0},{1,3},{3,5},{5,7},{7,1},{8,10},{10,12},{12... | collective-permute-start | bytes 786440 | tf_op jit(solution)/shard_map/ppermute | solution.py:160
  17.2 15.6 %collective-permute-start.6 = (bf16[512,512]{1,0:T(8,128)(2,1)S(1)}, bf16[512,512]{1,0:T(8,128)(2,1)}, u32[]{:S(2)}, u32[]{:S(2)}) collective-permute-start(bf16[512,512]{1,0:T(8,128)(2,1)S(1)} %collective-permute-done.refs_1_), channel_id=1, source_target_pairs={{0,8},{8,64},{64,72},{72,0},{1,9},{9,65},{65,73},{73,1},{2,10},{10... | collective-permute-start | bytes 1572872 | tf_op jit(solution)/shard_map/ppermute | solution.py:139
  19.9 24.3 %collective-permute-start.7 = (bf16[512,512]{1,0:T(8,128)(2,1)S(1)}, bf16[512,512]{1,0:T(8,128)(2,1)}, u32[]{:S(2)}, u32[]{:S(2)}) collective-permute-start(bf16[512,512]{1,0:T(8,128)(2,1)S(1)} %collective-permute-done.1.refs_2_), channel_id=1, source_target_pairs={{0,72},{8,0},{64,8},{72,64},{1,73},{9,1},{65,9},{73,65},{2,74},{10... | collective-permute-start | bytes 1572872 | tf_op jit(solution)/shard_map/ppermute | solution.py:139
  22.3 22.5 %collective-permute-start.20 = (bf16[2,256,512]{2,1,0:T(8,128)(2,1)}, bf16[2,256,512]{2,1,0:T(8,128)(2,1)S(1)}, u32[]{:S(2)}, u32[]{:S(2)}) collective-permute-start(bf16[2,256,512]{2,1,0:T(8,128)(2,1)} %get-tuple-element.39), channel_id=1, source_target_pairs={{0,16},{16,0},{1,17},{17,1},{2,18},{18,2},{3,19},{19,3},{4,20},{20... | collective-permute-start | bytes 1572872 | tf_op jit(solution)/shard_map/ppermute | solution.py:155
  25.3 7.5 %collective-permute-start.3 = (bf16[256,512]{1,0:T(8,128)(2,1)S(1)}, bf16[256,512]{1,0:T(8,128)(2,1)S(1)}, u32[]{:S(2)}, u32[]{:S(2)}) collective-permute-start(bf16[256,512]{1,0:T(8,128)(2,1)S(1)} %slice.37), channel_id=1, source_target_pairs={{0,6},{2,0},{4,2},{6,4},{1,7},{3,1},{5,3},{7,5},{8,14},{10,8},{12,... | collective-permute-start | bytes 786440 | tf_op jit(solution)/shard_map/ppermute | solution.py:161
  27.0 17.3 %all-to-all-start = ((s32[4,3,24]{2,1,0:T(4,128)}), s32[4,3,24]{2,1,0:T(4,128)S(1)}, u32[]{:S(2)}, u32[]{:S(2)}) async-start(s32[4,3,24]{2,1,0:T(4,128)} %broadcast_in_dim.45), calls=%async_computation | async-start | bytes 16384 | tf_op jit(solution)/shard_map/all_to_all | solution.py:166
  32.8 12.3 %collective-permute-start.8 = (bf16[256,512]{1,0:T(8,128)(2,1)}, bf16[256,512]{1,0:T(8,128)(2,1)}, u32[]{:S(2)}, u32[]{:S(2)}) collective-permute-start(bf16[256,512]{1,0:T(8,128)(2,1)} %collective-permute-done.2.refs_3_), channel_id=1, source_target_pairs={{0,8},{8,64},{64,72},{72,0},{1,9},{9,65},{65,73},{73,1},{2,10},{10... | collective-permute-start | bytes 786440 | tf_op jit(solution)/shard_map/ppermute | solution.py:139
  32.8 12.8 %collective-permute-start.9 = (bf16[256,512]{1,0:T(8,128)(2,1)S(1)}, bf16[256,512]{1,0:T(8,128)(2,1)}, u32[]{:S(2)}, u32[]{:S(2)}) collective-permute-start(bf16[256,512]{1,0:T(8,128)(2,1)S(1)} %collective-permute-done.3.refs_4_), channel_id=1, source_target_pairs={{0,72},{8,0},{64,8},{72,64},{1,73},{9,1},{65,9},{73,65},{2,74},{10... | collective-permute-start | bytes 786440 | tf_op jit(solution)/shard_map/ppermute | solution.py:139
  45.1 4.1 %collective-permute-start.10 = (bf16[512,512]{1,0:T(8,128)(2,1)S(1)}, bf16[512,512]{1,0:T(8,128)(2,1)S(1)}, u32[]{:S(2)}, u32[]{:S(2)}) collective-permute-start(bf16[512,512]{1,0:T(8,128)(2,1)S(1)} %bitcast.28), channel_id=1, source_target_pairs={{0,1},{1,0},{2,3},{3,2},{4,5},{5,4},{6,7},{7,6},{8,9},{9,8},{10,11... | collective-permute-start | bytes 1572872 | tf_op jit(solution)/shard_map/ppermute | solution.py:143
  45.7 2.5 %collective-permute-start.16 = (bf16[256,512]{1,0:T(8,128)(2,1)}, bf16[256,512]{1,0:T(8,128)(2,1)S(1)}, u32[]{:S(2)}, u32[]{:S(2)}) collective-permute-start(bf16[256,512]{1,0:T(8,128)(2,1)} %collective-permute-done.5.refs_6_), channel_id=1, source_target_pairs={{0,1},{1,0},{2,3},{3,2},{4,5},{5,4},{6,7},{7,6},{8,9},{9,8},{10,11... | collective-permute-start | bytes 786440 | tf_op jit(solution)/shard_map/ppermute | solution.py:143
  47.9 8.9 %collective-permute-start.23 = (bf16[2,512,512]{2,1,0:T(8,128)(2,1)}, bf16[2,512,512]{2,1,0:T(8,128)(2,1)S(1)}, u32[]{:S(2)}, u32[]{:S(2)}) collective-permute-start(bf16[2,512,512]{2,1,0:T(8,128)(2,1)} %refs_22_.1), channel_id=1, source_target_pairs={{0,1},{1,0},{2,3},{3,2},{4,5},{5,4},{6,7},{7,6},{8,9},{9,8},{10,11... | collective-permute-start | bytes 3145736 | tf_op jit(solution)/shard_map/ppermute | solution.py:143
  48.3 3.9 %collective-permute-start.11 = (bf16[512,512]{1,0:T(8,128)(2,1)S(1)}, bf16[512,512]{1,0:T(8,128)(2,1)}, u32[]{:S(2)}, u32[]{:S(2)}) collective-permute-start(bf16[512,512]{1,0:T(8,128)(2,1)S(1)} %collective-permute-done.refs_1_), channel_id=1, source_target_pairs={{0,1},{1,0},{2,3},{3,2},{4,5},{5,4},{6,7},{7,6},{8,9},{9,8},{10,11... | collective-permute-start | bytes 1572872 | tf_op jit(solution)/shard_map/ppermute | solution.py:143
  48.5 5.2 %collective-permute-start.12 = (bf16[512,512]{1,0:T(8,128)(2,1)S(1)}, bf16[512,512]{1,0:T(8,128)(2,1)}, u32[]{:S(2)}, u32[]{:S(2)}) collective-permute-start(bf16[512,512]{1,0:T(8,128)(2,1)S(1)} %collective-permute-done.1.refs_2_), channel_id=1, source_target_pairs={{0,1},{1,0},{2,3},{3,2},{4,5},{5,4},{6,7},{7,6},{8,9},{9,8},{10,11... | collective-permute-start | bytes 1572872 | tf_op jit(solution)/shard_map/ppermute | solution.py:143
  48.9 5.2 %collective-permute-start.17 = (bf16[512,512]{1,0:T(8,128)(2,1)}, bf16[512,512]{1,0:T(8,128)(2,1)}, u32[]{:S(2)}, u32[]{:S(2)}) collective-permute-start(bf16[512,512]{1,0:T(8,128)(2,1)} %collective-permute-done.6.refs_7_), channel_id=1, source_target_pairs={{0,1},{1,0},{2,3},{3,2},{4,5},{5,4},{6,7},{7,6},{8,9},{9,8},{10,11... | collective-permute-start | bytes 1572872 | tf_op jit(solution)/shard_map/ppermute | solution.py:143
  50.0 6.8 %collective-permute-start.25 = (bf16[2,512,512]{2,1,0:T(8,128)(2,1)}, bf16[2,512,512]{2,1,0:T(8,128)(2,1)}, u32[]{:S(2)}, u32[]{:S(2)}) collective-permute-start(bf16[2,512,512]{2,1,0:T(8,128)(2,1)} %collective-permute-done.19.refs_26_), channel_id=1, source_target_pairs={{0,1},{1,0},{2,3},{3,2},{4,5},{5,4},{6,7},{7,6},{8,9},{9,8},{10,11... | collective-permute-start | bytes 3145736 | tf_op jit(solution)/shard_map/ppermute | solution.py:143
  52.2 3.2 %collective-permute-start.18 = (bf16[512,512]{1,0:T(8,128)(2,1)}, bf16[512,512]{1,0:T(8,128)(2,1)S(1)}, u32[]{:S(2)}, u32[]{:S(2)}) collective-permute-start(bf16[512,512]{1,0:T(8,128)(2,1)} %collective-permute-done.7.refs_8_), channel_id=1, source_target_pairs={{0,1},{1,0},{2,3},{3,2},{4,5},{5,4},{6,7},{7,6},{8,9},{9,8},{10,11... | collective-permute-start | bytes 1572872 | tf_op jit(solution)/shard_map/ppermute | solution.py:143
  53.7 2.8 %collective-permute-start.24 = (bf16[2,256,512]{2,1,0:T(8,128)(2,1)S(1)}, bf16[2,256,512]{2,1,0:T(8,128)(2,1)S(1)}, u32[]{:S(2)}, u32[]{:S(2)}) collective-permute-start(bf16[2,256,512]{2,1,0:T(8,128)(2,1)S(1)} %get-tuple-element.34.refs_23_), channel_id=1, source_target_pairs={{0,1},{1,0},{2,3},{3,2},{4,5},{5,4},{6,7},{7,6},{8,9},{9,8},{10,11... | collective-permute-start | bytes 1572872 | tf_op jit(solution)/shard_map/ppermute | solution.py:143
  54.1 2.7 %collective-permute-start.26 = (bf16[2,256,512]{2,1,0:T(8,128)(2,1)}, bf16[2,256,512]{2,1,0:T(8,128)(2,1)S(1)}, u32[]{:S(2)}, u32[]{:S(2)}) collective-permute-start(bf16[2,256,512]{2,1,0:T(8,128)(2,1)} %copy-done.5), channel_id=1, source_target_pairs={{0,1},{1,0},{2,3},{3,2},{4,5},{5,4},{6,7},{7,6},{8,9},{9,8},{10,11... | collective-permute-start | bytes 1572872 | tf_op jit(solution)/shard_map/ppermute | solution.py:143
  83.5 35.8 %all-to-all-start.1 = ((bf16[32,2,32,512]{3,2,1,0:T(8,128)(2,1)}), bf16[32,2,32,512]{3,2,1,0:T(8,128)(2,1)S(1)}, u32[]{:S(2)}, u32[]{:S(2)}) async-start(bf16[32,2,32,512]{3,2,1,0:T(8,128)(2,1)} %bitcast.23), calls=%async_computation.1 | async-start | bytes 4194304 | tf_op jit(solution)/shard_map/all_to_all | solution.py:219
  (27 other events, 235.3 us)

commit v5 on v4

v5 whole, which is shorter than its diff:
```python
import jax
import jax.numpy as jnp
from jax import lax
from jax.experimental import pallas as pl
from jax.experimental.pallas import tpu as pltpu
from jax.sharding import Mesh, PartitionSpec as P

AXES = ("x_hi", "y_hi", "y_lo", "x_lo", "z", "core")
SIZES = (2, 2, 2, 2, 4, 2)
SECTOR = ("x_lo", "z", "core")
REDUCE = ("x_hi", "y_hi", "x_lo", "z")
SPREAD = ("x_hi", "y_hi", "y_lo", "core")
RING = 4
GROUP = 4
LEVELS = 4
GRAIN = 128
SLICE = GRAIN // GROUP
STEP = 8
KINDS = 4
MIB = 1024 * 1024
SWAP = [(0, 1), (1, 0)]
UP = [(i, (i + 1) % RING) for i in range(RING)]
DOWN = [(i, (i - 1) % RING) for i in range(RING)]
SHIFTS = (0, RING - 1, 1, 2)


def plan_couplings(source, target, op, dims, half):
    sectors = dims.shape[0]
    count = source.shape[0]
    steps = (count + KINDS * (STEP - 1)) // STEP
    index = jnp.arange(sectors, dtype=jnp.int32)[None, :]
    wide = (dims > half).astype(jnp.int32)[None, :]
    wide_source = jnp.sum(jnp.where(source[:, None] == index, wide, 0), axis=1)
    wide_target = jnp.sum(jnp.where(target[:, None] == index, wide, 0), axis=1)
    kind = 2 * wide_source + wide_target
    kinds = jnp.arange(KINDS, dtype=jnp.int32)
    is_kind = kind[:, None] == kinds[None, :]
    taken = (jnp.sum(is_kind.astype(jnp.int32), axis=0) + STEP - 1) // STEP
    end = jnp.sum(jnp.where(kinds[:, None] <= kinds[None, :], taken[:, None], 0), axis=0)
    start = end - taken
    spot = jnp.arange(count, dtype=jnp.int32)
    earlier = (kind[:, None] == kind[None, :]) & (spot[:, None] < spot[None, :])
    rank = jnp.sum(earlier.astype(jnp.int32), axis=0)
    place = rank + STEP * jnp.sum(jnp.where(is_kind, start[None, :], 0), axis=1)
    here = place[:, None] == jnp.arange(steps * STEP, dtype=jnp.int32)[None, :]
    code = (op * sectors + source) * (2 * sectors) + target - sectors
    return sectors + jnp.sum(jnp.where(here, code[:, None], 0), axis=0), end


def couplings_kernel(table, ends, dims, *refs):
    own_waves, mate_waves = refs[:11], refs[11:22]
    own_right, own_left, mate_right, mate_left, far_right, far_left, far_mate_right, far_mate_left = refs[22:30]
    out, left, right, waves, halves, sums, rounded, op_sems, wave_sems, out_sems = refs[30:]
    y, x, z, core = (lax.axis_index(name) for name in ("y_lo", "x_lo", "z", "core"))
    sectors, width, _ = waves.shape
    rows = sums.shape[1]
    ops = own_right.shape[0]
    half = width // 2
    left_copies, right_copies = [], []
    for n, (pair, c, left_rows, right_ops) in enumerate((
        (y, core, own_left, own_right),
        (y, 1 - core, mate_left, mate_right),
        (1 - y, core, far_left, far_right),
        (1 - y, 1 - core, far_mate_left, far_mate_right),
    )):
        first = (pair * 2 + c) * ops
        size = ops * rows
        to = left.at[pl.ds(pl.multiple_of(first * rows, size), size)]
        left_copies.append(pltpu.make_async_copy(left_rows.at[core], to, op_sems.at[2 * n]))
        right_copies.append(
            pltpu.make_async_copy(right_ops, right.at[pl.ds(first, ops)], op_sems.at[2 * n + 1])
        )
    for copy in left_copies:
        copy.start()
    whole, low, high = (pl.ds(0, width), pl.ds(0, half), pl.ds(half, half))
    places = (
        (0, whole), (1, whole), (2, whole), (3, low), (3, high),
        (4, low), (4, high), (5, whole), (6, whole), (7, low), (7, high),
    )
    for c, pieces in ((0, own_waves), (1, mate_waves)):
        for piece, (place, part) in zip(pieces, places):
            slot = c * (sectors // 2) + place
            pltpu.make_async_copy(piece, waves.at[slot, part], wave_sems.at[slot]).start()
    for copy in right_copies:
        copy.start()
    sums[...] = jnp.zeros_like(sums)
    for copy in left_copies:
        copy.wait()

    def first_half(slot, carry):
        pltpu.make_async_copy(waves.at[slot], waves.at[slot], wave_sems.at[slot]).wait()
        other_core = lax.div(slot, sectors // 2)
        other_x = lax.rem(lax.div(slot, RING), 2)
        step = lax.rem(slot, RING)
        shift = jnp.where(step == 1, RING - 1, jnp.where(step == 2, 1, jnp.where(step == 3, 2, 0)))
        x_at = lax.rem(x + other_x, 2)
        core_at = lax.rem(core + other_core, 2)
        s = (x_at * RING + lax.rem(z + shift, RING)) * 2 + core_at
        level = dims[s] // GRAIN
        for sl in range(1, LEVELS + 1):

            @pl.when(level == sl)
            def _(sl=sl):
                inner = sl * GRAIN
                halves[s, :, :inner] = jnp.dot(
                    left[:, :inner], waves[slot, :inner, :inner], preferred_element_type=jnp.float32
                ).astype(jnp.bfloat16)
                if sl % 2:
                    halves[s, :, inner:inner + GRAIN] = jnp.zeros((left.shape[0], GRAIN), jnp.bfloat16)

        return carry

    lax.fori_loop(0, sectors, first_half, 0)
    for copy in right_copies:
        copy.wait()

    for kind in range(KINDS):
        inner = width if kind >= 2 else half
        cols = width if kind % 2 else half
        used = rows if kind % 2 else rows // 2

        def second_half(i, carry, inner=inner, cols=cols, used=used):
            for u in range(STEP):
                code = table[i * STEP + u]
                target = jnp.bitwise_and(code, 2 * sectors - 1)
                source = jnp.bitwise_and(lax.shift_right_logical(code, 5), sectors - 1)
                op = lax.shift_right_logical(code, 9)
                block = halves[source, pl.ds(pl.multiple_of(op * rows, rows), used), :inner]
                sums[target, :used, :cols] += jnp.dot(
                    block, right[op, :inner, :cols], preferred_element_type=jnp.float32
                )
            return carry

        lax.fori_loop(0 if kind == 0 else ends[kind - 1], ends[kind], second_half, 0)
    parts = out.shape[0]
    size = rows // parts
    column = lax.broadcasted_iota(jnp.int32, (size, width), 1)
    copies = []
    for part in range(parts):

        def finish(s, carry, part=part):
            limit = jnp.where(dims[s] > part * GRAIN, dims[s], 0)
            total = jnp.where(column < limit, sums[s, part * size:(part + 1) * size, :], 0.0)
            rounded[part, s] = total.astype(jnp.bfloat16)
            return carry

        lax.fori_loop(0, sectors, finish, 0)
        copy = pltpu.make_async_copy(rounded.at[part], out.at[part], out_sems.at[part])
        copy.start()
        copies.append(copy)
    for copy in copies:
        copy.wait()


def along_x(part, steps):
    return lax.ppermute(part, ("x_hi", "x_lo"), steps)


def to_mate(part):
    return lax.ppermute(part, "core", SWAP)


def share(block, left_ops, right_ops, meta):
    ops, width, _ = left_ops.shape
    half = width // 2
    rows = left_ops.reshape(ops, LEVELS, 2, 2, SLICE, width).transpose(2, 3, 0, 1, 4, 5)
    rows = rows.reshape(2, 2, ops * LEVELS * SLICE, width)
    y = lax.axis_index("y_lo")
    near_rows = lax.dynamic_index_in_dim(rows, y, 0, keepdims=False)
    sent_rows = lax.dynamic_index_in_dim(rows, 1 - y, 0, keepdims=False)
    far_right = lax.ppermute(right_ops, "y_lo", SWAP)
    far_rows = lax.ppermute(sent_rows, "y_lo", SWAP)
    before = lax.ppermute(block, "z", UP)
    after = lax.ppermute(block, "z", DOWN)
    side_low = along_x(block[:half], UP)
    side_high = along_x(block[half:], DOWN)
    across_low = lax.ppermute(before[:half], "z", UP)
    across_high = lax.ppermute(after[half:], "z", DOWN)
    side_before = along_x(before, UP)
    side_after = along_x(after, DOWN)
    corner_low = along_x(across_low, UP)
    corner_high = along_x(across_high, DOWN)
    metas = jnp.stack([meta, lax.ppermute(meta, "y_lo", SWAP)])
    metas = jnp.concatenate([metas, to_mate(metas)])
    early = (
        block, before, after, across_low, across_high, side_low, side_high, side_before, side_after,
    )
    own_waves = early + (corner_low, corner_high)
    held = lax.optimization_barrier(early + (right_ops, near_rows))
    mate_early = [to_mate(part) for part in held]
    mate_late = [to_mate(part) for part in (corner_low, corner_high, far_right, far_rows)]
    mate_waves = tuple(mate_early[:9] + mate_late[:2])
    operators = (right_ops, near_rows, mate_early[9], mate_early[10], far_right, far_rows, mate_late[2], mate_late[3])
    return own_waves + mate_waves + operators, metas


def body(
    wavefunction,
    left_ops,
    right_ops,
    sector_dims,
    coupling_source,
    coupling_target,
    coupling_operator,
):
    ops, width, _ = left_ops.shape
    sectors = 4 * RING
    meta = jnp.stack([coupling_source, coupling_target, coupling_operator])
    shared, metas = share(wavefunction[0], left_ops, right_ops, meta)
    y, core = lax.axis_index("y_lo"), lax.axis_index("core")
    owners = jnp.stack([2 * y + core, 2 * (1 - y) + core, 2 * y + 1 - core, 2 * (1 - y) + 1 - core])
    chosen = metas[:, 2] + ops * owners.astype(jnp.int32)[:, None]
    table, ends = plan_couplings(
        metas[:, 0].reshape(-1), metas[:, 1].reshape(-1), chosen.reshape(-1), sector_dims, width // 2
    )
    smem = pl.BlockSpec(memory_space=pltpu.SMEM)
    hbm = pl.BlockSpec(memory_space=pltpu.HBM)
    rows = width // GROUP
    partial = pl.pallas_call(
        couplings_kernel,
        out_shape=jax.ShapeDtypeStruct((LEVELS, sectors, SLICE, width), jnp.bfloat16),
        in_specs=[smem] * 3 + [hbm] * len(shared),
        out_specs=hbm,
        scratch_shapes=[
            pltpu.VMEM((ops * width, width), jnp.bfloat16),
            pltpu.VMEM((ops * GROUP, width, width), jnp.bfloat16),
            pltpu.VMEM((sectors, width, width), jnp.bfloat16),
            pltpu.VMEM((sectors, ops * width, width), jnp.bfloat16),
            pltpu.VMEM((sectors + 1, rows, width), jnp.float32),
            pltpu.VMEM((LEVELS, sectors, SLICE, width), jnp.bfloat16),
            pltpu.SemaphoreType.DMA((8,)),
            pltpu.SemaphoreType.DMA((sectors,)),
            pltpu.SemaphoreType.DMA((LEVELS,)),
        ],
        compiler_params=pltpu.CompilerParams(vmem_limit_bytes=56 * MIB),
        name="couplings",
    )(table, ends, sector_dims, *shared)
    got = lax.all_to_all(partial.reshape(-1, 2, SLICE, width), REDUCE, 0, 0, tiled=True)
    total = jnp.sum(got.astype(jnp.float32), axis=0).astype(jnp.bfloat16)
    spread = jnp.broadcast_to(total[None], (8,) + total.shape).reshape((16,) + total.shape[1:])
    whole = lax.all_to_all(spread, SPREAD, 0, 0, tiled=True)
    return whole.reshape(1, width, width).astype(jnp.float32)


def solution(mesh):
    fine = Mesh(mesh.devices.reshape(SIZES), AXES)
    everyone = P(AXES)
    placed = (
        P(SECTOR, None, None),
        P(AXES, None, None),
        P(AXES, None, None),
        P(),
        everyone,
        everyone,
        everyone,
    )
    return jax.shard_map(
        body, mesh=fine, in_specs=placed, out_specs=P(SECTOR, None, None), check_vma=False
    )
```

time: 139 us -> 139 us (level)
  blocking collectives: 18.2 us -> 53 us
  waiting for transfers between devices: 48.6 us -> 17.9 us
  Pallas kernels: 25.6 us -> 21.4 us
    all_to_all x2 -> x0, waiting for transfers between devices: 36.2 us -> none  [the longest x1 27.6 us: body(): lax.all_to_all(partial.reshape(-1, 2, SLICE, width), REDUCE, 0, 0, tiled=...]
    all_to_all x0 -> x1, blocking collectives: none -> 34.9 us  [body(): lax.all_to_all(partial.reshape(-1, 2, SLICE, width), REDUCE, 0, 0, tiled=...]
    all_to_all x2 -> x0, starting transfers between devices: 13.8 us -> none  [the longest x1 7.96 us: body(): lax.all_to_all(partial.reshape(-1, 2, SLICE, width), REDUCE, 0, 0, tiled=...]
    ppermute x15 -> x16, starting transfers between devices: 4.5 us -> 16.9 us  [to_mate(): return lax.ppermute(part, 'core', SWAP)]
    ppermute x1, waiting for transfers between devices: 6.1 us -> 0.01 us  [share(): before = lax.ppermute(block, 'z', UP)]
    ppermute x6, waiting for transfers between devices: 0.02 us -> 5.3 us  [along_x(): return lax.ppermute(part, ('x_hi', 'x_lo'), steps)]
    pallas_call x1, Pallas kernels: 25.6 us -> 21.4 us  [body(): pl.pallas_call(couplings_kernel, out_shape=jax.ShapeDtypeStruct((LEVELS,...]
    ppermute x1, starting transfers between devices: 2.47 us -> 0.01 us  [share(): before = lax.ppermute(block, 'z', UP)]
  transfers between devices with their start and end apart: 29 -> 29, of which waited for: 9 -> 14; matrix products, arithmetic and copies ran while one was open for 6% -> 6% of each run, Pallas kernels for 0% -> 0%
where the time goes in v5:
time: 139 us
  blocking collectives  53 us (38%)
  starting transfers between devices  36 us (26%)
  Pallas kernels  21.4 us (15%)
  waiting for transfers between devices  17.9 us (13%)
  local copies, waits for them, and re-layouts  6.8 us (5%)
  other arithmetic  3.47 us (2%)
    all_to_all x1, blocking collectives, body(): lax.all_to_all(partial.reshape(-1, 2, SLICE, width), REDUCE, 0, 0, tiled=...  34.9 us
    pallas_call x1, Pallas kernels, body(): pl.pallas_call(couplings_kernel, out_shape=jax.ShapeDtypeStruct((LEVELS,...  21.4 us
    all_to_all x1, blocking collectives, body(): whole = lax.all_to_all(spread, SPREAD, 0, 0, tiled=True)  18.1 us
    ppermute x16, starting transfers between devices, to_mate(): return lax.ppermute(part, 'core', SWAP)  16.9 us
    ppermute x6, starting transfers between devices, along_x(): return lax.ppermute(part, ('x_hi', 'x_lo'), steps)  8.37 us
    ppermute x16, waiting for transfers between devices, to_mate(): return lax.ppermute(part, 'core', SWAP)  6.19 us
    ppermute x6, waiting for transfers between devices, along_x(): return lax.ppermute(part, ('x_hi', 'x_lo'), steps)  5.3 us
    ppermute x1, starting transfers between devices, share(): after = lax.ppermute(block, 'z', DOWN)  4.59 us
  transfers between devices with their start and end apart: 29, of which 14 were waited for; matrix products, arithmetic and copies ran while one was open for 6% of the time, Pallas kernels for 0%

profile of v5, /device:TPU:1, one launch (start us, length us, event | category | flops | bytes accessed | tf_op | source)
XLA Modules:
  0.0 138.8 jit_solution(16339616313519197619)
XLA Ops:
  0.0 4.6 %collective-permute-start.3 = (bf16[512,512]{1,0:T(8,128)(2,1)}, bf16[512,512]{1,0:T(8,128)(2,1)S(1)}, u32[]{:S(2)}, u32[]{:S(2)}) collective-permute-start(bf16[512,512]{1,0:T(8,128)(2,1)} %bitcast.31), channel_id=1, source_target_pairs={{0,6},{2,0},{4,2},{6,4},{1,7},{3,1},{5,3},{7,5},{8,14},{10,8},{12,... | collective-permute-start | bytes 1572872 | tf_op jit(solution)/shard_map/ppermute | solution.py:174
  5.3 1.4 collective-permute-start
  6.6 1.9 %slice_bitcast_fusion = (bf16[256,512]{1,0:T(8,128)(2,1)}, bf16[256,512]{1,0:T(8,128)(2,1)}) fusion(bf16[1,512,512]{2,1,0:T(8,128)(2,1)} %param.7), kind=kLoop, calls=%fused_computation.3 | loop fusion | bytes 1048576 | tf_op jit(solution)/shard_map/slice | solution.py:176
  8.5 2.5 %collective-permute-start.7 = (bf16[256,512]{1,0:T(8,128)(2,1)}, bf16[256,512]{1,0:T(8,128)(2,1)S(1)}, u32[]{:S(2)}, u32[]{:S(2)}) collective-permute-start(bf16[256,512]{1,0:T(8,128)(2,1)} %get-tuple-element.34), channel_id=1, source_target_pairs={{0,72},{8,0},{64,8},{72,64},{1,73},{9,1},{65,9},{73,65},{2,74},{10... | collective-permute-start | bytes 786440 | tf_op jit(solution)/shard_map/ppermute | solution.py:156
  11.0 1.3 copy.9
  12.3 1.6 %collective-permute-start.1 = (s32[2,3,24]{2,1,0:T(4,128)S(1)}, s32[2,3,24]{2,1,0:T(4,128)S(1)}, u32[]{:S(2)}, u32[]{:S(2)}) collective-permute-start(s32[2,3,24]{2,1,0:T(4,128)S(1)} %pad_add_fusion), channel_id=1, source_target_pairs={{0,1},{1,0},{2,3},{3,2},{4,5},{5,4},{6,7},{7,6},{8,9},{9,8},{10,11... | collective-permute-start | bytes 1736 | tf_op jit(solution)/shard_map/ppermute | solution.py:160
  15.5 1.3 collective-permute-start.25
  17.5 3.3 %collective-permute-start.5 = (bf16[256,512]{1,0:T(8,128)(2,1)}, bf16[256,512]{1,0:T(8,128)(2,1)}, u32[]{:S(2)}, u32[]{:S(2)}) collective-permute-start(bf16[256,512]{1,0:T(8,128)(2,1)} %slice.37), channel_id=1, source_target_pairs={{0,6},{2,0},{4,2},{6,4},{1,7},{3,1},{5,3},{7,5},{8,14},{10,8},{12,... | collective-permute-start | bytes 786440 | tf_op jit(solution)/shard_map/ppermute | solution.py:178
  20.8 2.5 %collective-permute-start.9 = (bf16[512,512]{1,0:T(8,128)(2,1)S(1)}, bf16[512,512]{1,0:T(8,128)(2,1)}, u32[]{:S(2)}, u32[]{:S(2)}) collective-permute-start(bf16[512,512]{1,0:T(8,128)(2,1)S(1)} %collective-permute-done.3.refs_2_), channel_id=1, source_target_pairs={{0,72},{8,0},{64,8},{72,64},{1,73},{9,1},{65,9},{73,65},{2,74},{10... | collective-permute-start | bytes 1572872 | tf_op jit(solution)/shard_map/ppermute | solution.py:156
  24.9 2.5 %collective-permute-start.11 = (bf16[256,512]{1,0:T(8,128)(2,1)}, bf16[256,512]{1,0:T(8,128)(2,1)}, u32[]{:S(2)}, u32[]{:S(2)}) collective-permute-start(bf16[256,512]{1,0:T(8,128)(2,1)} %collective-permute-done.5.refs_4_), channel_id=1, source_target_pairs={{0,72},{8,0},{64,8},{72,64},{1,73},{9,1},{65,9},{73,65},{2,74},{10... | collective-permute-start | bytes 786440 | tf_op jit(solution)/shard_map/ppermute | solution.py:156
  28.7 3.0 %collective-permute-done.4.refs_3_ = bf16[256,512]{1,0:T(8,128)(2,1)} collective-permute-done((bf16[256,512]{1,0:T(8,128)(2,1)}, bf16[256,512]{1,0:T(8,128)(2,1)}, u32[]{:S(2)}, u32[]{:S(2)}) %collective-permute-start.4) | collective-permute-done | bytes 262176 | tf_op jit(solution)/shard_map/ppermute | solution.py:177
  31.7 3.0 %collective-permute-start.28 = (bf16[2,256,512]{2,1,0:T(8,128)(2,1)}, bf16[2,256,512]{2,1,0:T(8,128)(2,1)}, u32[]{:S(2)}, u32[]{:S(2)}) collective-permute-start(bf16[2,256,512]{2,1,0:T(8,128)(2,1)} %collective-permute-done.26.refs_27_), channel_id=1, source_target_pairs={{0,1},{1,0},{2,3},{3,2},{4,5},{5,4},{6,7},{7,6},{8,9},{9,8},{10,11... | collective-permute-start | bytes 1572872 | tf_op jit(solution)/shard_map/ppermute | solution.py:160
  34.8 3.3 %collective-permute-done.11.refs_10_ = bf16[256,512]{1,0:T(8,128)(2,1)} collective-permute-done((bf16[256,512]{1,0:T(8,128)(2,1)}, bf16[256,512]{1,0:T(8,128)(2,1)}, u32[]{:S(2)}, u32[]{:S(2)}) %collective-permute-start.11) | collective-permute-done | bytes 262176 | tf_op jit(solution)/shard_map/ppermute | solution.py:156
  39.1 3.3 %collective-permute-start.22 = (bf16[256,512]{1,0:T(8,128)(2,1)}, bf16[256,512]{1,0:T(8,128)(2,1)S(1)}, u32[]{:S(2)}, u32[]{:S(2)}) collective-permute-start(bf16[256,512]{1,0:T(8,128)(2,1)} %collective-permute-done.11.refs_10_), channel_id=1, source_target_pairs={{0,1},{1,0},{2,3},{3,2},{4,5},{5,4},{6,7},{7,6},{8,9},{9,8},{10,11... | collective-permute-start | bytes 786440 | tf_op jit(solution)/shard_map/ppermute | solution.py:160
  42.5 2.6 %collective-permute-start.15 = (bf16[256,512]{1,0:T(8,128)(2,1)}, bf16[256,512]{1,0:T(8,128)(2,1)S(1)}, u32[]{:S(2)}, u32[]{:S(2)}) collective-permute-start(bf16[256,512]{1,0:T(8,128)(2,1)} %collective-permute-done.4.refs_3_), channel_id=1, source_target_pairs={{0,1},{1,0},{2,3},{3,2},{4,5},{5,4},{6,7},{7,6},{8,9},{9,8},{10,11... | collective-permute-start | bytes 786440 | tf_op jit(solution)/shard_map/ppermute | solution.py:160
  45.1 1.9 %collective-permute-done.10.refs_9_ = bf16[256,512]{1,0:T(8,128)(2,1)S(1)} collective-permute-done((bf16[256,512]{1,0:T(8,128)(2,1)}, bf16[256,512]{1,0:T(8,128)(2,1)S(1)}, u32[]{:S(2)}, u32[]{:S(2)}) %collective-permute-start.10) | collective-permute-done | bytes 262176 | tf_op jit(solution)/shard_map/ppermute | solution.py:156
  47.0 2.9 %collective-permute-start.16 = (bf16[256,512]{1,0:T(8,128)(2,1)}, bf16[256,512]{1,0:T(8,128)(2,1)S(1)}, u32[]{:S(2)}, u32[]{:S(2)}) collective-permute-start(bf16[256,512]{1,0:T(8,128)(2,1)} %collective-permute-done.5.refs_4_), channel_id=1, source_target_pairs={{0,1},{1,0},{2,3},{3,2},{4,5},{5,4},{6,7},{7,6},{8,9},{9,8},{10,11... | collective-permute-start | bytes 786440 | tf_op jit(solution)/shard_map/ppermute | solution.py:160
  49.9 1.1 collective-permute-done.25.refs_26_
  52.1 1.3 collective-permute-done.21.refs_20_
  57.3 1.9 %collective-permute-done.14.refs_13_ = bf16[512,512]{1,0:T(8,128)(2,1)} collective-permute-done((bf16[512,512]{1,0:T(8,128)(2,1)S(1)}, bf16[512,512]{1,0:T(8,128)(2,1)}, u32[]{:S(2)}, u32[]{:S(2)}) %collective-permute-start.14) | collective-permute-done | bytes 524320 | tf_op jit(solution)/shard_map/ppermute | solution.py:160
  60.3 1.2 collective-permute-done.20.refs_19_
  62.9 21.4 %couplings.1 = bf16[4,16,32,512]{3,2,1,0:T(8,128)(2,1)} custom-call(s32[120]{0:T(128)} %broadcast_add_fusion.table, s32[4]{0:T(128)} %copy-done.17, s32[16]{0:T(128)} %dims.1, bf16[512,512]{1,0:T(8,128)(2,1)} %bitcast.33, bf16[512,512]{1,0:T(8,128)(2,1)} %copy-done.3, bf16[512,512]{1,0:T(8,128)(2,1)} %copy-done.2, ...), custom_call_target="tpu_custom_call" | custom-call | tf_op jit(solution)/shard_map/couplings/pallas_call | solution.py:219
  84.3 34.9 %all_to_all.10 = bf16[32,2,32,512]{3,2,1,0:T(8,128)(2,1)S(1)} all-to-all(bf16[32,2,32,512]{3,2,1,0:T(8,128)(2,1)} %bitcast.29), channel_id=1, replica_groups=mesh['x_hi'=2,'y_hi'=2,'y_lo'=2,'x_lo'=2,'z'=4,'core'=2] {'x_hi','y_hi',..., dimensions={0} | all-to-all | bytes 4194304 | tf_op jit(solution)/shard_map/all_to_all | solution.py:238
  119.5 18.1 %all_to_all.11 = bf16[16,32,512]{2,1,0:T(8,128)(2,1)S(1)} all-to-all(bf16[16,32,512]{2,1,0:T(8,128)(2,1)S(1)} %bitcast.36), channel_id=1, replica_groups=mesh['x_hi'=2,'y_hi'=2,'y_lo'=2,'x_lo'=2,'z'=4,'core'=2] {'x_hi','y_hi',..., dimensions={0} | all-to-all | bytes 1048576 | tf_op jit(solution)/shard_map/all_to_all | solution.py:241
  (102 shorter events, 16.0 us)
Async XLA Ops:
  0.0 15.5 %collective-permute-start.3 = (bf16[512,512]{1,0:T(8,128)(2,1)}, bf16[512,512]{1,0:T(8,128)(2,1)S(1)}, u32[]{:S(2)}, u32[]{:S(2)}) collective-permute-start(bf16[512,512]{1,0:T(8,128)(2,1)} %bitcast.31), channel_id=1, source_target_pairs={{0,6},{2,0},{4,2},{6,4},{1,7},{3,1},{5,3},{7,5},{8,14},{10,8},{12,... | collective-permute-start | bytes 1572872 | tf_op jit(solution)/shard_map/ppermute | solution.py:174
  4.6 16.3 %collective-permute-start.2 = (bf16[512,512]{1,0:T(8,128)(2,1)}, bf16[512,512]{1,0:T(8,128)(2,1)S(1)}, u32[]{:S(2)}, u32[]{:S(2)}) collective-permute-start(bf16[512,512]{1,0:T(8,128)(2,1)} %bitcast.32), channel_id=1, source_target_pairs={{0,2},{2,4},{4,6},{6,0},{1,3},{3,5},{5,7},{7,1},{8,10},{10,12},{12... | collective-permute-start | bytes 1572872 | tf_op jit(solution)/shard_map/ppermute | solution.py:173
  5.3 7.0 %collective-permute-start = (s32[3,24]{1,0:T(4,128)S(1)}, s32[3,24]{1,0:T(4,128)S(1)}, u32[]{:S(2)}, u32[]{:S(2)}) collective-permute-start(s32[3,24]{1,0:T(4,128)S(1)} %get-tuple-element.37), channel_id=1, source_target_pairs={{0,16},{16,0},{1,17},{17,1},{2,18},{18,2},{3,19},{19,3},{4,20},{20... | collective-permute-start | bytes 872 | tf_op jit(solution)/shard_map/ppermute | solution.py:183
  8.5 9.0 %collective-permute-start.7 = (bf16[256,512]{1,0:T(8,128)(2,1)}, bf16[256,512]{1,0:T(8,128)(2,1)S(1)}, u32[]{:S(2)}, u32[]{:S(2)}) collective-permute-start(bf16[256,512]{1,0:T(8,128)(2,1)} %get-tuple-element.34), channel_id=1, source_target_pairs={{0,72},{8,0},{64,8},{72,64},{1,73},{9,1},{65,9},{73,65},{2,74},{10... | collective-permute-start | bytes 786440 | tf_op jit(solution)/shard_map/ppermute | solution.py:156
  14.8 13.8 %collective-permute-start.26 = (bf16[2,256,512]{2,1,0:T(8,128)(2,1)}, bf16[2,256,512]{2,1,0:T(8,128)(2,1)}, u32[]{:S(2)}, u32[]{:S(2)}) collective-permute-start(bf16[2,256,512]{2,1,0:T(8,128)(2,1)} %get-tuple-element.32), channel_id=1, source_target_pairs={{0,16},{16,0},{1,17},{17,1},{2,18},{18,2},{3,19},{19,3},{4,20},{20... | collective-permute-start | bytes 1572872 | tf_op jit(solution)/shard_map/ppermute | solution.py:172
  15.0 9.1 %collective-permute-start.6 = (bf16[256,512]{1,0:T(8,128)(2,1)}, bf16[256,512]{1,0:T(8,128)(2,1)}, u32[]{:S(2)}, u32[]{:S(2)}) collective-permute-start(bf16[256,512]{1,0:T(8,128)(2,1)} %get-tuple-element.35), channel_id=1, source_target_pairs={{0,8},{8,64},{64,72},{72,0},{1,9},{9,65},{65,73},{73,1},{2,10},{10... | collective-permute-start | bytes 786440 | tf_op jit(solution)/shard_map/ppermute | solution.py:156
  15.5 35.5 %collective-permute-start.25 = (bf16[2,512,512]{2,1,0:T(8,128)(2,1)}, bf16[2,512,512]{2,1,0:T(8,128)(2,1)S(1)}, u32[]{:S(2)}, u32[]{:S(2)}) collective-permute-start(bf16[2,512,512]{2,1,0:T(8,128)(2,1)} %refs_22_.1), channel_id=1, source_target_pairs={{0,16},{16,0},{1,17},{17,1},{2,18},{18,2},{3,19},{19,3},{4,20},{20... | collective-permute-start | bytes 3145736 | tf_op jit(solution)/shard_map/ppermute | solution.py:171
  17.5 7.4 %collective-permute-start.5 = (bf16[256,512]{1,0:T(8,128)(2,1)}, bf16[256,512]{1,0:T(8,128)(2,1)}, u32[]{:S(2)}, u32[]{:S(2)}) collective-permute-start(bf16[256,512]{1,0:T(8,128)(2,1)} %slice.37), channel_id=1, source_target_pairs={{0,6},{2,0},{4,2},{6,4},{1,7},{3,1},{5,3},{7,5},{8,14},{10,8},{12,... | collective-permute-start | bytes 786440 | tf_op jit(solution)/shard_map/ppermute | solution.py:178
  20.8 18.2 %collective-permute-start.9 = (bf16[512,512]{1,0:T(8,128)(2,1)S(1)}, bf16[512,512]{1,0:T(8,128)(2,1)}, u32[]{:S(2)}, u32[]{:S(2)}) collective-permute-start(bf16[512,512]{1,0:T(8,128)(2,1)S(1)} %collective-permute-done.3.refs_2_), channel_id=1, source_target_pairs={{0,72},{8,0},{64,8},{72,64},{1,73},{9,1},{65,9},{73,65},{2,74},{10... | collective-permute-start | bytes 1572872 | tf_op jit(solution)/shard_map/ppermute | solution.py:156
  24.1 7.6 %collective-permute-start.4 = (bf16[256,512]{1,0:T(8,128)(2,1)}, bf16[256,512]{1,0:T(8,128)(2,1)}, u32[]{:S(2)}, u32[]{:S(2)}) collective-permute-start(bf16[256,512]{1,0:T(8,128)(2,1)} %slice.36), channel_id=1, source_target_pairs={{0,2},{2,4},{4,6},{6,0},{1,3},{3,5},{5,7},{7,1},{8,10},{10,12},{12... | collective-permute-start | bytes 786440 | tf_op jit(solution)/shard_map/ppermute | solution.py:177
  24.9 13.2 %collective-permute-start.11 = (bf16[256,512]{1,0:T(8,128)(2,1)}, bf16[256,512]{1,0:T(8,128)(2,1)}, u32[]{:S(2)}, u32[]{:S(2)}) collective-permute-start(bf16[256,512]{1,0:T(8,128)(2,1)} %collective-permute-done.5.refs_4_), channel_id=1, source_target_pairs={{0,72},{8,0},{64,8},{72,64},{1,73},{9,1},{65,9},{73,65},{2,74},{10... | collective-permute-start | bytes 786440 | tf_op jit(solution)/shard_map/ppermute | solution.py:156
  28.7 13.8 %collective-permute-start.8 = (bf16[512,512]{1,0:T(8,128)(2,1)S(1)}, bf16[512,512]{1,0:T(8,128)(2,1)}, u32[]{:S(2)}, u32[]{:S(2)}) collective-permute-start(bf16[512,512]{1,0:T(8,128)(2,1)S(1)} %collective-permute-done.2.refs_1_), channel_id=1, source_target_pairs={{0,8},{8,64},{64,72},{72,0},{1,9},{9,65},{65,73},{73,1},{2,10},{10... | collective-permute-start | bytes 1572872 | tf_op jit(solution)/shard_map/ppermute | solution.py:156
  31.7 18.2 %collective-permute-start.28 = (bf16[2,256,512]{2,1,0:T(8,128)(2,1)}, bf16[2,256,512]{2,1,0:T(8,128)(2,1)}, u32[]{:S(2)}, u32[]{:S(2)}) collective-permute-start(bf16[2,256,512]{2,1,0:T(8,128)(2,1)} %collective-permute-done.26.refs_27_), channel_id=1, source_target_pairs={{0,1},{1,0},{2,3},{3,2},{4,5},{5,4},{6,7},{7,6},{8,9},{9,8},{10,11... | collective-permute-start | bytes 1572872 | tf_op jit(solution)/shard_map/ppermute | solution.py:160
  38.2 8.8 %collective-permute-start.10 = (bf16[256,512]{1,0:T(8,128)(2,1)}, bf16[256,512]{1,0:T(8,128)(2,1)S(1)}, u32[]{:S(2)}, u32[]{:S(2)}) collective-permute-start(bf16[256,512]{1,0:T(8,128)(2,1)} %collective-permute-done.4.refs_3_), channel_id=1, source_target_pairs={{0,8},{8,64},{64,72},{72,0},{1,9},{9,65},{65,73},{73,1},{2,10},{10... | collective-permute-start | bytes 786440 | tf_op jit(solution)/shard_map/ppermute | solution.py:156
  39.1 12.8 %collective-permute-start.22 = (bf16[256,512]{1,0:T(8,128)(2,1)}, bf16[256,512]{1,0:T(8,128)(2,1)S(1)}, u32[]{:S(2)}, u32[]{:S(2)}) collective-permute-start(bf16[256,512]{1,0:T(8,128)(2,1)} %collective-permute-done.11.refs_10_), channel_id=1, source_target_pairs={{0,1},{1,0},{2,3},{3,2},{4,5},{5,4},{6,7},{7,6},{8,9},{9,8},{10,11... | collective-permute-start | bytes 786440 | tf_op jit(solution)/shard_map/ppermute | solution.py:160
  42.5 11.3 %collective-permute-start.15 = (bf16[256,512]{1,0:T(8,128)(2,1)}, bf16[256,512]{1,0:T(8,128)(2,1)S(1)}, u32[]{:S(2)}, u32[]{:S(2)}) collective-permute-start(bf16[256,512]{1,0:T(8,128)(2,1)} %collective-permute-done.4.refs_3_), channel_id=1, source_target_pairs={{0,1},{1,0},{2,3},{3,2},{4,5},{5,4},{6,7},{7,6},{8,9},{9,8},{10,11... | collective-permute-start | bytes 786440 | tf_op jit(solution)/shard_map/ppermute | solution.py:160
  47.0 6.9 %collective-permute-start.16 = (bf16[256,512]{1,0:T(8,128)(2,1)}, bf16[256,512]{1,0:T(8,128)(2,1)S(1)}, u32[]{:S(2)}, u32[]{:S(2)}) collective-permute-start(bf16[256,512]{1,0:T(8,128)(2,1)} %collective-permute-done.5.refs_4_), channel_id=1, source_target_pairs={{0,1},{1,0},{2,3},{3,2},{4,5},{5,4},{6,7},{7,6},{8,9},{9,8},{10,11... | collective-permute-start | bytes 786440 | tf_op jit(solution)/shard_map/ppermute | solution.py:160
  49.8 4.4 %collective-permute-start.17 = (bf16[256,512]{1,0:T(8,128)(2,1)}, bf16[256,512]{1,0:T(8,128)(2,1)S(1)}, u32[]{:S(2)}, u32[]{:S(2)}) collective-permute-start(bf16[256,512]{1,0:T(8,128)(2,1)} %collective-permute-done.6.refs_5_), channel_id=1, source_target_pairs={{0,1},{1,0},{2,3},{3,2},{4,5},{5,4},{6,7},{7,6},{8,9},{9,8},{10,11... | collective-permute-start | bytes 786440 | tf_op jit(solution)/shard_map/ppermute | solution.py:160
  51.0 3.4 %collective-permute-start.18 = (bf16[256,512]{1,0:T(8,128)(2,1)S(1)}, bf16[256,512]{1,0:T(8,128)(2,1)S(1)}, u32[]{:S(2)}, u32[]{:S(2)}) collective-permute-start(bf16[256,512]{1,0:T(8,128)(2,1)S(1)} %collective-permute-done.7.refs_6_), channel_id=1, source_target_pairs={{0,1},{1,0},{2,3},{3,2},{4,5},{5,4},{6,7},{7,6},{8,9},{9,8},{10,11... | collective-permute-start | bytes 786440 | tf_op jit(solution)/shard_map/ppermute | solution.py:160
  53.9 5.3 %collective-permute-start.14 = (bf16[512,512]{1,0:T(8,128)(2,1)S(1)}, bf16[512,512]{1,0:T(8,128)(2,1)}, u32[]{:S(2)}, u32[]{:S(2)}) collective-permute-start(bf16[512,512]{1,0:T(8,128)(2,1)S(1)} %collective-permute-done.3.refs_2_), channel_id=1, source_target_pairs={{0,1},{1,0},{2,3},{3,2},{4,5},{5,4},{6,7},{7,6},{8,9},{9,8},{10,11... | collective-permute-start | bytes 1572872 | tf_op jit(solution)/shard_map/ppermute | solution.py:160
  54.3 7.8 %collective-permute-start.23 = (bf16[2,512,512]{2,1,0:T(8,128)(2,1)}, bf16[2,512,512]{2,1,0:T(8,128)(2,1)}, u32[]{:S(2)}, u32[]{:S(2)}) collective-permute-start(bf16[2,512,512]{2,1,0:T(8,128)(2,1)} %refs_22_.1), channel_id=1, source_target_pairs={{0,1},{1,0},{2,3},{3,2},{4,5},{5,4},{6,7},{7,6},{8,9},{9,8},{10,11... | collective-permute-start | bytes 3145736 | tf_op jit(solution)/shard_map/ppermute | solution.py:160
  54.4 7.7 %collective-permute-start.27 = (bf16[2,512,512]{2,1,0:T(8,128)(2,1)S(1)}, bf16[2,512,512]{2,1,0:T(8,128)(2,1)}, u32[]{:S(2)}, u32[]{:S(2)}) collective-permute-start(bf16[2,512,512]{2,1,0:T(8,128)(2,1)S(1)} %collective-permute-done.25.refs_26_), channel_id=1, source_target_pairs={{0,1},{1,0},{2,3},{3,2},{4,5},{5,4},{6,7},{7,6},{8,9},{9,8},{10,11... | collective-permute-start | bytes 3145736 | tf_op jit(solution)/shard_map/ppermute | solution.py:160
  55.4 4.8 %collective-permute-start.19 = (bf16[512,512]{1,0:T(8,128)(2,1)}, bf16[512,512]{1,0:T(8,128)(2,1)S(1)}, u32[]{:S(2)}, u32[]{:S(2)}) collective-permute-start(bf16[512,512]{1,0:T(8,128)(2,1)} %collective-permute-done.8.refs_7_), channel_id=1, source_target_pairs={{0,1},{1,0},{2,3},{3,2},{4,5},{5,4},{6,7},{7,6},{8,9},{9,8},{10,11... | collective-permute-start | bytes 1572872 | tf_op jit(solution)/shard_map/ppermute | solution.py:160
  56.9 4.6 %collective-permute-start.20 = (bf16[512,512]{1,0:T(8,128)(2,1)}, bf16[512,512]{1,0:T(8,128)(2,1)S(1)}, u32[]{:S(2)}, u32[]{:S(2)}) collective-permute-start(bf16[512,512]{1,0:T(8,128)(2,1)} %collective-permute-done.9.refs_8_), channel_id=1, source_target_pairs={{0,1},{1,0},{2,3},{3,2},{4,5},{5,4},{6,7},{7,6},{8,9},{9,8},{10,11... | collective-permute-start | bytes 1572872 | tf_op jit(solution)/shard_map/ppermute | solution.py:160
  (23 other events, 293.4 us)

commit v6 on v5

--- a/solution.py
+++ b/solution.py
@@ -8,7 +8,7 @@
 AXES = ("x_hi", "y_hi", "y_lo", "x_lo", "z", "core")
 SIZES = (2, 2, 2, 2, 4, 2)
 SECTOR = ("x_lo", "z", "core")
-REDUCE = ("x_hi", "y_hi", "x_lo", "z")
+REDUCE = ("x_hi", "y_lo", "x_lo", "z")
 SPREAD = ("x_hi", "y_hi", "y_lo", "core")
 RING = 4
 GROUP = 4
@@ -48,34 +48,35 @@
 
 
 def couplings_kernel(table, ends, dims, *refs):
-    own_waves, mate_waves = refs[:11], refs[11:22]
-    own_right, own_left, mate_right, mate_left, far_right, far_left, far_mate_right, far_mate_left = refs[22:30]
-    out, left, right, waves, halves, sums, rounded, op_sems, wave_sems, out_sems = refs[30:]
-    y, x, z, core = (lax.axis_index(name) for name in ("y_lo", "x_lo", "z", "core"))
+    own_waves, mate_waves = refs[:10], refs[10:20]
+    own_right, own_left, mate_right, mate_left, far, far_mate = refs[20:26]
+    out, left, right, waves, halves, sums, rounded, op_sems, wave_sems, out_sems = refs[26:]
+    y, x, z, core = (lax.axis_index(name) for name in ("y_hi", "x_lo", "z", "core"))
     sectors, width, _ = waves.shape
     rows = sums.shape[1]
-    ops = own_right.shape[0]
+    ops = own_right.shape[0] // width
     half = width // 2
     left_copies, right_copies = [], []
-    for n, (pair, c, left_rows, right_ops) in enumerate((
-        (y, core, own_left, own_right),
-        (y, 1 - core, mate_left, mate_right),
-        (1 - y, core, far_left, far_right),
-        (1 - y, 1 - core, far_mate_left, far_mate_right),
+    for n, (pair, c, left_rows, skip, right_ops) in enumerate((
+        (y, core, own_left, 0, own_right),
+        (y, 1 - core, mate_left, 0, mate_right),
+        (1 - y, core, far, ops * width, far),
+        (1 - y, 1 - core, far_mate, ops * width, far_mate),
     )):
         first = (pair * 2 + c) * ops
         size = ops * rows
+        part = left_rows.at[pl.ds(pl.multiple_of(skip + core * size, size), size)]
         to = left.at[pl.ds(pl.multiple_of(first * rows, size), size)]
-        left_copies.append(pltpu.make_async_copy(left_rows.at[core], to, op_sems.at[2 * n]))
-        right_copies.append(
-            pltpu.make_async_copy(right_ops, right.at[pl.ds(first, ops)], op_sems.at[2 * n + 1])
-        )
+        left_copies.append(pltpu.make_async_copy(part, to, op_sems.at[2 * n]))
+        part = right_ops.at[pl.ds(0, ops * width)]
+        to = right.at[pl.ds(pl.multiple_of(first * width, ops * width), ops * width)]
+        right_copies.append(pltpu.make_async_copy(part, to, op_sems.at[2 * n + 1]))
     for copy in left_copies:
         copy.start()
     whole, low, high = (pl.ds(0, width), pl.ds(0, half), pl.ds(half, half))
     places = (
         (0, whole), (1, whole), (2, whole), (3, low), (3, high),
-        (4, low), (4, high), (5, whole), (6, whole), (7, low), (7, high),
+        (4, whole), (5, whole), (6, whole), (7, low), (7, high),
     )
     for c, pieces in ((0, own_waves), (1, mate_waves)):
         for piece, (place, part) in zip(pieces, places):
@@ -127,7 +128,9 @@
                 op = lax.shift_right_logical(code, 9)
                 block = halves[source, pl.ds(pl.multiple_of(op * rows, rows), used), :inner]
                 sums[target, :used, :cols] += jnp.dot(
-                    block, right[op, :inner, :cols], preferred_element_type=jnp.float32
+                    block,
+                    right[pl.ds(pl.multiple_of(op * width, width), inner), :cols],
+                    preferred_element_type=jnp.float32,
                 )
             return carry
 
@@ -163,35 +166,31 @@
 def share(block, left_ops, right_ops, meta):
     ops, width, _ = left_ops.shape
     half = width // 2
+    size = ops * LEVELS * SLICE * 2
     rows = left_ops.reshape(ops, LEVELS, 2, 2, SLICE, width).transpose(2, 3, 0, 1, 4, 5)
-    rows = rows.reshape(2, 2, ops * LEVELS * SLICE, width)
-    y = lax.axis_index("y_lo")
+    rows = rows.reshape(2, size, width)
+    y = lax.axis_index("y_hi")
     near_rows = lax.dynamic_index_in_dim(rows, y, 0, keepdims=False)
     sent_rows = lax.dynamic_index_in_dim(rows, 1 - y, 0, keepdims=False)
-    far_right = lax.ppermute(right_ops, "y_lo", SWAP)
-    far_rows = lax.ppermute(sent_rows, "y_lo", SWAP)
+    near_right = right_ops.reshape(ops * width, width)
+    far = lax.ppermute(jnp.concatenate([near_right, sent_rows]), "y_hi", SWAP)
     before = lax.ppermute(block, "z", UP)
     after = lax.ppermute(block, "z", DOWN)
-    side_low = along_x(block[:half], UP)
-    side_high = along_x(block[half:], DOWN)
+    side = along_x(block, UP)
     across_low = lax.ppermute(before[:half], "z", UP)
     across_high = lax.ppermute(after[half:], "z", DOWN)
     side_before = along_x(before, UP)
     side_after = along_x(after, DOWN)
     corner_low = along_x(across_low, UP)
     corner_high = along_x(across_high, DOWN)
-    metas = jnp.stack([meta, lax.ppermute(meta, "y_lo", SWAP)])
+    early = (block, before, after, across_low, across_high, side, side_before, side_after)
+    held = lax.optimization_barrier(early + (near_right, near_rows))
+    mate_early = [to_mate(part) for part in held]
+    mate_late = [to_mate(part) for part in (corner_low, corner_high, far)]
+    metas = jnp.stack([meta, lax.ppermute(meta, "y_hi", SWAP)])
     metas = jnp.concatenate([metas, to_mate(metas)])
-    early = (
-        block, before, after, across_low, across_high, side_low, side_high, side_before, side_after,
-    )
-    own_waves = early + (corner_low, corner_high)
-    held = lax.optimization_barrier(early + (right_ops, near_rows))
-    mate_early = [to_mate(part) for part in held]
-    mate_late = [to_mate(part) for part in (corner_low, corner_high, far_right, far_rows)]
-    mate_waves = tuple(mate_early[:9] + mate_late[:2])
-    operators = (right_ops, near_rows, mate_early[9], mate_early[10], far_right, far_rows, mate_late[2], mate_late[3])
-    return own_waves + mate_waves + operators, metas
+    waves = early + (corner_low, corner_high) + tuple(mate_early[:8] + mate_late[:2])
+    return waves + (near_right, near_rows, mate_early[8], mate_early[9], far, mate_late[2]), metas
 
 
 def body(
@@ -207,7 +206,7 @@
     sectors = 4 * RING
     meta = jnp.stack([coupling_source, coupling_target, coupling_operator])
     shared, metas = share(wavefunction[0], left_ops, right_ops, meta)
-    y, core = lax.axis_index("y_lo"), lax.axis_index("core")
+    y, core = lax.axis_index("y_hi"), lax.axis_index("core")
     owners = jnp.stack([2 * y + core, 2 * (1 - y) + core, 2 * y + 1 - core, 2 * (1 - y) + 1 - core])
     chosen = metas[:, 2] + ops * owners.astype(jnp.int32)[:, None]
     table, ends = plan_couplings(
@@ -223,7 +222,7 @@
         out_specs=hbm,
         scratch_shapes=[
             pltpu.VMEM((ops * width, width), jnp.bfloat16),
-            pltpu.VMEM((ops * GROUP, width, width), jnp.bfloat16),
+            pltpu.VMEM((ops * GROUP * width, width), jnp.bfloat16),
             pltpu.VMEM((sectors, width, width), jnp.bfloat16),
             pltpu.VMEM((sectors, ops * width, width), jnp.bfloat16),
             pltpu.VMEM((sectors + 1, rows, width), jnp.float32),
@@ -239,6 +238,7 @@
     total = jnp.sum(got.astype(jnp.float32), axis=0).astype(jnp.bfloat16)
     spread = jnp.broadcast_to(total[None], (8,) + total.shape).reshape((16,) + total.shape[1:])
     whole = lax.all_to_all(spread, SPREAD, 0, 0, tiled=True)
+    whole = whole.reshape(2, 2, 2, 2, SLICE, width).transpose(0, 2, 1, 3, 4, 5)
     return whole.reshape(1, width, width).astype(jnp.float32)
 
 

time: 139 us -> 154 us (1.11)
  waiting for transfers between devices: 17.9 us -> 42.8 us
  starting transfers between devices: 36 us -> 26.4 us
  Pallas kernels: 21.4 us -> 19.6 us
    ppermute x3 -> x2, waiting for transfers between devices: 2.14 us -> 15.7 us  [the longest x1 15.7 us: share(): metas = jnp.stack([meta, lax.ppermute(meta, 'y_hi', SWAP)])]
    ppermute x16 -> x14, starting transfers between devices: 16.9 us -> 7.29 us  [to_mate(): return lax.ppermute(part, 'core', SWAP)]
    ppermute x1, waiting for transfers between devices: 0.49 us -> 9.06 us  [share(): after = lax.ppermute(block, 'z', DOWN)]
    ppermute x1, waiting for transfers between devices: 3.01 us -> 5.48 us  [share(): across_low = lax.ppermute(before[:half], 'z', UP)]
    ppermute x6 -> x5, starting transfers between devices: 8.37 us -> 6.34 us  [along_x(): return lax.ppermute(part, ('x_hi', 'x_lo'), steps)]
    slice x1 -> x0, local copies, waits for them, and re-layouts: 1.86 us -> none  [share(): side_high = along_x(block[half:], DOWN)]
    pallas_call x1, Pallas kernels: 21.4 us -> 19.6 us  [body(): pl.pallas_call(couplings_kernel, out_shape=jax.ShapeDtypeStruct((LEVELS,...]
    unnamed x36 -> x40, local copies, waits for them, and re-layouts: 0.86 us -> 2.61 us
  transfers between devices with their start and end apart: 29 -> 25, of which waited for: 14 -> 12; matrix products, arithmetic and copies ran while one was open for 6% -> 2% of each run, Pallas kernels for 0% -> 0%
where the time goes in v6:
time: 154 us; the launch traced here: 153 us
  blocking collectives  53.4 us (35%)
  waiting for transfers between devices  42.8 us (28%)
  starting transfers between devices  26.4 us (17%)
  Pallas kernels  19.6 us (13%)
  local copies, waits for them, and re-layouts  7.1 us (5%)
  other arithmetic  3.04 us (2%)
    all_to_all x1, blocking collectives, body(): lax.all_to_all(partial.reshape(-1, 2, SLICE, width), REDUCE, 0, 0, tiled=...  34 us
    pallas_call x1, Pallas kernels, body(): pl.pallas_call(couplings_kernel, out_shape=jax.ShapeDtypeStruct((LEVELS,...  19.6 us
    all_to_all x1, blocking collectives, body(): whole = lax.all_to_all(spread, SPREAD, 0, 0, tiled=True)  19.4 us
    ppermute x1, waiting for transfers between devices, share(): metas = jnp.stack([meta, lax.ppermute(meta, 'y_hi', SWAP)])  15.7 us
    ppermute x1, waiting for transfers between devices, share(): after = lax.ppermute(block, 'z', DOWN)  9.06 us
    ppermute x14, starting transfers between devices, to_mate(): return lax.ppermute(part, 'core', SWAP)  7.29 us
    ppermute x14, waiting for transfers between devices, to_mate(): return lax.ppermute(part, 'core', SWAP)  6.35 us
    ppermute x5, starting transfers between devices, along_x(): return lax.ppermute(part, ('x_hi', 'x_lo'), steps)  6.34 us
  transfers between devices with their start and end apart: 25, of which 12 were waited for; matrix products, arithmetic and copies ran while one was open for 2% of the time, Pallas kernels for 0%

profile of v6, /device:TPU:1, one launch (start us, length us, event | category | flops | bytes accessed | tf_op | source)
XLA Modules:
  0.0 152.6 jit_solution(1560736846057821532)
XLA Ops:
  0.0 1.3 copy.12
  1.4 1.3 copy-done
  2.7 1.3 pad_maximum_fusion
  4.0 3.7 %collective-permute-start.23 = (bf16[1536,512]{1,0:T(8,128)(2,1)}, bf16[1536,512]{1,0:T(8,128)(2,1)}, u32[]{:S(2)}, u32[]{:S(2)}) collective-permute-start(bf16[1536,512]{1,0:T(8,128)(2,1)} %pad_maximum_fusion), channel_id=1, source_target_pairs={{0,32},{32,0},{1,33},{33,1},{2,34},{34,2},{3,35},{35,3},{4,36},{36... | collective-permute-start | bytes 4718600 | tf_op jit(solution)/shard_map/ppermute | solution.py:176
  7.8 3.8 %collective-permute-start.3 = (bf16[512,512]{1,0:T(8,128)(2,1)S(1)}, bf16[512,512]{1,0:T(8,128)(2,1)S(1)}, u32[]{:S(2)}, u32[]{:S(2)}) collective-permute-start(bf16[512,512]{1,0:T(8,128)(2,1)S(1)} %bitcast.36), channel_id=1, source_target_pairs={{0,6},{2,0},{4,2},{6,4},{1,7},{3,1},{5,3},{7,5},{8,14},{10,8},{12,... | collective-permute-start | bytes 1572872 | tf_op jit(solution)/shard_map/ppermute | solution.py:178
  11.5 1.2 collective-permute-start.6
  12.7 9.1 %collective-permute-done.3.refs_2_ = bf16[512,512]{1,0:T(8,128)(2,1)S(1)} collective-permute-done((bf16[512,512]{1,0:T(8,128)(2,1)S(1)}, bf16[512,512]{1,0:T(8,128)(2,1)S(1)}, u32[]{:S(2)}, u32[]{:S(2)}) %collective-permute-start.3) | collective-permute-done | bytes 524320 | tf_op jit(solution)/shard_map/ppermute | solution.py:178
  22.6 3.5 %collective-permute-start.5 = (bf16[256,512]{1,0:T(8,128)(2,1)}, bf16[256,512]{1,0:T(8,128)(2,1)S(1)}, u32[]{:S(2)}, u32[]{:S(2)}) collective-permute-start(bf16[256,512]{1,0:T(8,128)(2,1)} %slice.21), channel_id=1, source_target_pairs={{0,6},{2,0},{4,2},{6,4},{1,7},{3,1},{5,3},{7,5},{8,14},{10,8},{12,... | collective-permute-start | bytes 786440 | tf_op jit(solution)/shard_map/ppermute | solution.py:181
  26.3 15.7 %collective-permute-done = s32[3,24]{1,0:T(4,128)S(1)} collective-permute-done((s32[3,24]{1,0:T(4,128)S(1)}, s32[3,24]{1,0:T(4,128)S(1)}, u32[]{:S(2)}, u32[]{:S(2)}) %collective-permute-start) | collective-permute-done | bytes 320 | tf_op jit(solution)/shard_map/ppermute | solution.py:190
  42.0 1.5 collective-permute-start.1
  44.3 2.5 %collective-permute-start.8 = (bf16[512,512]{1,0:T(8,128)(2,1)S(1)}, bf16[512,512]{1,0:T(8,128)(2,1)}, u32[]{:S(2)}, u32[]{:S(2)}) collective-permute-start(bf16[512,512]{1,0:T(8,128)(2,1)S(1)} %collective-permute-done.3.refs_2_), channel_id=1, source_target_pairs={{0,72},{8,0},{64,8},{72,64},{1,73},{9,1},{65,9},{73,65},{2,74},{10... | collective-permute-start | bytes 1572872 | tf_op jit(solution)/shard_map/ppermute | solution.py:159
  47.6 1.6 %collective-permute-start.4 = (bf16[256,512]{1,0:T(8,128)(2,1)}, bf16[256,512]{1,0:T(8,128)(2,1)}, u32[]{:S(2)}, u32[]{:S(2)}) collective-permute-start(bf16[256,512]{1,0:T(8,128)(2,1)} %slice.20), channel_id=1, source_target_pairs={{0,2},{2,4},{4,6},{6,0},{1,3},{3,5},{5,7},{7,1},{8,10},{10,12},{12... | collective-permute-start | bytes 786440 | tf_op jit(solution)/shard_map/ppermute | solution.py:180
  49.3 2.6 %collective-permute-start.10 = (bf16[256,512]{1,0:T(8,128)(2,1)S(1)}, bf16[256,512]{1,0:T(8,128)(2,1)}, u32[]{:S(2)}, u32[]{:S(2)}) collective-permute-start(bf16[256,512]{1,0:T(8,128)(2,1)S(1)} %collective-permute-done.5.refs_4_), channel_id=1, source_target_pairs={{0,72},{8,0},{64,8},{72,64},{1,73},{9,1},{65,9},{73,65},{2,74},{10... | collective-permute-start | bytes 786440 | tf_op jit(solution)/shard_map/ppermute | solution.py:159
  52.3 5.5 %collective-permute-done.4.refs_3_ = bf16[256,512]{1,0:T(8,128)(2,1)} collective-permute-done((bf16[256,512]{1,0:T(8,128)(2,1)}, bf16[256,512]{1,0:T(8,128)(2,1)}, u32[]{:S(2)}, u32[]{:S(2)}) %collective-permute-start.4) | collective-permute-done | bytes 262176 | tf_op jit(solution)/shard_map/ppermute | solution.py:180
  57.8 5.6 %collective-permute-done.10.refs_9_ = bf16[256,512]{1,0:T(8,128)(2,1)} collective-permute-done((bf16[256,512]{1,0:T(8,128)(2,1)S(1)}, bf16[256,512]{1,0:T(8,128)(2,1)}, u32[]{:S(2)}, u32[]{:S(2)}) %collective-permute-start.10) | collective-permute-done | bytes 262176 | tf_op jit(solution)/shard_map/ppermute | solution.py:159
  63.4 1.2 collective-permute-start.20
  66.0 2.0 %collective-permute-start.15 = (bf16[256,512]{1,0:T(8,128)(2,1)S(1)}, bf16[256,512]{1,0:T(8,128)(2,1)S(1)}, u32[]{:S(2)}, u32[]{:S(2)}) collective-permute-start(bf16[256,512]{1,0:T(8,128)(2,1)S(1)} %collective-permute-done.5.refs_4_), channel_id=1, source_target_pairs={{0,1},{1,0},{2,3},{3,2},{4,5},{5,4},{6,7},{7,6},{8,9},{9,8},{10,11... | collective-permute-start | bytes 786440 | tf_op jit(solution)/shard_map/ppermute | solution.py:163
  68.2 1.8 %collective-permute-done.19.refs_18_ = bf16[256,512]{1,0:T(8,128)(2,1)S(1)} collective-permute-done((bf16[256,512]{1,0:T(8,128)(2,1)S(1)}, bf16[256,512]{1,0:T(8,128)(2,1)S(1)}, u32[]{:S(2)}, u32[]{:S(2)}) %collective-permute-start.19) | collective-permute-done | bytes 262176 | tf_op jit(solution)/shard_map/ppermute | solution.py:163
  72.4 1.2 collective-permute-done.13.refs_12_
  75.1 1.5 collective-permute-done.18.refs_17_
  78.0 19.6 %couplings.1 = bf16[4,16,32,512]{3,2,1,0:T(8,128)(2,1)} custom-call(s32[120]{0:T(128)} %broadcast_add_fusion.table, s32[4]{0:T(128)} %copy-done.16, s32[16]{0:T(128)} %dims.1, bf16[512,512]{1,0:T(8,128)(2,1)} %bitcast.35, bf16[512,512]{1,0:T(8,128)(2,1)} %copy-done.3, bf16[512,512]{1,0:T(8,128)(2,1)} %copy-done.2, ...), custom_call_target="tpu_custom_call" | custom-call | tf_op jit(solution)/shard_map/couplings/pallas_call | solution.py:218
  97.6 34.0 %all_to_all.10 = bf16[32,2,32,512]{3,2,1,0:T(8,128)(2,1)S(1)} all-to-all(bf16[32,2,32,512]{3,2,1,0:T(8,128)(2,1)} %bitcast.27), channel_id=1, replica_groups=mesh['x_hi'=2,'y_hi'=2,'y_lo'=2,'x_lo'=2,'z'=4,'core'=2] {'x_hi','y_lo',..., dimensions={0} | all-to-all | bytes 4194304 | tf_op jit(solution)/shard_map/all_to_all | solution.py:237
  132.0 19.4 %all_to_all.11 = bf16[16,32,512]{2,1,0:T(8,128)(2,1)S(1)} all-to-all(bf16[16,32,512]{2,1,0:T(8,128)(2,1)S(1)} %bitcast.33), channel_id=1, replica_groups=mesh['x_hi'=2,'y_hi'=2,'y_lo'=2,'x_lo'=2,'z'=4,'core'=2] {'x_hi','y_hi',..., dimensions={0} | all-to-all | bytes 1048576 | tf_op jit(solution)/shard_map/all_to_all | solution.py:240
  151.5 1.1 copy.13
  (99 shorter events, 10.4 us)
Async XLA Ops:
  4.0 60.7 %collective-permute-start.23 = (bf16[1536,512]{1,0:T(8,128)(2,1)}, bf16[1536,512]{1,0:T(8,128)(2,1)}, u32[]{:S(2)}, u32[]{:S(2)}) collective-permute-start(bf16[1536,512]{1,0:T(8,128)(2,1)} %pad_maximum_fusion), channel_id=1, source_target_pairs={{0,32},{32,0},{1,33},{33,1},{2,34},{34,2},{3,35},{35,3},{4,36},{36... | collective-permute-start | bytes 4718600 | tf_op jit(solution)/shard_map/ppermute | solution.py:176
  7.8 14.0 %collective-permute-start.3 = (bf16[512,512]{1,0:T(8,128)(2,1)S(1)}, bf16[512,512]{1,0:T(8,128)(2,1)S(1)}, u32[]{:S(2)}, u32[]{:S(2)}) collective-permute-start(bf16[512,512]{1,0:T(8,128)(2,1)S(1)} %bitcast.36), channel_id=1, source_target_pairs={{0,6},{2,0},{4,2},{6,4},{1,7},{3,1},{5,3},{7,5},{8,14},{10,8},{12,... | collective-permute-start | bytes 1572872 | tf_op jit(solution)/shard_map/ppermute | solution.py:178
  11.5 35.3 %collective-permute-start.2 = (bf16[512,512]{1,0:T(8,128)(2,1)S(1)}, bf16[512,512]{1,0:T(8,128)(2,1)S(1)}, u32[]{:S(2)}, u32[]{:S(2)}) collective-permute-start(bf16[512,512]{1,0:T(8,128)(2,1)S(1)} %bitcast.37), channel_id=1, source_target_pairs={{0,2},{2,4},{4,6},{6,0},{1,3},{3,5},{5,7},{7,1},{8,10},{10,12},{12... | collective-permute-start | bytes 1572872 | tf_op jit(solution)/shard_map/ppermute | solution.py:177
  11.5 36.1 %collective-permute-start.6 = (bf16[512,512]{1,0:T(8,128)(2,1)S(1)}, bf16[512,512]{1,0:T(8,128)(2,1)}, u32[]{:S(2)}, u32[]{:S(2)}) collective-permute-start(bf16[512,512]{1,0:T(8,128)(2,1)S(1)} %bitcast.38), channel_id=1, source_target_pairs={{0,8},{8,64},{64,72},{72,0},{1,9},{9,65},{65,73},{73,1},{2,10},{10... | collective-permute-start | bytes 1572872 | tf_op jit(solution)/shard_map/ppermute | solution.py:159
  22.6 26.6 %collective-permute-start.5 = (bf16[256,512]{1,0:T(8,128)(2,1)}, bf16[256,512]{1,0:T(8,128)(2,1)S(1)}, u32[]{:S(2)}, u32[]{:S(2)}) collective-permute-start(bf16[256,512]{1,0:T(8,128)(2,1)} %slice.21), channel_id=1, source_target_pairs={{0,6},{2,0},{4,2},{6,4},{1,7},{3,1},{5,3},{7,5},{8,14},{10,8},{12,... | collective-permute-start | bytes 786440 | tf_op jit(solution)/shard_map/ppermute | solution.py:181
  26.1 15.8 %collective-permute-start = (s32[3,24]{1,0:T(4,128)S(1)}, s32[3,24]{1,0:T(4,128)S(1)}, u32[]{:S(2)}, u32[]{:S(2)}) collective-permute-start(s32[3,24]{1,0:T(4,128)S(1)} %get-tuple-element.33), channel_id=1, source_target_pairs={{0,32},{32,0},{1,33},{33,1},{2,34},{34,2},{3,35},{35,3},{4,36},{36... | collective-permute-start | bytes 872 | tf_op jit(solution)/shard_map/ppermute | solution.py:190
  42.0 2.3 %collective-permute-start.1 = (s32[2,3,24]{2,1,0:T(4,128)S(1)}, s32[2,3,24]{2,1,0:T(4,128)S(1)}, u32[]{:S(2)}, u32[]{:S(2)}) collective-permute-start(s32[2,3,24]{2,1,0:T(4,128)S(1)} %pad_add_fusion), channel_id=1, source_target_pairs={{0,1},{1,0},{2,3},{3,2},{4,5},{5,4},{6,7},{7,6},{8,9},{9,8},{10,11... | collective-permute-start | bytes 1736 | tf_op jit(solution)/shard_map/ppermute | solution.py:163
  44.3 20.4 %collective-permute-start.8 = (bf16[512,512]{1,0:T(8,128)(2,1)S(1)}, bf16[512,512]{1,0:T(8,128)(2,1)}, u32[]{:S(2)}, u32[]{:S(2)}) collective-permute-start(bf16[512,512]{1,0:T(8,128)(2,1)S(1)} %collective-permute-done.3.refs_2_), channel_id=1, source_target_pairs={{0,72},{8,0},{64,8},{72,64},{1,73},{9,1},{65,9},{73,65},{2,74},{10... | collective-permute-start | bytes 1572872 | tf_op jit(solution)/shard_map/ppermute | solution.py:159
  46.8 17.8 %collective-permute-start.7 = (bf16[512,512]{1,0:T(8,128)(2,1)S(1)}, bf16[512,512]{1,0:T(8,128)(2,1)}, u32[]{:S(2)}, u32[]{:S(2)}) collective-permute-start(bf16[512,512]{1,0:T(8,128)(2,1)S(1)} %collective-permute-done.2.refs_1_), channel_id=1, source_target_pairs={{0,8},{8,64},{64,72},{72,0},{1,9},{9,65},{65,73},{73,1},{2,10},{10... | collective-permute-start | bytes 1572872 | tf_op jit(solution)/shard_map/ppermute | solution.py:159
  47.6 10.2 %collective-permute-start.4 = (bf16[256,512]{1,0:T(8,128)(2,1)}, bf16[256,512]{1,0:T(8,128)(2,1)}, u32[]{:S(2)}, u32[]{:S(2)}) collective-permute-start(bf16[256,512]{1,0:T(8,128)(2,1)} %slice.20), channel_id=1, source_target_pairs={{0,2},{2,4},{4,6},{6,0},{1,3},{3,5},{5,7},{7,1},{8,10},{10,12},{12... | collective-permute-start | bytes 786440 | tf_op jit(solution)/shard_map/ppermute | solution.py:180
  49.3 14.1 %collective-permute-start.10 = (bf16[256,512]{1,0:T(8,128)(2,1)S(1)}, bf16[256,512]{1,0:T(8,128)(2,1)}, u32[]{:S(2)}, u32[]{:S(2)}) collective-permute-start(bf16[256,512]{1,0:T(8,128)(2,1)S(1)} %collective-permute-done.5.refs_4_), channel_id=1, source_target_pairs={{0,72},{8,0},{64,8},{72,64},{1,73},{9,1},{65,9},{73,65},{2,74},{10... | collective-permute-start | bytes 786440 | tf_op jit(solution)/shard_map/ppermute | solution.py:159
  57.8 8.2 %collective-permute-start.9 = (bf16[256,512]{1,0:T(8,128)(2,1)}, bf16[256,512]{1,0:T(8,128)(2,1)S(1)}, u32[]{:S(2)}, u32[]{:S(2)}) collective-permute-start(bf16[256,512]{1,0:T(8,128)(2,1)} %collective-permute-done.4.refs_3_), channel_id=1, source_target_pairs={{0,8},{8,64},{64,72},{72,0},{1,9},{9,65},{65,73},{73,1},{2,10},{10... | collective-permute-start | bytes 786440 | tf_op jit(solution)/shard_map/ppermute | solution.py:159
  63.4 4.6 %collective-permute-start.20 = (bf16[256,512]{1,0:T(8,128)(2,1)}, bf16[256,512]{1,0:T(8,128)(2,1)S(1)}, u32[]{:S(2)}, u32[]{:S(2)}) collective-permute-start(bf16[256,512]{1,0:T(8,128)(2,1)} %collective-permute-done.10.refs_9_), channel_id=1, source_target_pairs={{0,1},{1,0},{2,3},{3,2},{4,5},{5,4},{6,7},{7,6},{8,9},{9,8},{10,11... | collective-permute-start | bytes 786440 | tf_op jit(solution)/shard_map/ppermute | solution.py:163
  64.7 6.1 %collective-permute-start.11 = (bf16[512,512]{1,0:T(8,128)(2,1)S(1)}, bf16[512,512]{1,0:T(8,128)(2,1)S(1)}, u32[]{:S(2)}, u32[]{:S(2)}) collective-permute-start(bf16[512,512]{1,0:T(8,128)(2,1)S(1)} %bitcast.39), channel_id=1, source_target_pairs={{0,1},{1,0},{2,3},{3,2},{4,5},{5,4},{6,7},{7,6},{8,9},{9,8},{10,11... | collective-permute-start | bytes 1572872 | tf_op jit(solution)/shard_map/ppermute | solution.py:163
  64.8 12.4 %collective-permute-start.24 = (bf16[1536,512]{1,0:T(8,128)(2,1)}, bf16[1536,512]{1,0:T(8,128)(2,1)}, u32[]{:S(2)}, u32[]{:S(2)}) collective-permute-start(bf16[1536,512]{1,0:T(8,128)(2,1)} %collective-permute-done.23.refs_24_), channel_id=1, source_target_pairs={{0,1},{1,0},{2,3},{3,2},{4,5},{5,4},{6,7},{7,6},{8,9},{9,8},{10,11... | collective-permute-start | bytes 4718600 | tf_op jit(solution)/shard_map/ppermute | solution.py:163
  65.3 5.0 %collective-permute-start.14 = (bf16[256,512]{1,0:T(8,128)(2,1)}, bf16[256,512]{1,0:T(8,128)(2,1)S(1)}, u32[]{:S(2)}, u32[]{:S(2)}) collective-permute-start(bf16[256,512]{1,0:T(8,128)(2,1)} %collective-permute-done.4.refs_3_), channel_id=1, source_target_pairs={{0,1},{1,0},{2,3},{3,2},{4,5},{5,4},{6,7},{7,6},{8,9},{9,8},{10,11... | collective-permute-start | bytes 786440 | tf_op jit(solution)/shard_map/ppermute | solution.py:163
  66.0 4.6 %collective-permute-start.15 = (bf16[256,512]{1,0:T(8,128)(2,1)S(1)}, bf16[256,512]{1,0:T(8,128)(2,1)S(1)}, u32[]{:S(2)}, u32[]{:S(2)}) collective-permute-start(bf16[256,512]{1,0:T(8,128)(2,1)S(1)} %collective-permute-done.5.refs_4_), channel_id=1, source_target_pairs={{0,1},{1,0},{2,3},{3,2},{4,5},{5,4},{6,7},{7,6},{8,9},{9,8},{10,11... | collective-permute-start | bytes 786440 | tf_op jit(solution)/shard_map/ppermute | solution.py:163
  70.0 2.0 %collective-permute-start.12 = (bf16[512,512]{1,0:T(8,128)(2,1)S(1)}, bf16[512,512]{1,0:T(8,128)(2,1)}, u32[]{:S(2)}, u32[]{:S(2)}) collective-permute-start(bf16[512,512]{1,0:T(8,128)(2,1)S(1)} %collective-permute-done.2.refs_1_), channel_id=1, source_target_pairs={{0,1},{1,0},{2,3},{3,2},{4,5},{5,4},{6,7},{7,6},{8,9},{9,8},{10,11... | collective-permute-start | bytes 1572872 | tf_op jit(solution)/shard_map/ppermute | solution.py:163
  70.2 3.3 %collective-permute-start.13 = (bf16[512,512]{1,0:T(8,128)(2,1)S(1)}, bf16[512,512]{1,0:T(8,128)(2,1)}, u32[]{:S(2)}, u32[]{:S(2)}) collective-permute-start(bf16[512,512]{1,0:T(8,128)(2,1)S(1)} %collective-permute-done.3.refs_2_), channel_id=1, source_target_pairs={{0,1},{1,0},{2,3},{3,2},{4,5},{5,4},{6,7},{7,6},{8,9},{9,8},{10,11... | collective-permute-start | bytes 1572872 | tf_op jit(solution)/shard_map/ppermute | solution.py:163
  70.5 3.2 %collective-permute-start.16 = (bf16[512,512]{1,0:T(8,128)(2,1)}, bf16[512,512]{1,0:T(8,128)(2,1)}, u32[]{:S(2)}, u32[]{:S(2)}) collective-permute-start(bf16[512,512]{1,0:T(8,128)(2,1)} %collective-permute-done.6.refs_5_), channel_id=1, source_target_pairs={{0,1},{1,0},{2,3},{3,2},{4,5},{5,4},{6,7},{7,6},{8,9},{9,8},{10,11... | collective-permute-start | bytes 1572872 | tf_op jit(solution)/shard_map/ppermute | solution.py:163
  70.8 6.4 %collective-permute-start.21 = (bf16[1024,512]{1,0:T(8,128)(2,1)S(1)}, bf16[1024,512]{1,0:T(8,128)(2,1)}, u32[]{:S(2)}, u32[]{:S(2)}) collective-permute-start(bf16[1024,512]{1,0:T(8,128)(2,1)S(1)} %bitcast.30), channel_id=1, source_target_pairs={{0,1},{1,0},{2,3},{3,2},{4,5},{5,4},{6,7},{7,6},{8,9},{9,8},{10,11... | collective-permute-start | bytes 3145736 | tf_op jit(solution)/shard_map/ppermute | solution.py:163
  72.1 3.1 %collective-permute-start.17 = (bf16[512,512]{1,0:T(8,128)(2,1)}, bf16[512,512]{1,0:T(8,128)(2,1)S(1)}, u32[]{:S(2)}, u32[]{:S(2)}) collective-permute-start(bf16[512,512]{1,0:T(8,128)(2,1)} %collective-permute-done.7.refs_6_), channel_id=1, source_target_pairs={{0,1},{1,0},{2,3},{3,2},{4,5},{5,4},{6,7},{7,6},{8,9},{9,8},{10,11... | collective-permute-start | bytes 1572872 | tf_op jit(solution)/shard_map/ppermute | solution.py:163
  73.6 3.1 %collective-permute-start.18 = (bf16[512,512]{1,0:T(8,128)(2,1)}, bf16[512,512]{1,0:T(8,128)(2,1)S(1)}, u32[]{:S(2)}, u32[]{:S(2)}) collective-permute-start(bf16[512,512]{1,0:T(8,128)(2,1)} %collective-permute-done.8.refs_7_), channel_id=1, source_target_pairs={{0,1},{1,0},{2,3},{3,2},{4,5},{5,4},{6,7},{7,6},{8,9},{9,8},{10,11... | collective-permute-start | bytes 1572872 | tf_op jit(solution)/shard_map/ppermute | solution.py:163
  73.8 3.4 %collective-permute-start.22 = (bf16[512,512]{1,0:T(8,128)(2,1)S(1)}, bf16[512,512]{1,0:T(8,128)(2,1)S(1)}, u32[]{:S(2)}, u32[]{:S(2)}) collective-permute-start(bf16[512,512]{1,0:T(8,128)(2,1)S(1)} %get-tuple-element.24.refs_21_), channel_id=1, source_target_pairs={{0,1},{1,0},{2,3},{3,2},{4,5},{5,4},{6,7},{7,6},{8,9},{9,8},{10,11... | collective-permute-start | bytes 1572872 | tf_op jit(solution)/shard_map/ppermute | solution.py:163
  (21 other events, 337.8 us)

commit v7 on v6

--- a/solution.py
+++ b/solution.py
@@ -17,6 +17,7 @@
 SLICE = GRAIN // GROUP
 STEP = 8
 KINDS = 4
+AHEAD = 4
 MIB = 1024 * 1024
 SWAP = [(0, 1), (1, 0)]
 UP = [(i, (i + 1) % RING) for i in range(RING)]
@@ -78,17 +79,31 @@
         (0, whole), (1, whole), (2, whole), (3, low), (3, high),
         (4, whole), (5, whole), (6, whole), (7, low), (7, high),
     )
+    wave_copies = [[] for _ in range(sectors)]
     for c, pieces in ((0, own_waves), (1, mate_waves)):
         for piece, (place, part) in zip(pieces, places):
             slot = c * (sectors // 2) + place
-            pltpu.make_async_copy(piece, waves.at[slot, part], wave_sems.at[slot]).start()
-    for copy in right_copies:
-        copy.start()
+            wave_copies[slot].append(pltpu.make_async_copy(piece, waves.at[slot, part], wave_sems.at[slot]))
+    for slot in range(AHEAD):
+        for copy in wave_copies[slot]:
+            copy.start()
     sums[...] = jnp.zeros_like(sums)
     for copy in left_copies:
         copy.wait()
 
     def first_half(slot, carry):
+        for later in range(AHEAD, sectors):
+
+            @pl.when(slot == later - AHEAD)
+            def _(later=later):
+                for copy in wave_copies[later]:
+                    copy.start()
+
+        @pl.when(slot == sectors - AHEAD)
+        def _():
+            for copy in right_copies:
+                copy.start()
+
         pltpu.make_async_copy(waves.at[slot], waves.at[slot], wave_sems.at[slot]).wait()
         other_core = lax.div(slot, sectors // 2)
         other_x = lax.rem(lax.div(slot, RING), 2)
@@ -173,7 +188,9 @@
     near_rows = lax.dynamic_index_in_dim(rows, y, 0, keepdims=False)
     sent_rows = lax.dynamic_index_in_dim(rows, 1 - y, 0, keepdims=False)
     near_right = right_ops.reshape(ops * width, width)
-    far = lax.ppermute(jnp.concatenate([near_right, sent_rows]), "y_hi", SWAP)
+    far_meta = lax.ppermute(meta, "y_hi", SWAP)
+    sent_right, sent_rows, far_meta = lax.optimization_barrier((near_right, sent_rows, far_meta))
+    far = lax.ppermute(jnp.concatenate([sent_right, sent_rows]), "y_hi", SWAP)
     before = lax.ppermute(block, "z", UP)
     after = lax.ppermute(block, "z", DOWN)
     side = along_x(block, UP)
@@ -187,7 +204,8 @@
     held = lax.optimization_barrier(early + (near_right, near_rows))
     mate_early = [to_mate(part) for part in held]
     mate_late = [to_mate(part) for part in (corner_low, corner_high, far)]
-    metas = jnp.stack([meta, lax.ppermute(meta, "y_hi", SWAP)])
+    metas = jnp.stack([meta, far_meta])
+    metas, _ = lax.optimization_barrier((metas, held[6]))
     metas = jnp.concatenate([metas, to_mate(metas)])
     waves = early + (corner_low, corner_high) + tuple(mate_early[:8] + mate_late[:2])
     return waves + (near_right, near_rows, mate_early[8], mate_early[9], far, mate_late[2]), metas

time: 154 us -> 133 us (0.86)
  waiting for transfers between devices: 42.8 us -> 19.6 us
  starting transfers between devices: 26.4 us -> 30.5 us
  blocking collectives: 53.4 us -> 51.7 us
    ppermute x2, waiting for transfers between devices: 15.7 us -> 0.67 us  [the longest x1 0.67 us: share(): far = lax.ppermute(jnp.concatenate([sent_right, sent_rows]), 'y_hi', SWAP)]
    ppermute x5, waiting for transfers between devices: 6.21 us -> 0.01 us  [along_x(): return lax.ppermute(part, ('x_hi', 'x_lo'), steps)]
    ppermute x14, starting transfers between devices: 7.29 us -> 13.1 us  [to_mate(): return lax.ppermute(part, 'core', SWAP)]
    ppermute x1, waiting for transfers between devices: 5.48 us -> 2.09 us  [share(): across_low = lax.ppermute(before[:half], 'z', UP)]
    ppermute x1, waiting for transfers between devices: 0.01 us -> 2.65 us  [share(): across_high = lax.ppermute(after[half:], 'z', DOWN)]
    ppermute x1, starting transfers between devices: 3.52 us -> 1.61 us  [share(): across_high = lax.ppermute(after[half:], 'z', DOWN)]
    ppermute x1, starting transfers between devices: 1.64 us -> 0.01 us  [share(): across_low = lax.ppermute(before[:half], 'z', UP)]
    unnamed x40 -> x29, local copies, waits for them, and re-layouts: 2.61 us -> 3.27 us
  transfers between devices with their start and end apart: 25 -> 25, of which waited for: 12 -> 10; matrix products, arithmetic and copies ran while one was open for 2% -> 3% of each run, Pallas kernels for 0% -> 0%
where the time goes in v7:
time: 133 us
  blocking collectives  51.7 us (39%)
  starting transfers between devices  30.5 us (23%)
  waiting for transfers between devices  19.6 us (15%)
  Pallas kernels  19.2 us (14%)
  local copies, waits for them, and re-layouts  7.68 us (6%)
  other arithmetic  3.69 us (3%)
    all_to_all x1, blocking collectives, body(): lax.all_to_all(partial.reshape(-1, 2, SLICE, width), REDUCE, 0, 0, tiled=...  32.5 us
    pallas_call x1, Pallas kernels, body(): pl.pallas_call(couplings_kernel, out_shape=jax.ShapeDtypeStruct((LEVELS,...  19.2 us
    all_to_all x1, blocking collectives, body(): whole = lax.all_to_all(spread, SPREAD, 0, 0, tiled=True)  19.2 us
    ppermute x14, starting transfers between devices, to_mate(): return lax.ppermute(part, 'core', SWAP)  13.1 us
    ppermute x1, waiting for transfers between devices, share(): after = lax.ppermute(block, 'z', DOWN)  7.9 us
    ppermute x5, starting transfers between devices, along_x(): return lax.ppermute(part, ('x_hi', 'x_lo'), steps)  7.07 us
    ppermute x14, waiting for transfers between devices, to_mate(): return lax.ppermute(part, 'core', SWAP)  5.55 us
    ppermute x1, starting transfers between devices, share(): far_meta = lax.ppermute(meta, 'y_hi', SWAP)  3.81 us
  transfers between devices with their start and end apart: 25, of which 10 were waited for; matrix products, arithmetic and copies ran while one was open for 3% of the time, Pallas kernels for 0%

profile of v7, /device:TPU:1, one launch (start us, length us, event | category | flops | bytes accessed | tf_op | source)
XLA Modules:
  0.0 132.6 jit_solution(17823972678143039467)
XLA Ops:
  0.7 3.8 %collective-permute-start = (s32[3,24]{1,0:T(4,128)S(1)}, s32[3,24]{1,0:T(4,128)S(1)}, u32[]{:S(2)}, u32[]{:S(2)}) collective-permute-start(s32[3,24]{1,0:T(4,128)S(1)} %get-tuple-element.41), channel_id=1, source_target_pairs={{0,32},{32,0},{1,33},{33,1},{2,34},{34,2},{3,35},{35,3},{4,36},{36... | collective-permute-start | bytes 872 | tf_op jit(solution)/shard_map/ppermute | solution.py:191
  4.5 1.3 copy.12
  6.0 1.3 copy-done
  7.3 1.3 pad_maximum_fusion
  8.5 1.2 collective-permute-start.23
  9.7 3.8 %collective-permute-start.2 = (bf16[512,512]{1,0:T(8,128)(2,1)S(1)}, bf16[512,512]{1,0:T(8,128)(2,1)S(1)}, u32[]{:S(2)}, u32[]{:S(2)}) collective-permute-start(bf16[512,512]{1,0:T(8,128)(2,1)S(1)} %bitcast.36), channel_id=1, source_target_pairs={{0,6},{2,0},{4,2},{6,4},{1,7},{3,1},{5,3},{7,5},{8,14},{10,8},{12,... | collective-permute-start | bytes 1572872 | tf_op jit(solution)/shard_map/ppermute | solution.py:195
  13.5 1.2 collective-permute-start.5
  14.7 7.9 %collective-permute-done.2.refs_2_ = bf16[512,512]{1,0:T(8,128)(2,1)S(1)} collective-permute-done((bf16[512,512]{1,0:T(8,128)(2,1)S(1)}, bf16[512,512]{1,0:T(8,128)(2,1)S(1)}, u32[]{:S(2)}, u32[]{:S(2)}) %collective-permute-start.2) | collective-permute-done | bytes 524320 | tf_op jit(solution)/shard_map/ppermute | solution.py:195
  22.6 2.5 %collective-permute-start.7 = (bf16[512,512]{1,0:T(8,128)(2,1)S(1)}, bf16[512,512]{1,0:T(8,128)(2,1)}, u32[]{:S(2)}, u32[]{:S(2)}) collective-permute-start(bf16[512,512]{1,0:T(8,128)(2,1)S(1)} %collective-permute-done.2.refs_2_), channel_id=1, source_target_pairs={{0,72},{8,0},{64,8},{72,64},{1,73},{9,1},{65,9},{73,65},{2,74},{10... | collective-permute-start | bytes 1572872 | tf_op jit(solution)/shard_map/ppermute | solution.py:174
  25.8 1.2 collective-permute-start.6
  27.8 1.6 %collective-permute-start.4 = (bf16[256,512]{1,0:T(8,128)(2,1)}, bf16[256,512]{1,0:T(8,128)(2,1)S(1)}, u32[]{:S(2)}, u32[]{:S(2)}) collective-permute-start(bf16[256,512]{1,0:T(8,128)(2,1)} %slice.21), channel_id=1, source_target_pairs={{0,6},{2,0},{4,2},{6,4},{1,7},{3,1},{5,3},{7,5},{8,14},{10,8},{12,... | collective-permute-start | bytes 786440 | tf_op jit(solution)/shard_map/ppermute | solution.py:198
  30.9 2.7 %collective-permute-done.4.refs_4_ = bf16[256,512]{1,0:T(8,128)(2,1)S(1)} collective-permute-done((bf16[256,512]{1,0:T(8,128)(2,1)}, bf16[256,512]{1,0:T(8,128)(2,1)S(1)}, u32[]{:S(2)}, u32[]{:S(2)}) %collective-permute-start.4) | collective-permute-done | bytes 262176 | tf_op jit(solution)/shard_map/ppermute | solution.py:198
  33.6 2.0 %collective-permute-start.10 = (bf16[256,512]{1,0:T(8,128)(2,1)S(1)}, bf16[256,512]{1,0:T(8,128)(2,1)}, u32[]{:S(2)}, u32[]{:S(2)}) collective-permute-start(bf16[256,512]{1,0:T(8,128)(2,1)S(1)} %collective-permute-done.4.refs_4_), channel_id=1, source_target_pairs={{0,72},{8,0},{64,8},{72,64},{1,73},{9,1},{65,9},{73,65},{2,74},{10... | collective-permute-start | bytes 786440 | tf_op jit(solution)/shard_map/ppermute | solution.py:174
  35.9 2.1 %collective-permute-done.3.refs_3_ = bf16[256,512]{1,0:T(8,128)(2,1)} collective-permute-done((bf16[256,512]{1,0:T(8,128)(2,1)}, bf16[256,512]{1,0:T(8,128)(2,1)}, u32[]{:S(2)}, u32[]{:S(2)}) %collective-permute-start.3) | collective-permute-done | bytes 262176 | tf_op jit(solution)/shard_map/ppermute | solution.py:197
  38.1 4.9 %collective-permute-start.8 = (s32[2,3,24]{2,1,0:T(4,128)S(1)}, s32[2,3,24]{2,1,0:T(4,128)S(1)}, u32[]{:S(2)}, u32[]{:S(2)}) collective-permute-start(s32[2,3,24]{2,1,0:T(4,128)S(1)} %pad_add_fusion), channel_id=1, source_target_pairs={{0,1},{1,0},{2,3},{3,2},{4,5},{5,4},{6,7},{7,6},{8,9},{9,8},{10,11... | collective-permute-start | bytes 1736 | tf_op jit(solution)/shard_map/ppermute | solution.py:178
  43.1 1.2 collective-permute-start.11
  45.3 1.9 %collective-permute-start.24 = (bf16[1536,512]{1,0:T(8,128)(2,1)}, bf16[1536,512]{1,0:T(8,128)(2,1)}, u32[]{:S(2)}, u32[]{:S(2)}) collective-permute-start(bf16[1536,512]{1,0:T(8,128)(2,1)} %collective-permute-done.23.refs_24_), channel_id=1, source_target_pairs={{0,1},{1,0},{2,3},{3,2},{4,5},{5,4},{6,7},{7,6},{8,9},{9,8},{10,11... | collective-permute-start | bytes 4718600 | tf_op jit(solution)/shard_map/ppermute | solution.py:178
  47.2 3.0 %collective-permute-start.15 = (bf16[256,512]{1,0:T(8,128)(2,1)S(1)}, bf16[256,512]{1,0:T(8,128)(2,1)S(1)}, u32[]{:S(2)}, u32[]{:S(2)}) collective-permute-start(bf16[256,512]{1,0:T(8,128)(2,1)S(1)} %collective-permute-done.4.refs_4_), channel_id=1, source_target_pairs={{0,1},{1,0},{2,3},{3,2},{4,5},{5,4},{6,7},{7,6},{8,9},{9,8},{10,11... | collective-permute-start | bytes 786440 | tf_op jit(solution)/shard_map/ppermute | solution.py:178
  50.3 1.6 %collective-permute-done.19.refs_18_ = bf16[256,512]{1,0:T(8,128)(2,1)S(1)} collective-permute-done((bf16[256,512]{1,0:T(8,128)(2,1)}, bf16[256,512]{1,0:T(8,128)(2,1)S(1)}, u32[]{:S(2)}, u32[]{:S(2)}) %collective-permute-start.19) | collective-permute-done | bytes 262176 | tf_op jit(solution)/shard_map/ppermute | solution.py:178
  54.4 1.1 collective-permute-done.13.refs_12_
  56.8 1.8 %collective-permute-done.18.refs_17_ = bf16[512,512]{1,0:T(8,128)(2,1)S(1)} collective-permute-done((bf16[512,512]{1,0:T(8,128)(2,1)}, bf16[512,512]{1,0:T(8,128)(2,1)S(1)}, u32[]{:S(2)}, u32[]{:S(2)}) %collective-permute-start.18) | collective-permute-done | bytes 524320 | tf_op jit(solution)/shard_map/ppermute | solution.py:178
  60.1 19.2 %couplings.1 = bf16[4,16,32,512]{3,2,1,0:T(8,128)(2,1)} custom-call(s32[120]{0:T(128)} %broadcast_add_fusion.table, s32[4]{0:T(128)} %copy-done.13, s32[16]{0:T(128)} %dims.1, bf16[512,512]{1,0:T(8,128)(2,1)} %bitcast.35, bf16[512,512]{1,0:T(8,128)(2,1)} %copy-done.3, bf16[512,512]{1,0:T(8,128)(2,1)} %copy-done.2, ...), custom_call_target="tpu_custom_call" | custom-call | tf_op jit(solution)/shard_map/couplings/pallas_call | solution.py:236
  79.3 32.5 %all_to_all.10 = bf16[32,2,32,512]{3,2,1,0:T(8,128)(2,1)S(1)} all-to-all(bf16[32,2,32,512]{3,2,1,0:T(8,128)(2,1)} %bitcast.27), channel_id=1, replica_groups=mesh['x_hi'=2,'y_hi'=2,'y_lo'=2,'x_lo'=2,'z'=4,'core'=2] {'x_hi','y_lo',..., dimensions={0} | all-to-all | bytes 4194304 | tf_op jit(solution)/shard_map/all_to_all | solution.py:255
  112.2 19.2 %all_to_all.11 = bf16[16,32,512]{2,1,0:T(8,128)(2,1)S(1)} all-to-all(bf16[16,32,512]{2,1,0:T(8,128)(2,1)S(1)} %bitcast.33), channel_id=1, replica_groups=mesh['x_hi'=2,'y_hi'=2,'y_lo'=2,'x_lo'=2,'z'=4,'core'=2] {'x_hi','y_hi',..., dimensions={0} | all-to-all | bytes 1048576 | tf_op jit(solution)/shard_map/all_to_all | solution.py:258
  (89 shorter events, 12.2 us)
Async XLA Ops:
  0.7 5.2 %collective-permute-start = (s32[3,24]{1,0:T(4,128)S(1)}, s32[3,24]{1,0:T(4,128)S(1)}, u32[]{:S(2)}, u32[]{:S(2)}) collective-permute-start(s32[3,24]{1,0:T(4,128)S(1)} %get-tuple-element.41), channel_id=1, source_target_pairs={{0,32},{32,0},{1,33},{33,1},{2,34},{34,2},{3,35},{35,3},{4,36},{36... | collective-permute-start | bytes 872 | tf_op jit(solution)/shard_map/ppermute | solution.py:191
  8.5 36.8 %collective-permute-start.23 = (bf16[1536,512]{1,0:T(8,128)(2,1)}, bf16[1536,512]{1,0:T(8,128)(2,1)}, u32[]{:S(2)}, u32[]{:S(2)}) collective-permute-start(bf16[1536,512]{1,0:T(8,128)(2,1)} %pad_maximum_fusion), channel_id=1, source_target_pairs={{0,32},{32,0},{1,33},{33,1},{2,34},{34,2},{3,35},{35,3},{4,36},{36... | collective-permute-start | bytes 4718600 | tf_op jit(solution)/shard_map/ppermute | solution.py:193
  9.7 12.9 %collective-permute-start.2 = (bf16[512,512]{1,0:T(8,128)(2,1)S(1)}, bf16[512,512]{1,0:T(8,128)(2,1)S(1)}, u32[]{:S(2)}, u32[]{:S(2)}) collective-permute-start(bf16[512,512]{1,0:T(8,128)(2,1)S(1)} %bitcast.36), channel_id=1, source_target_pairs={{0,6},{2,0},{4,2},{6,4},{1,7},{3,1},{5,3},{7,5},{8,14},{10,8},{12,... | collective-permute-start | bytes 1572872 | tf_op jit(solution)/shard_map/ppermute | solution.py:195
  13.5 12.3 %collective-permute-start.1 = (bf16[512,512]{1,0:T(8,128)(2,1)S(1)}, bf16[512,512]{1,0:T(8,128)(2,1)S(1)}, u32[]{:S(2)}, u32[]{:S(2)}) collective-permute-start(bf16[512,512]{1,0:T(8,128)(2,1)S(1)} %bitcast.37), channel_id=1, source_target_pairs={{0,2},{2,4},{4,6},{6,0},{1,3},{3,5},{5,7},{7,1},{8,10},{10,12},{12... | collective-permute-start | bytes 1572872 | tf_op jit(solution)/shard_map/ppermute | solution.py:194
  13.5 16.6 %collective-permute-start.5 = (bf16[512,512]{1,0:T(8,128)(2,1)S(1)}, bf16[512,512]{1,0:T(8,128)(2,1)S(1)}, u32[]{:S(2)}, u32[]{:S(2)}) collective-permute-start(bf16[512,512]{1,0:T(8,128)(2,1)S(1)} %bitcast.38), channel_id=1, source_target_pairs={{0,8},{8,64},{64,72},{72,0},{1,9},{9,65},{65,73},{73,1},{2,10},{10... | collective-permute-start | bytes 1572872 | tf_op jit(solution)/shard_map/ppermute | solution.py:174
  22.6 15.5 %collective-permute-start.7 = (bf16[512,512]{1,0:T(8,128)(2,1)S(1)}, bf16[512,512]{1,0:T(8,128)(2,1)}, u32[]{:S(2)}, u32[]{:S(2)}) collective-permute-start(bf16[512,512]{1,0:T(8,128)(2,1)S(1)} %collective-permute-done.2.refs_2_), channel_id=1, source_target_pairs={{0,72},{8,0},{64,8},{72,64},{1,73},{9,1},{65,9},{73,65},{2,74},{10... | collective-permute-start | bytes 1572872 | tf_op jit(solution)/shard_map/ppermute | solution.py:174
  25.8 12.3 %collective-permute-start.6 = (bf16[512,512]{1,0:T(8,128)(2,1)S(1)}, bf16[512,512]{1,0:T(8,128)(2,1)}, u32[]{:S(2)}, u32[]{:S(2)}) collective-permute-start(bf16[512,512]{1,0:T(8,128)(2,1)S(1)} %collective-permute-done.1.refs_1_), channel_id=1, source_target_pairs={{0,8},{8,64},{64,72},{72,0},{1,9},{9,65},{65,73},{73,1},{2,10},{10... | collective-permute-start | bytes 1572872 | tf_op jit(solution)/shard_map/ppermute | solution.py:174
  27.8 5.8 %collective-permute-start.4 = (bf16[256,512]{1,0:T(8,128)(2,1)}, bf16[256,512]{1,0:T(8,128)(2,1)S(1)}, u32[]{:S(2)}, u32[]{:S(2)}) collective-permute-start(bf16[256,512]{1,0:T(8,128)(2,1)} %slice.21), channel_id=1, source_target_pairs={{0,6},{2,0},{4,2},{6,4},{1,7},{3,1},{5,3},{7,5},{8,14},{10,8},{12,... | collective-permute-start | bytes 786440 | tf_op jit(solution)/shard_map/ppermute | solution.py:198
  30.9 7.0 %collective-permute-start.3 = (bf16[256,512]{1,0:T(8,128)(2,1)}, bf16[256,512]{1,0:T(8,128)(2,1)}, u32[]{:S(2)}, u32[]{:S(2)}) collective-permute-start(bf16[256,512]{1,0:T(8,128)(2,1)} %slice.20), channel_id=1, source_target_pairs={{0,2},{2,4},{4,6},{6,0},{1,3},{3,5},{5,7},{7,1},{8,10},{10,12},{12... | collective-permute-start | bytes 786440 | tf_op jit(solution)/shard_map/ppermute | solution.py:197
  33.6 9.5 %collective-permute-start.10 = (bf16[256,512]{1,0:T(8,128)(2,1)S(1)}, bf16[256,512]{1,0:T(8,128)(2,1)}, u32[]{:S(2)}, u32[]{:S(2)}) collective-permute-start(bf16[256,512]{1,0:T(8,128)(2,1)S(1)} %collective-permute-done.4.refs_4_), channel_id=1, source_target_pairs={{0,72},{8,0},{64,8},{72,64},{1,73},{9,1},{65,9},{73,65},{2,74},{10... | collective-permute-start | bytes 786440 | tf_op jit(solution)/shard_map/ppermute | solution.py:174
  38.0 9.2 %collective-permute-start.9 = (bf16[256,512]{1,0:T(8,128)(2,1)}, bf16[256,512]{1,0:T(8,128)(2,1)}, u32[]{:S(2)}, u32[]{:S(2)}) collective-permute-start(bf16[256,512]{1,0:T(8,128)(2,1)} %collective-permute-done.3.refs_3_), channel_id=1, source_target_pairs={{0,8},{8,64},{64,72},{72,0},{1,9},{9,65},{65,73},{73,1},{2,10},{10... | collective-permute-start | bytes 786440 | tf_op jit(solution)/shard_map/ppermute | solution.py:174
  38.1 6.2 %collective-permute-start.8 = (s32[2,3,24]{2,1,0:T(4,128)S(1)}, s32[2,3,24]{2,1,0:T(4,128)S(1)}, u32[]{:S(2)}, u32[]{:S(2)}) collective-permute-start(s32[2,3,24]{2,1,0:T(4,128)S(1)} %pad_add_fusion), channel_id=1, source_target_pairs={{0,1},{1,0},{2,3},{3,2},{4,5},{5,4},{6,7},{7,6},{8,9},{9,8},{10,11... | collective-permute-start | bytes 1736 | tf_op jit(solution)/shard_map/ppermute | solution.py:178
  43.0 9.3 %collective-permute-start.14 = (bf16[256,512]{1,0:T(8,128)(2,1)}, bf16[256,512]{1,0:T(8,128)(2,1)}, u32[]{:S(2)}, u32[]{:S(2)}) collective-permute-start(bf16[256,512]{1,0:T(8,128)(2,1)} %collective-permute-done.3.refs_3_), channel_id=1, source_target_pairs={{0,1},{1,0},{2,3},{3,2},{4,5},{5,4},{6,7},{7,6},{8,9},{9,8},{10,11... | collective-permute-start | bytes 786440 | tf_op jit(solution)/shard_map/ppermute | solution.py:178
  43.1 9.7 %collective-permute-start.11 = (bf16[512,512]{1,0:T(8,128)(2,1)S(1)}, bf16[512,512]{1,0:T(8,128)(2,1)}, u32[]{:S(2)}, u32[]{:S(2)}) collective-permute-start(bf16[512,512]{1,0:T(8,128)(2,1)S(1)} %bitcast.39), channel_id=1, source_target_pairs={{0,1},{1,0},{2,3},{3,2},{4,5},{5,4},{6,7},{7,6},{8,9},{9,8},{10,11... | collective-permute-start | bytes 1572872 | tf_op jit(solution)/shard_map/ppermute | solution.py:178
  44.3 5.9 %collective-permute-start.20 = (bf16[256,512]{1,0:T(8,128)(2,1)}, bf16[256,512]{1,0:T(8,128)(2,1)}, u32[]{:S(2)}, u32[]{:S(2)}) collective-permute-start(bf16[256,512]{1,0:T(8,128)(2,1)} %collective-permute-done.10.refs_9_), channel_id=1, source_target_pairs={{0,1},{1,0},{2,3},{3,2},{4,5},{5,4},{6,7},{7,6},{8,9},{9,8},{10,11... | collective-permute-start | bytes 786440 | tf_op jit(solution)/shard_map/ppermute | solution.py:178
  45.3 13.8 %collective-permute-start.24 = (bf16[1536,512]{1,0:T(8,128)(2,1)}, bf16[1536,512]{1,0:T(8,128)(2,1)}, u32[]{:S(2)}, u32[]{:S(2)}) collective-permute-start(bf16[1536,512]{1,0:T(8,128)(2,1)} %collective-permute-done.23.refs_24_), channel_id=1, source_target_pairs={{0,1},{1,0},{2,3},{3,2},{4,5},{5,4},{6,7},{7,6},{8,9},{9,8},{10,11... | collective-permute-start | bytes 4718600 | tf_op jit(solution)/shard_map/ppermute | solution.py:178
  47.2 5.3 %collective-permute-start.15 = (bf16[256,512]{1,0:T(8,128)(2,1)S(1)}, bf16[256,512]{1,0:T(8,128)(2,1)S(1)}, u32[]{:S(2)}, u32[]{:S(2)}) collective-permute-start(bf16[256,512]{1,0:T(8,128)(2,1)S(1)} %collective-permute-done.4.refs_4_), channel_id=1, source_target_pairs={{0,1},{1,0},{2,3},{3,2},{4,5},{5,4},{6,7},{7,6},{8,9},{9,8},{10,11... | collective-permute-start | bytes 786440 | tf_op jit(solution)/shard_map/ppermute | solution.py:178
  52.0 2.0 %collective-permute-start.12 = (bf16[512,512]{1,0:T(8,128)(2,1)S(1)}, bf16[512,512]{1,0:T(8,128)(2,1)}, u32[]{:S(2)}, u32[]{:S(2)}) collective-permute-start(bf16[512,512]{1,0:T(8,128)(2,1)S(1)} %collective-permute-done.1.refs_1_), channel_id=1, source_target_pairs={{0,1},{1,0},{2,3},{3,2},{4,5},{5,4},{6,7},{7,6},{8,9},{9,8},{10,11... | collective-permute-start | bytes 1572872 | tf_op jit(solution)/shard_map/ppermute | solution.py:178
  52.3 3.2 %collective-permute-start.13 = (bf16[512,512]{1,0:T(8,128)(2,1)S(1)}, bf16[512,512]{1,0:T(8,128)(2,1)}, u32[]{:S(2)}, u32[]{:S(2)}) collective-permute-start(bf16[512,512]{1,0:T(8,128)(2,1)S(1)} %collective-permute-done.2.refs_2_), channel_id=1, source_target_pairs={{0,1},{1,0},{2,3},{3,2},{4,5},{5,4},{6,7},{7,6},{8,9},{9,8},{10,11... | collective-permute-start | bytes 1572872 | tf_op jit(solution)/shard_map/ppermute | solution.py:178
  52.5 3.4 %collective-permute-start.16 = (bf16[512,512]{1,0:T(8,128)(2,1)}, bf16[512,512]{1,0:T(8,128)(2,1)}, u32[]{:S(2)}, u32[]{:S(2)}) collective-permute-start(bf16[512,512]{1,0:T(8,128)(2,1)} %copy-done.5), channel_id=1, source_target_pairs={{0,1},{1,0},{2,3},{3,2},{4,5},{5,4},{6,7},{7,6},{8,9},{9,8},{10,11... | collective-permute-start | bytes 1572872 | tf_op jit(solution)/shard_map/ppermute | solution.py:178
  52.8 6.3 %collective-permute-start.21 = (bf16[1024,512]{1,0:T(8,128)(2,1)S(1)}, bf16[1024,512]{1,0:T(8,128)(2,1)}, u32[]{:S(2)}, u32[]{:S(2)}) collective-permute-start(bf16[1024,512]{1,0:T(8,128)(2,1)S(1)} %bitcast.30), channel_id=1, source_target_pairs={{0,1},{1,0},{2,3},{3,2},{4,5},{5,4},{6,7},{7,6},{8,9},{9,8},{10,11... | collective-permute-start | bytes 3145736 | tf_op jit(solution)/shard_map/ppermute | solution.py:178
  54.0 5.1 %collective-permute-start.17 = (bf16[512,512]{1,0:T(8,128)(2,1)}, bf16[512,512]{1,0:T(8,128)(2,1)S(1)}, u32[]{:S(2)}, u32[]{:S(2)}) collective-permute-start(bf16[512,512]{1,0:T(8,128)(2,1)} %collective-permute-done.6.refs_6_), channel_id=1, source_target_pairs={{0,1},{1,0},{2,3},{3,2},{4,5},{5,4},{6,7},{7,6},{8,9},{9,8},{10,11... | collective-permute-start | bytes 1572872 | tf_op jit(solution)/shard_map/ppermute | solution.py:178
  55.5 3.1 %collective-permute-start.18 = (bf16[512,512]{1,0:T(8,128)(2,1)}, bf16[512,512]{1,0:T(8,128)(2,1)S(1)}, u32[]{:S(2)}, u32[]{:S(2)}) collective-permute-start(bf16[512,512]{1,0:T(8,128)(2,1)} %collective-permute-done.7.refs_7_), channel_id=1, source_target_pairs={{0,1},{1,0},{2,3},{3,2},{4,5},{5,4},{6,7},{7,6},{8,9},{9,8},{10,11... | collective-permute-start | bytes 1572872 | tf_op jit(solution)/shard_map/ppermute | solution.py:178
  55.9 3.2 %collective-permute-start.22 = (bf16[512,512]{1,0:T(8,128)(2,1)S(1)}, bf16[512,512]{1,0:T(8,128)(2,1)S(1)}, u32[]{:S(2)}, u32[]{:S(2)}) collective-permute-start(bf16[512,512]{1,0:T(8,128)(2,1)S(1)} %get-tuple-element.30.refs_21_), channel_id=1, source_target_pairs={{0,1},{1,0},{2,3},{3,2},{4,5},{5,4},{6,7},{7,6},{8,9},{9,8},{10,11... | collective-permute-start | bytes 1572872 | tf_op jit(solution)/shard_map/ppermute | solution.py:178
  (15 other events, 186.0 us)

commit v8 on v7

--- a/solution.py
+++ b/solution.py
@@ -201,8 +201,9 @@
     corner_low = along_x(across_low, UP)
     corner_high = along_x(across_high, DOWN)
     early = (block, before, after, across_low, across_high, side, side_before, side_after)
-    held = lax.optimization_barrier(early + (near_right, near_rows))
-    mate_early = [to_mate(part) for part in held]
+    first = tuple(to_mate(part) for part in (block, near_right, near_rows))
+    held = lax.optimization_barrier(early + first)
+    mate_early = [held[8]] + [to_mate(part) for part in held[1:8]] + list(held[9:])
     mate_late = [to_mate(part) for part in (corner_low, corner_high, far)]
     metas = jnp.stack([meta, far_meta])
     metas, _ = lax.optimization_barrier((metas, held[6]))

time: 133 us -> 135 us (1.015)
  blocking collectives: 51.7 us -> 48.7 us
  Pallas kernels: 19.2 us -> 22 us
  waiting for transfers between devices: 19.6 us -> 21.7 us
    ppermute x1, waiting for transfers between devices: 7.9 us -> 0.37 us  [share(): after = lax.ppermute(block, 'z', DOWN)]
    ppermute x1, waiting for transfers between devices: 0.76 us -> 6.56 us  [share(): before = lax.ppermute(block, 'z', UP)]
    ppermute x1, waiting for transfers between devices: 2.09 us -> 7 us  [share(): across_low = lax.ppermute(before[:half], 'z', UP)]
    pallas_call x1, Pallas kernels: 19.2 us -> 22 us  [body(): pl.pallas_call(couplings_kernel, out_shape=jax.ShapeDtypeStruct((LEVELS,...]
    ppermute x1, waiting for transfers between devices: 2.65 us -> 0.01 us  [share(): across_high = lax.ppermute(after[half:], 'z', DOWN)]
    all_to_all x1, blocking collectives: 32.5 us -> 30 us  [body(): lax.all_to_all(partial.reshape(-1, 2, SLICE, width), REDUCE, 0, 0, tiled=...]
    ppermute x5, starting transfers between devices: 7.07 us -> 4.72 us  [along_x(): return lax.ppermute(part, ('x_hi', 'x_lo'), steps)]
    ppermute x1, starting transfers between devices: 1.61 us -> 3.37 us  [share(): across_high = lax.ppermute(after[half:], 'z', DOWN)]
  transfers between devices with their start and end apart: 25 -> 25, of which waited for: 10 -> 9; matrix products, arithmetic and copies ran while one was open for 3% -> 4% of each run, Pallas kernels for 0% -> 0%
where the time goes in v8:
time: 135 us; the launch traced here: 136 us
  blocking collectives  48.7 us (36%)
  starting transfers between devices  31.2 us (23%)
  Pallas kernels  22 us (16%)
  waiting for transfers between devices  21.7 us (16%)
  local copies, waits for them, and re-layouts  7.94 us (6%)
  other arithmetic  3.7 us (3%)
    all_to_all x1, blocking collectives, body(): lax.all_to_all(partial.reshape(-1, 2, SLICE, width), REDUCE, 0, 0, tiled=...  30 us
    pallas_call x1, Pallas kernels, body(): pl.pallas_call(couplings_kernel, out_shape=jax.ShapeDtypeStruct((LEVELS,...  22 us
    all_to_all x1, blocking collectives, body(): whole = lax.all_to_all(spread, SPREAD, 0, 0, tiled=True)  18.7 us
    ppermute x14, starting transfers between devices, to_mate(): return lax.ppermute(part, 'core', SWAP)  14.8 us
    ppermute x1, waiting for transfers between devices, share(): across_low = lax.ppermute(before[:half], 'z', UP)  7 us
    ppermute x1, waiting for transfers between devices, share(): before = lax.ppermute(block, 'z', UP)  6.56 us
    ppermute x14, waiting for transfers between devices, to_mate(): return lax.ppermute(part, 'core', SWAP)  5.48 us
    ppermute x5, starting transfers between devices, along_x(): return lax.ppermute(part, ('x_hi', 'x_lo'), steps)  4.72 us
  transfers between devices with their start and end apart: 25, of which 9 were waited for; matrix products, arithmetic and copies ran while one was open for 4% of the time, Pallas kernels for 0%

profile of v8, /device:TPU:1, one launch (start us, length us, event | category | flops | bytes accessed | tf_op | source)
XLA Modules:
  0.0 135.5 jit_solution(11358341637751298780)
XLA Ops:
  0.0 1.4 %collective-permute-start.8 = (bf16[512,512]{1,0:T(8,128)(2,1)}, bf16[512,512]{1,0:T(8,128)(2,1)}, u32[]{:S(2)}, u32[]{:S(2)}) collective-permute-start(bf16[512,512]{1,0:T(8,128)(2,1)} %bitcast.35), channel_id=1, source_target_pairs={{0,1},{1,0},{2,3},{3,2},{4,5},{5,4},{6,7},{7,6},{8,9},{9,8},{10,11... | collective-permute-start | bytes 1572872 | tf_op jit(solution)/shard_map/ppermute | solution.py:178
  1.4 1.3 collective-permute-start.5
  2.7 3.8 %collective-permute-start.2 = (bf16[512,512]{1,0:T(8,128)(2,1)}, bf16[512,512]{1,0:T(8,128)(2,1)S(1)}, u32[]{:S(2)}, u32[]{:S(2)}) collective-permute-start(bf16[512,512]{1,0:T(8,128)(2,1)} %bitcast.37), channel_id=1, source_target_pairs={{0,6},{2,0},{4,2},{6,4},{1,7},{3,1},{5,3},{7,5},{8,14},{10,8},{12,... | collective-permute-start | bytes 1572872 | tf_op jit(solution)/shard_map/ppermute | solution.py:195
  7.2 3.0 %collective-permute-start = (s32[3,24]{1,0:T(4,128)S(1)}, s32[3,24]{1,0:T(4,128)S(1)}, u32[]{:S(2)}, u32[]{:S(2)}) collective-permute-start(s32[3,24]{1,0:T(4,128)S(1)} %get-tuple-element.41), channel_id=1, source_target_pairs={{0,32},{32,0},{1,33},{33,1},{2,34},{34,2},{3,35},{35,3},{4,36},{36... | collective-permute-start | bytes 872 | tf_op jit(solution)/shard_map/ppermute | solution.py:191
  10.2 1.3 copy.12
  11.6 1.3 copy-done
  12.9 1.3 pad_maximum_fusion
  14.1 1.6 %collective-permute-start.23 = (bf16[1536,512]{1,0:T(8,128)(2,1)}, bf16[1536,512]{1,0:T(8,128)(2,1)}, u32[]{:S(2)}, u32[]{:S(2)}) collective-permute-start(bf16[1536,512]{1,0:T(8,128)(2,1)} %pad_maximum_fusion), channel_id=1, source_target_pairs={{0,32},{32,0},{1,33},{33,1},{2,34},{34,2},{3,35},{35,3},{4,36},{36... | collective-permute-start | bytes 4718600 | tf_op jit(solution)/shard_map/ppermute | solution.py:193
  15.8 1.7 %collective-permute-start.10 = (bf16[512,512]{1,0:T(8,128)(2,1)S(1)}, bf16[512,512]{1,0:T(8,128)(2,1)S(1)}, u32[]{:S(2)}, u32[]{:S(2)}) collective-permute-start(bf16[512,512]{1,0:T(8,128)(2,1)S(1)} %get-tuple-element.38.refs_21_), channel_id=1, source_target_pairs={{0,1},{1,0},{2,3},{3,2},{4,5},{5,4},{6,7},{7,6},{8,9},{9,8},{10,11... | collective-permute-start | bytes 1572872 | tf_op jit(solution)/shard_map/ppermute | solution.py:178
  17.8 1.1 collective-permute-start.9
  19.0 3.4 %collective-permute-start.4 = (bf16[256,512]{1,0:T(8,128)(2,1)S(1)}, bf16[256,512]{1,0:T(8,128)(2,1)S(1)}, u32[]{:S(2)}, u32[]{:S(2)}) collective-permute-start(bf16[256,512]{1,0:T(8,128)(2,1)S(1)} %slice.21), channel_id=1, source_target_pairs={{0,6},{2,0},{4,2},{6,4},{1,7},{3,1},{5,3},{7,5},{8,14},{10,8},{12,... | collective-permute-start | bytes 786440 | tf_op jit(solution)/shard_map/ppermute | solution.py:198
  22.3 6.6 %collective-permute-done.1.refs_1_ = bf16[512,512]{1,0:T(8,128)(2,1)S(1)} collective-permute-done((bf16[512,512]{1,0:T(8,128)(2,1)S(1)}, bf16[512,512]{1,0:T(8,128)(2,1)S(1)}, u32[]{:S(2)}, u32[]{:S(2)}) %collective-permute-start.1) | collective-permute-done | bytes 524320 | tf_op jit(solution)/shard_map/ppermute | solution.py:194
  32.0 7.0 %collective-permute-done.3.refs_3_ = bf16[256,512]{1,0:T(8,128)(2,1)} collective-permute-done((bf16[256,512]{1,0:T(8,128)(2,1)}, bf16[256,512]{1,0:T(8,128)(2,1)}, u32[]{:S(2)}, u32[]{:S(2)}) %collective-permute-start.3) | collective-permute-done | bytes 262176 | tf_op jit(solution)/shard_map/ppermute | solution.py:197
  39.0 1.9 %collective-permute-start.13 = (bf16[256,512]{1,0:T(8,128)(2,1)S(1)}, bf16[256,512]{1,0:T(8,128)(2,1)}, u32[]{:S(2)}, u32[]{:S(2)}) collective-permute-start(bf16[256,512]{1,0:T(8,128)(2,1)S(1)} %collective-permute-done.4.refs_4_), channel_id=1, source_target_pairs={{0,72},{8,0},{64,8},{72,64},{1,73},{9,1},{65,9},{73,65},{2,74},{10... | collective-permute-start | bytes 786440 | tf_op jit(solution)/shard_map/ppermute | solution.py:174
  42.1 4.1 %collective-permute-start.11 = (s32[2,3,24]{2,1,0:T(4,128)S(1)}, s32[2,3,24]{2,1,0:T(4,128)S(1)}, u32[]{:S(2)}, u32[]{:S(2)}) collective-permute-start(s32[2,3,24]{2,1,0:T(4,128)S(1)} %pad_add_fusion), channel_id=1, source_target_pairs={{0,1},{1,0},{2,3},{3,2},{4,5},{5,4},{6,7},{7,6},{8,9},{9,8},{10,11... | collective-permute-start | bytes 1736 | tf_op jit(solution)/shard_map/ppermute | solution.py:178
  46.2 3.0 %collective-permute-start.14 = (bf16[512,512]{1,0:T(8,128)(2,1)S(1)}, bf16[512,512]{1,0:T(8,128)(2,1)}, u32[]{:S(2)}, u32[]{:S(2)}) collective-permute-start(bf16[512,512]{1,0:T(8,128)(2,1)S(1)} %collective-permute-done.1.refs_1_), channel_id=1, source_target_pairs={{0,1},{1,0},{2,3},{3,2},{4,5},{5,4},{6,7},{7,6},{8,9},{9,8},{10,11... | collective-permute-start | bytes 1572872 | tf_op jit(solution)/shard_map/ppermute | solution.py:178
  49.6 1.4 %collective-permute-done.23.refs_24_ = bf16[1536,512]{1,0:T(8,128)(2,1)} collective-permute-done((bf16[1536,512]{1,0:T(8,128)(2,1)}, bf16[1536,512]{1,0:T(8,128)(2,1)}, u32[]{:S(2)}, u32[]{:S(2)}) %collective-permute-start.23) | collective-permute-done | bytes 1572896 | tf_op jit(solution)/shard_map/ppermute | solution.py:193
  51.0 1.7 %collective-permute-start.24 = (bf16[1536,512]{1,0:T(8,128)(2,1)}, bf16[1536,512]{1,0:T(8,128)(2,1)S(1)}, u32[]{:S(2)}, u32[]{:S(2)}) collective-permute-start(bf16[1536,512]{1,0:T(8,128)(2,1)} %collective-permute-done.23.refs_24_), channel_id=1, source_target_pairs={{0,1},{1,0},{2,3},{3,2},{4,5},{5,4},{6,7},{7,6},{8,9},{9,8},{10,11... | collective-permute-start | bytes 4718600 | tf_op jit(solution)/shard_map/ppermute | solution.py:178
  53.9 3.0 %collective-permute-done.21.refs_18_ = bf16[256,512]{1,0:T(8,128)(2,1)} collective-permute-done((bf16[256,512]{1,0:T(8,128)(2,1)}, bf16[256,512]{1,0:T(8,128)(2,1)}, u32[]{:S(2)}, u32[]{:S(2)}) %collective-permute-start.21) | collective-permute-done | bytes 262176 | tf_op jit(solution)/shard_map/ppermute | solution.py:178
  58.6 1.7 %collective-permute-done.15.refs_12_ = bf16[512,512]{1,0:T(8,128)(2,1)S(1)} collective-permute-done((bf16[512,512]{1,0:T(8,128)(2,1)S(1)}, bf16[512,512]{1,0:T(8,128)(2,1)S(1)}, u32[]{:S(2)}, u32[]{:S(2)}) %collective-permute-start.15) | collective-permute-done | bytes 524320 | tf_op jit(solution)/shard_map/ppermute | solution.py:178
  62.1 1.1 copy-done.2
  63.2 22.0 %couplings.1 = bf16[4,16,32,512]{3,2,1,0:T(8,128)(2,1)} custom-call(s32[120]{0:T(128)} %broadcast_add_fusion.table, s32[4]{0:T(128)} %copy-done.15, s32[16]{0:T(128)} %dims.1, bf16[512,512]{1,0:T(8,128)(2,1)} %bitcast.38, bf16[512,512]{1,0:T(8,128)(2,1)} %copy-done.4, bf16[512,512]{1,0:T(8,128)(2,1)} %copy-done.3, ...), custom_call_target="tpu_custom_call" | custom-call | tf_op jit(solution)/shard_map/couplings/pallas_call | solution.py:237
  85.2 30.0 %all_to_all.10 = bf16[32,2,32,512]{3,2,1,0:T(8,128)(2,1)S(1)} all-to-all(bf16[32,2,32,512]{3,2,1,0:T(8,128)(2,1)} %bitcast.27), channel_id=1, replica_groups=mesh['x_hi'=2,'y_hi'=2,'y_lo'=2,'x_lo'=2,'z'=4,'core'=2] {'x_hi','y_lo',..., dimensions={0} | all-to-all | bytes 4194304 | tf_op jit(solution)/shard_map/all_to_all | solution.py:256
  115.6 18.7 %all_to_all.11 = bf16[16,32,512]{2,1,0:T(8,128)(2,1)S(1)} all-to-all(bf16[16,32,512]{2,1,0:T(8,128)(2,1)S(1)} %bitcast.33), channel_id=1, replica_groups=mesh['x_hi'=2,'y_hi'=2,'y_lo'=2,'x_lo'=2,'z'=4,'core'=2] {'x_hi','y_hi',..., dimensions={0} | all-to-all | bytes 1048576 | tf_op jit(solution)/shard_map/all_to_all | solution.py:259
  (93 shorter events, 11.9 us)
Async XLA Ops:
  0.0 15.8 %collective-permute-start.8 = (bf16[512,512]{1,0:T(8,128)(2,1)}, bf16[512,512]{1,0:T(8,128)(2,1)}, u32[]{:S(2)}, u32[]{:S(2)}) collective-permute-start(bf16[512,512]{1,0:T(8,128)(2,1)} %bitcast.35), channel_id=1, source_target_pairs={{0,1},{1,0},{2,3},{3,2},{4,5},{5,4},{6,7},{7,6},{8,9},{9,8},{10,11... | collective-permute-start | bytes 1572872 | tf_op jit(solution)/shard_map/ppermute | solution.py:178
  1.4 17.5 %collective-permute-start.5 = (bf16[512,512]{1,0:T(8,128)(2,1)}, bf16[512,512]{1,0:T(8,128)(2,1)}, u32[]{:S(2)}, u32[]{:S(2)}) collective-permute-start(bf16[512,512]{1,0:T(8,128)(2,1)} %bitcast.36), channel_id=1, source_target_pairs={{0,8},{8,64},{64,72},{72,0},{1,9},{9,65},{65,73},{73,1},{2,10},{10... | collective-permute-start | bytes 1572872 | tf_op jit(solution)/shard_map/ppermute | solution.py:174
  2.7 15.1 %collective-permute-start.2 = (bf16[512,512]{1,0:T(8,128)(2,1)}, bf16[512,512]{1,0:T(8,128)(2,1)S(1)}, u32[]{:S(2)}, u32[]{:S(2)}) collective-permute-start(bf16[512,512]{1,0:T(8,128)(2,1)} %bitcast.37), channel_id=1, source_target_pairs={{0,6},{2,0},{4,2},{6,4},{1,7},{3,1},{5,3},{7,5},{8,14},{10,8},{12,... | collective-permute-start | bytes 1572872 | tf_op jit(solution)/shard_map/ppermute | solution.py:195
  7.2 4.4 %collective-permute-start = (s32[3,24]{1,0:T(4,128)S(1)}, s32[3,24]{1,0:T(4,128)S(1)}, u32[]{:S(2)}, u32[]{:S(2)}) collective-permute-start(s32[3,24]{1,0:T(4,128)S(1)} %get-tuple-element.41), channel_id=1, source_target_pairs={{0,32},{32,0},{1,33},{33,1},{2,34},{34,2},{3,35},{35,3},{4,36},{36... | collective-permute-start | bytes 872 | tf_op jit(solution)/shard_map/ppermute | solution.py:191
  14.1 36.9 %collective-permute-start.23 = (bf16[1536,512]{1,0:T(8,128)(2,1)}, bf16[1536,512]{1,0:T(8,128)(2,1)}, u32[]{:S(2)}, u32[]{:S(2)}) collective-permute-start(bf16[1536,512]{1,0:T(8,128)(2,1)} %pad_maximum_fusion), channel_id=1, source_target_pairs={{0,32},{32,0},{1,33},{33,1},{2,34},{34,2},{3,35},{35,3},{4,36},{36... | collective-permute-start | bytes 4718600 | tf_op jit(solution)/shard_map/ppermute | solution.py:193
  15.8 13.1 %collective-permute-start.1 = (bf16[512,512]{1,0:T(8,128)(2,1)S(1)}, bf16[512,512]{1,0:T(8,128)(2,1)S(1)}, u32[]{:S(2)}, u32[]{:S(2)}) collective-permute-start(bf16[512,512]{1,0:T(8,128)(2,1)S(1)} %bitcast.39), channel_id=1, source_target_pairs={{0,2},{2,4},{4,6},{6,0},{1,3},{3,5},{5,7},{7,1},{8,10},{10,12},{12... | collective-permute-start | bytes 1572872 | tf_op jit(solution)/shard_map/ppermute | solution.py:194
  15.8 13.8 %collective-permute-start.10 = (bf16[512,512]{1,0:T(8,128)(2,1)S(1)}, bf16[512,512]{1,0:T(8,128)(2,1)S(1)}, u32[]{:S(2)}, u32[]{:S(2)}) collective-permute-start(bf16[512,512]{1,0:T(8,128)(2,1)S(1)} %get-tuple-element.38.refs_21_), channel_id=1, source_target_pairs={{0,1},{1,0},{2,3},{3,2},{4,5},{5,4},{6,7},{7,6},{8,9},{9,8},{10,11... | collective-permute-start | bytes 1572872 | tf_op jit(solution)/shard_map/ppermute | solution.py:178
  17.8 24.2 %collective-permute-start.9 = (bf16[1024,512]{1,0:T(8,128)(2,1)S(1)}, bf16[1024,512]{1,0:T(8,128)(2,1)}, u32[]{:S(2)}, u32[]{:S(2)}) collective-permute-start(bf16[1024,512]{1,0:T(8,128)(2,1)S(1)} %bitcast.30), channel_id=1, source_target_pairs={{0,1},{1,0},{2,3},{3,2},{4,5},{5,4},{6,7},{7,6},{8,9},{9,8},{10,11... | collective-permute-start | bytes 3145736 | tf_op jit(solution)/shard_map/ppermute | solution.py:178
  19.0 13.0 %collective-permute-start.4 = (bf16[256,512]{1,0:T(8,128)(2,1)S(1)}, bf16[256,512]{1,0:T(8,128)(2,1)S(1)}, u32[]{:S(2)}, u32[]{:S(2)}) collective-permute-start(bf16[256,512]{1,0:T(8,128)(2,1)S(1)} %slice.21), channel_id=1, source_target_pairs={{0,6},{2,0},{4,2},{6,4},{1,7},{3,1},{5,3},{7,5},{8,14},{10,8},{12,... | collective-permute-start | bytes 786440 | tf_op jit(solution)/shard_map/ppermute | solution.py:198
  28.9 12.2 %collective-permute-start.7 = (bf16[512,512]{1,0:T(8,128)(2,1)S(1)}, bf16[512,512]{1,0:T(8,128)(2,1)S(1)}, u32[]{:S(2)}, u32[]{:S(2)}) collective-permute-start(bf16[512,512]{1,0:T(8,128)(2,1)S(1)} %collective-permute-done.2.refs_2_), channel_id=1, source_target_pairs={{0,72},{8,0},{64,8},{72,64},{1,73},{9,1},{65,9},{73,65},{2,74},{10... | collective-permute-start | bytes 1572872 | tf_op jit(solution)/shard_map/ppermute | solution.py:174
  30.4 11.6 %collective-permute-start.6 = (bf16[512,512]{1,0:T(8,128)(2,1)S(1)}, bf16[512,512]{1,0:T(8,128)(2,1)S(1)}, u32[]{:S(2)}, u32[]{:S(2)}) collective-permute-start(bf16[512,512]{1,0:T(8,128)(2,1)S(1)} %collective-permute-done.1.refs_1_), channel_id=1, source_target_pairs={{0,8},{8,64},{64,72},{72,0},{1,9},{9,65},{65,73},{73,1},{2,10},{10... | collective-permute-start | bytes 1572872 | tf_op jit(solution)/shard_map/ppermute | solution.py:174
  31.9 7.0 %collective-permute-start.3 = (bf16[256,512]{1,0:T(8,128)(2,1)}, bf16[256,512]{1,0:T(8,128)(2,1)}, u32[]{:S(2)}, u32[]{:S(2)}) collective-permute-start(bf16[256,512]{1,0:T(8,128)(2,1)} %slice.20), channel_id=1, source_target_pairs={{0,2},{2,4},{4,6},{6,0},{1,3},{3,5},{5,7},{7,1},{8,10},{10,12},{12... | collective-permute-start | bytes 786440 | tf_op jit(solution)/shard_map/ppermute | solution.py:197
  39.0 7.3 %collective-permute-start.13 = (bf16[256,512]{1,0:T(8,128)(2,1)S(1)}, bf16[256,512]{1,0:T(8,128)(2,1)}, u32[]{:S(2)}, u32[]{:S(2)}) collective-permute-start(bf16[256,512]{1,0:T(8,128)(2,1)S(1)} %collective-permute-done.4.refs_4_), channel_id=1, source_target_pairs={{0,72},{8,0},{64,8},{72,64},{1,73},{9,1},{65,9},{73,65},{2,74},{10... | collective-permute-start | bytes 786440 | tf_op jit(solution)/shard_map/ppermute | solution.py:174
  41.1 11.9 %collective-permute-start.12 = (bf16[256,512]{1,0:T(8,128)(2,1)}, bf16[256,512]{1,0:T(8,128)(2,1)}, u32[]{:S(2)}, u32[]{:S(2)}) collective-permute-start(bf16[256,512]{1,0:T(8,128)(2,1)} %collective-permute-done.3.refs_3_), channel_id=1, source_target_pairs={{0,8},{8,64},{64,72},{72,0},{1,9},{9,65},{65,73},{73,1},{2,10},{10... | collective-permute-start | bytes 786440 | tf_op jit(solution)/shard_map/ppermute | solution.py:174
  42.1 7.2 %collective-permute-start.11 = (s32[2,3,24]{2,1,0:T(4,128)S(1)}, s32[2,3,24]{2,1,0:T(4,128)S(1)}, u32[]{:S(2)}, u32[]{:S(2)}) collective-permute-start(s32[2,3,24]{2,1,0:T(4,128)S(1)} %pad_add_fusion), channel_id=1, source_target_pairs={{0,1},{1,0},{2,3},{3,2},{4,5},{5,4},{6,7},{7,6},{8,9},{9,8},{10,11... | collective-permute-start | bytes 1736 | tf_op jit(solution)/shard_map/ppermute | solution.py:178
  46.2 11.1 %collective-permute-start.16 = (bf16[256,512]{1,0:T(8,128)(2,1)}, bf16[256,512]{1,0:T(8,128)(2,1)}, u32[]{:S(2)}, u32[]{:S(2)}) collective-permute-start(bf16[256,512]{1,0:T(8,128)(2,1)} %collective-permute-done.3.refs_3_), channel_id=1, source_target_pairs={{0,1},{1,0},{2,3},{3,2},{4,5},{5,4},{6,7},{7,6},{8,9},{9,8},{10,11... | collective-permute-start | bytes 786440 | tf_op jit(solution)/shard_map/ppermute | solution.py:178
  46.2 11.5 %collective-permute-start.14 = (bf16[512,512]{1,0:T(8,128)(2,1)S(1)}, bf16[512,512]{1,0:T(8,128)(2,1)}, u32[]{:S(2)}, u32[]{:S(2)}) collective-permute-start(bf16[512,512]{1,0:T(8,128)(2,1)S(1)} %collective-permute-done.1.refs_1_), channel_id=1, source_target_pairs={{0,1},{1,0},{2,3},{3,2},{4,5},{5,4},{6,7},{7,6},{8,9},{9,8},{10,11... | collective-permute-start | bytes 1572872 | tf_op jit(solution)/shard_map/ppermute | solution.py:178
  49.3 4.3 %collective-permute-start.22 = (bf16[256,512]{1,0:T(8,128)(2,1)}, bf16[256,512]{1,0:T(8,128)(2,1)}, u32[]{:S(2)}, u32[]{:S(2)}) collective-permute-start(bf16[256,512]{1,0:T(8,128)(2,1)} %collective-permute-done.13.refs_9_), channel_id=1, source_target_pairs={{0,1},{1,0},{2,3},{3,2},{4,5},{5,4},{6,7},{7,6},{8,9},{9,8},{10,11... | collective-permute-start | bytes 786440 | tf_op jit(solution)/shard_map/ppermute | solution.py:178
  51.0 10.0 %collective-permute-start.24 = (bf16[1536,512]{1,0:T(8,128)(2,1)}, bf16[1536,512]{1,0:T(8,128)(2,1)S(1)}, u32[]{:S(2)}, u32[]{:S(2)}) collective-permute-start(bf16[1536,512]{1,0:T(8,128)(2,1)} %collective-permute-done.23.refs_24_), channel_id=1, source_target_pairs={{0,1},{1,0},{2,3},{3,2},{4,5},{5,4},{6,7},{7,6},{8,9},{9,8},{10,11... | collective-permute-start | bytes 4718600 | tf_op jit(solution)/shard_map/ppermute | solution.py:178
  53.0 4.4 %collective-permute-start.17 = (bf16[256,512]{1,0:T(8,128)(2,1)S(1)}, bf16[256,512]{1,0:T(8,128)(2,1)}, u32[]{:S(2)}, u32[]{:S(2)}) collective-permute-start(bf16[256,512]{1,0:T(8,128)(2,1)S(1)} %collective-permute-done.4.refs_4_), channel_id=1, source_target_pairs={{0,1},{1,0},{2,3},{3,2},{4,5},{5,4},{6,7},{7,6},{8,9},{9,8},{10,11... | collective-permute-start | bytes 786440 | tf_op jit(solution)/shard_map/ppermute | solution.py:178
  53.6 3.3 %collective-permute-start.21 = (bf16[256,512]{1,0:T(8,128)(2,1)}, bf16[256,512]{1,0:T(8,128)(2,1)}, u32[]{:S(2)}, u32[]{:S(2)}) collective-permute-start(bf16[256,512]{1,0:T(8,128)(2,1)} %collective-permute-done.12.refs_8_), channel_id=1, source_target_pairs={{0,1},{1,0},{2,3},{3,2},{4,5},{5,4},{6,7},{7,6},{8,9},{9,8},{10,11... | collective-permute-start | bytes 786440 | tf_op jit(solution)/shard_map/ppermute | solution.py:178
  56.9 4.2 %collective-permute-start.19 = (bf16[512,512]{1,0:T(8,128)(2,1)}, bf16[512,512]{1,0:T(8,128)(2,1)S(1)}, u32[]{:S(2)}, u32[]{:S(2)}) collective-permute-start(bf16[512,512]{1,0:T(8,128)(2,1)} %copy-done.8), channel_id=1, source_target_pairs={{0,1},{1,0},{2,3},{3,2},{4,5},{5,4},{6,7},{7,6},{8,9},{9,8},{10,11... | collective-permute-start | bytes 1572872 | tf_op jit(solution)/shard_map/ppermute | solution.py:178
  57.4 3.1 %collective-permute-start.18 = (bf16[512,512]{1,0:T(8,128)(2,1)}, bf16[512,512]{1,0:T(8,128)(2,1)S(1)}, u32[]{:S(2)}, u32[]{:S(2)}) collective-permute-start(bf16[512,512]{1,0:T(8,128)(2,1)} %collective-permute-done.5.refs_5_), channel_id=1, source_target_pairs={{0,1},{1,0},{2,3},{3,2},{4,5},{5,4},{6,7},{7,6},{8,9},{9,8},{10,11... | collective-permute-start | bytes 1572872 | tf_op jit(solution)/shard_map/ppermute | solution.py:178
  57.8 3.3 %collective-permute-start.20 = (bf16[512,512]{1,0:T(8,128)(2,1)S(1)}, bf16[512,512]{1,0:T(8,128)(2,1)S(1)}, u32[]{:S(2)}, u32[]{:S(2)}) collective-permute-start(bf16[512,512]{1,0:T(8,128)(2,1)S(1)} %collective-permute-done.7.refs_7_), channel_id=1, source_target_pairs={{0,1},{1,0},{2,3},{3,2},{4,5},{5,4},{6,7},{7,6},{8,9},{9,8},{10,11... | collective-permute-start | bytes 1572872 | tf_op jit(solution)/shard_map/ppermute | solution.py:178
  (17 other events, 176.3 us)

commit v9 on v7

--- a/solution.py
+++ b/solution.py
@@ -50,28 +50,27 @@
 
 def couplings_kernel(table, ends, dims, *refs):
     own_waves, mate_waves = refs[:10], refs[10:20]
-    own_right, own_left, mate_right, mate_left, far, far_mate = refs[20:26]
-    out, left, right, waves, halves, sums, rounded, op_sems, wave_sems, out_sems = refs[26:]
+    own_right, own_left, mate_right, mate_left, far_right, far_left, far_mate_right, far_mate_left = refs[20:28]
+    out, left, right, waves, halves, sums, rounded, op_sems, wave_sems, out_sems = refs[28:]
     y, x, z, core = (lax.axis_index(name) for name in ("y_hi", "x_lo", "z", "core"))
     sectors, width, _ = waves.shape
     rows = sums.shape[1]
     ops = own_right.shape[0] // width
     half = width // 2
     left_copies, right_copies = [], []
-    for n, (pair, c, left_rows, skip, right_ops) in enumerate((
-        (y, core, own_left, 0, own_right),
-        (y, 1 - core, mate_left, 0, mate_right),
-        (1 - y, core, far, ops * width, far),
-        (1 - y, 1 - core, far_mate, ops * width, far_mate),
+    for n, (pair, c, left_rows, right_ops) in enumerate((
+        (y, core, own_left, own_right),
+        (y, 1 - core, mate_left, mate_right),
+        (1 - y, core, far_left, far_right),
+        (1 - y, 1 - core, far_mate_left, far_mate_right),
     )):
         first = (pair * 2 + c) * ops
         size = ops * rows
-        part = left_rows.at[pl.ds(pl.multiple_of(skip + core * size, size), size)]
+        part = left_rows.at[pl.ds(pl.multiple_of(core * size, size), size)]
         to = left.at[pl.ds(pl.multiple_of(first * rows, size), size)]
         left_copies.append(pltpu.make_async_copy(part, to, op_sems.at[2 * n]))
-        part = right_ops.at[pl.ds(0, ops * width)]
         to = right.at[pl.ds(pl.multiple_of(first * width, ops * width), ops * width)]
-        right_copies.append(pltpu.make_async_copy(part, to, op_sems.at[2 * n + 1]))
+        right_copies.append(pltpu.make_async_copy(right_ops, to, op_sems.at[2 * n + 1]))
     for copy in left_copies:
         copy.start()
     whole, low, high = (pl.ds(0, width), pl.ds(0, half), pl.ds(half, half))
@@ -188,9 +187,9 @@
     near_rows = lax.dynamic_index_in_dim(rows, y, 0, keepdims=False)
     sent_rows = lax.dynamic_index_in_dim(rows, 1 - y, 0, keepdims=False)
     near_right = right_ops.reshape(ops * width, width)
-    far_meta = lax.ppermute(meta, "y_hi", SWAP)
-    sent_right, sent_rows, far_meta = lax.optimization_barrier((near_right, sent_rows, far_meta))
-    far = lax.ppermute(jnp.concatenate([sent_right, sent_rows]), "y_hi", SWAP)
+    lists = jnp.pad(meta.astype(jnp.bfloat16), ((0, 16 - meta.shape[0]), (0, width - meta.shape[1])))
+    far_right = lax.ppermute(near_right, "y_hi", SWAP)
+    far_rows = lax.ppermute(jnp.concatenate([sent_rows, lists]), "y_hi", SWAP)
     before = lax.ppermute(block, "z", UP)
     after = lax.ppermute(block, "z", DOWN)
     side = along_x(block, UP)
@@ -203,12 +202,18 @@
     early = (block, before, after, across_low, across_high, side, side_before, side_after)
     held = lax.optimization_barrier(early + (near_right, near_rows))
     mate_early = [to_mate(part) for part in held]
-    mate_late = [to_mate(part) for part in (corner_low, corner_high, far)]
-    metas = jnp.stack([meta, far_meta])
-    metas, _ = lax.optimization_barrier((metas, held[6]))
-    metas = jnp.concatenate([metas, to_mate(metas)])
+    late = (corner_low, corner_high, far_right, far_rows)
+    mate_late = [to_mate(part) for part in late]
+    mate_meta = to_mate(lax.optimization_barrier((meta, held[6]))[0])
+    mate_late, mate_early = lax.optimization_barrier((mate_late, mate_early))
+
+    def listed(buffer):
+        return lax.slice(buffer, (size, 0), (size + meta.shape[0], meta.shape[1])).astype(jnp.int32)
+
+    metas = jnp.stack([meta, listed(lax.optimization_barrier((far_rows, mate_late[3]))[0]), mate_meta, listed(mate_late[3])])
     waves = early + (corner_low, corner_high) + tuple(mate_early[:8] + mate_late[:2])
-    return waves + (near_right, near_rows, mate_early[8], mate_early[9], far, mate_late[2]), metas
+    operators = (near_right, near_rows, mate_early[8], mate_early[9], far_right, far_rows, mate_late[2], mate_late[3])
+    return waves + operators, metas
 
 
 def body(

time: 133 us -> 133 us (level)
  waiting for transfers between devices: 19.6 us -> 23.6 us
  local copies, waits for them, and re-layouts: 7.68 us -> 4.34 us
  Pallas kernels: 19.2 us -> 20.7 us
    ppermute x1, waiting for transfers between devices: 2.09 us -> 8.86 us  [share(): across_low = lax.ppermute(before[:half], 'z', UP)]
    ppermute x5, waiting for transfers between devices: 0.01 us -> 3.46 us  [along_x(): return lax.ppermute(part, ('x_hi', 'x_lo'), steps)]
    ppermute x1, waiting for transfers between devices: 2.65 us -> 0.01 us  [share(): across_high = lax.ppermute(after[half:], 'z', DOWN)]
    ppermute x1, waiting for transfers between devices: 7.9 us -> 5.44 us  [share(): after = lax.ppermute(block, 'z', DOWN)]
    ppermute x5, starting transfers between devices: 7.07 us -> 5.1 us  [along_x(): return lax.ppermute(part, ('x_hi', 'x_lo'), steps)]
    ppermute x2, starting transfers between devices: 5 us -> 3.09 us  [the longest x1 2.99 us: share(): far_rows = lax.ppermute(jnp.concatenate([sent_rows, lists]), 'y_hi', SWAP)]
    ppermute x1, starting transfers between devices: 1.61 us -> 3.48 us  [share(): across_high = lax.ppermute(after[half:], 'z', DOWN)]
    unnamed x29 -> x42, local copies, waits for them, and re-layouts: 3.27 us -> 1.41 us
  transfers between devices with their start and end apart: 25 -> 26, of which waited for: 10 -> 12; matrix products, arithmetic and copies ran while one was open for 3% -> 2% of each run, Pallas kernels for 0% -> 0%
where the time goes in v9:
time: 133 us
  blocking collectives  52.5 us (39%)
  starting transfers between devices  29.3 us (22%)
  waiting for transfers between devices  23.6 us (18%)
  Pallas kernels  20.7 us (16%)
  local copies, waits for them, and re-layouts  4.34 us (3%)
  other arithmetic  2.52 us (2%)
    all_to_all x1, blocking collectives, body(): lax.all_to_all(partial.reshape(-1, 2, SLICE, width), REDUCE, 0, 0, tiled=...  32.3 us
    pallas_call x1, Pallas kernels, body(): pl.pallas_call(couplings_kernel, out_shape=jax.ShapeDtypeStruct((LEVELS,...  20.7 us
    all_to_all x1, blocking collectives, body(): whole = lax.all_to_all(spread, SPREAD, 0, 0, tiled=True)  20.1 us
    ppermute x15, starting transfers between devices, to_mate(): return lax.ppermute(part, 'core', SWAP)  13.8 us
    ppermute x1, waiting for transfers between devices, share(): across_low = lax.ppermute(before[:half], 'z', UP)  8.86 us
    ppermute x1, waiting for transfers between devices, share(): after = lax.ppermute(block, 'z', DOWN)  5.44 us
    ppermute x15, waiting for transfers between devices, to_mate(): return lax.ppermute(part, 'core', SWAP)  5.24 us
    ppermute x5, starting transfers between devices, along_x(): return lax.ppermute(part, ('x_hi', 'x_lo'), steps)  5.1 us
  transfers between devices with their start and end apart: 26, of which 12 were waited for; matrix products, arithmetic and copies ran while one was open for 2% of the time, Pallas kernels for 0%

profile of v9, /device:TPU:1, one launch (start us, length us, event | category | flops | bytes accessed | tf_op | source)
XLA Modules:
  0.0 133.2 jit_solution(4112666783320738870)
XLA Ops:
  0.0 2.0 %collective-permute-start.12 = (bf16[512,512]{1,0:T(8,128)(2,1)}, bf16[512,512]{1,0:T(8,128)(2,1)}, u32[]{:S(2)}, u32[]{:S(2)}) collective-permute-start(bf16[512,512]{1,0:T(8,128)(2,1)} %bitcast.38), channel_id=1, source_target_pairs={{0,8},{8,64},{64,72},{72,0},{1,9},{9,65},{65,73},{73,1},{2,10},{10... | collective-permute-start | bytes 1572872 | tf_op jit(solution)/shard_map/ppermute | solution.py:173
  2.0 3.8 %collective-permute-start.5 = (bf16[512,512]{1,0:T(8,128)(2,1)}, bf16[512,512]{1,0:T(8,128)(2,1)S(1)}, u32[]{:S(2)}, u32[]{:S(2)}) collective-permute-start(bf16[512,512]{1,0:T(8,128)(2,1)} %bitcast.39), channel_id=1, source_target_pairs={{0,6},{2,0},{4,2},{6,4},{1,7},{3,1},{5,3},{7,5},{8,14},{10,8},{12,... | collective-permute-start | bytes 1572872 | tf_op jit(solution)/shard_map/ppermute | solution.py:194
  5.8 1.3 copy.12
  7.9 3.0 %collective-permute-start = (bf16[528,512]{1,0:T(8,128)(2,1)S(1)}, bf16[528,512]{1,0:T(8,128)(2,1)S(1)}, u32[]{:S(2)}, u32[]{:S(2)}) collective-permute-start(bf16[528,512]{1,0:T(8,128)(2,1)S(1)} %fusion.1), channel_id=1, source_target_pairs={{0,32},{32,0},{1,33},{33,1},{2,34},{34,2},{3,35},{35,3},{4,36},{36... | collective-permute-start | bytes 1622024 | tf_op jit(solution)/shard_map/ppermute | solution.py:192
  10.9 5.4 %collective-permute-done.5.refs_2_ = bf16[512,512]{1,0:T(8,128)(2,1)S(1)} collective-permute-done((bf16[512,512]{1,0:T(8,128)(2,1)}, bf16[512,512]{1,0:T(8,128)(2,1)S(1)}, u32[]{:S(2)}, u32[]{:S(2)}) %collective-permute-start.5) | collective-permute-done | bytes 524320 | tf_op jit(solution)/shard_map/ppermute | solution.py:194
  16.4 3.5 %collective-permute-start.6 = (bf16[256,512]{1,0:T(8,128)(2,1)S(1)}, bf16[256,512]{1,0:T(8,128)(2,1)S(1)}, u32[]{:S(2)}, u32[]{:S(2)}) collective-permute-start(bf16[256,512]{1,0:T(8,128)(2,1)S(1)} %slice.29), channel_id=1, source_target_pairs={{0,6},{2,0},{4,2},{6,4},{1,7},{3,1},{5,3},{7,5},{8,14},{10,8},{12,... | collective-permute-start | bytes 786440 | tf_op jit(solution)/shard_map/ppermute | solution.py:197
  19.9 1.4 %collective-permute-start.14 = (bf16[512,512]{1,0:T(8,128)(2,1)S(1)}, bf16[512,512]{1,0:T(8,128)(2,1)}, u32[]{:S(2)}, u32[]{:S(2)}) collective-permute-start(bf16[512,512]{1,0:T(8,128)(2,1)S(1)} %collective-permute-done.5.refs_2_), channel_id=1, source_target_pairs={{0,72},{8,0},{64,8},{72,64},{1,73},{9,1},{65,9},{73,65},{2,74},{10... | collective-permute-start | bytes 1572872 | tf_op jit(solution)/shard_map/ppermute | solution.py:173
  21.4 0.6 collective-permute-done.refs_25_
  22.0 3.9 %collective-permute-start.11 = (bf16[528,512]{1,0:T(8,128)(2,1)S(1)}, bf16[528,512]{1,0:T(8,128)(2,1)S(1)}, u32[]{:S(2)}, u32[]{:S(2)}) collective-permute-start(bf16[528,512]{1,0:T(8,128)(2,1)S(1)} %collective-permute-done.refs_25_), channel_id=1, source_target_pairs={{0,1},{1,0},{2,3},{3,2},{4,5},{5,4},{6,7},{7,6},{8,9},{9,8},{10,11... | collective-permute-start | bytes 1622024 | tf_op jit(solution)/shard_map/ppermute | solution.py:177
  26.0 8.9 %collective-permute-done.2.refs_3_ = bf16[256,512]{1,0:T(8,128)(2,1)S(1)} collective-permute-done((bf16[256,512]{1,0:T(8,128)(2,1)S(1)}, bf16[256,512]{1,0:T(8,128)(2,1)S(1)}, u32[]{:S(2)}, u32[]{:S(2)}) %collective-permute-start.2) | collective-permute-done | bytes 262176 | tf_op jit(solution)/shard_map/ppermute | solution.py:196
  34.9 1.6 %collective-permute-start.7 = (bf16[256,512]{1,0:T(8,128)(2,1)S(1)}, bf16[256,512]{1,0:T(8,128)(2,1)S(1)}, u32[]{:S(2)}, u32[]{:S(2)}) collective-permute-start(bf16[256,512]{1,0:T(8,128)(2,1)S(1)} %collective-permute-done.6.refs_4_), channel_id=1, source_target_pairs={{0,72},{8,0},{64,8},{72,64},{1,73},{9,1},{65,9},{73,65},{2,74},{10... | collective-permute-start | bytes 786440 | tf_op jit(solution)/shard_map/ppermute | solution.py:173
  36.5 1.8 %collective-permute-start.15 = (bf16[512,512]{1,0:T(8,128)(2,1)S(1)}, bf16[512,512]{1,0:T(8,128)(2,1)S(1)}, u32[]{:S(2)}, u32[]{:S(2)}) collective-permute-start(bf16[512,512]{1,0:T(8,128)(2,1)S(1)} %bitcast.42), channel_id=1, source_target_pairs={{0,1},{1,0},{2,3},{3,2},{4,5},{5,4},{6,7},{7,6},{8,9},{9,8},{10,11... | collective-permute-start | bytes 1572872 | tf_op jit(solution)/shard_map/ppermute | solution.py:177
  38.3 3.1 %collective-permute-done.7.refs_9_ = bf16[256,512]{1,0:T(8,128)(2,1)S(1)} collective-permute-done((bf16[256,512]{1,0:T(8,128)(2,1)S(1)}, bf16[256,512]{1,0:T(8,128)(2,1)S(1)}, u32[]{:S(2)}, u32[]{:S(2)}) %collective-permute-start.7) | collective-permute-done | bytes 262176 | tf_op jit(solution)/shard_map/ppermute | solution.py:173
  41.3 2.3 %collective-permute-start.8 = (bf16[256,512]{1,0:T(8,128)(2,1)S(1)}, bf16[256,512]{1,0:T(8,128)(2,1)}, u32[]{:S(2)}, u32[]{:S(2)}) collective-permute-start(bf16[256,512]{1,0:T(8,128)(2,1)S(1)} %collective-permute-done.7.refs_9_), channel_id=1, source_target_pairs={{0,1},{1,0},{2,3},{3,2},{4,5},{5,4},{6,7},{7,6},{8,9},{9,8},{10,11... | collective-permute-start | bytes 786440 | tf_op jit(solution)/shard_map/ppermute | solution.py:177
  44.0 2.4 %collective-permute-start.4 = (bf16[256,512]{1,0:T(8,128)(2,1)S(1)}, bf16[256,512]{1,0:T(8,128)(2,1)}, u32[]{:S(2)}, u32[]{:S(2)}) collective-permute-start(bf16[256,512]{1,0:T(8,128)(2,1)S(1)} %collective-permute-done.3.refs_8_), channel_id=1, source_target_pairs={{0,1},{1,0},{2,3},{3,2},{4,5},{5,4},{6,7},{7,6},{8,9},{9,8},{10,11... | collective-permute-start | bytes 786440 | tf_op jit(solution)/shard_map/ppermute | solution.py:177
  50.2 2.1 %collective-permute-done.20.refs_15_ = bf16[512,512]{1,0:T(8,128)(2,1)S(1)} collective-permute-done((bf16[512,512]{1,0:T(8,128)(2,1)}, bf16[512,512]{1,0:T(8,128)(2,1)S(1)}, u32[]{:S(2)}, u32[]{:S(2)}) %collective-permute-start.20) | collective-permute-done | bytes 524320 | tf_op jit(solution)/shard_map/ppermute | solution.py:177
  52.3 0.8 copy-done.10
  53.7 1.7 %collective-permute-done.22.refs_17_ = bf16[512,512]{1,0:T(8,128)(2,1)} collective-permute-done((bf16[512,512]{1,0:T(8,128)(2,1)}, bf16[512,512]{1,0:T(8,128)(2,1)}, u32[]{:S(2)}, u32[]{:S(2)}) %collective-permute-start.22) | collective-permute-done | bytes 524320 | tf_op jit(solution)/shard_map/ppermute | solution.py:177
  56.2 0.7 bitcast_convert_fusion
  57.8 0.6 broadcast_add_fusion.table
  58.4 20.7 %couplings.1 = bf16[4,16,32,512]{3,2,1,0:T(8,128)(2,1)} custom-call(s32[120]{0:T(128)} %broadcast_add_fusion.table, s32[4]{0:T(128)} %copy-done.17, s32[16]{0:T(128)} %dims.1, bf16[512,512]{1,0:T(8,128)(2,1)} %bitcast.41, bf16[512,512]{1,0:T(8,128)(2,1)} %copy-done.2, bf16[512,512]{1,0:T(8,128)(2,1)} %copy-done.1, bf16[256,512]{1,0:T(8,128)(2,1)} %copy-done.12, ...), custom_call_target="tpu_custom_call" | custom-call | tf_op jit(solution)/shard_map/couplings/pallas_call | solution.py:241
  79.1 32.3 %all_to_all.10 = bf16[32,2,32,512]{3,2,1,0:T(8,128)(2,1)S(1)} all-to-all(bf16[32,2,32,512]{3,2,1,0:T(8,128)(2,1)} %bitcast.33), channel_id=1, replica_groups=mesh['x_hi'=2,'y_hi'=2,'y_lo'=2,'x_lo'=2,'z'=4,'core'=2] {'x_hi','y_lo',..., dimensions={0} | all-to-all | bytes 4194304 | tf_op jit(solution)/shard_map/all_to_all | solution.py:260
  111.9 20.1 %all_to_all.11 = bf16[16,32,512]{2,1,0:T(8,128)(2,1)S(1)} all-to-all(bf16[16,32,512]{2,1,0:T(8,128)(2,1)S(1)} %bitcast.36), channel_id=1, replica_groups=mesh['x_hi'=2,'y_hi'=2,'y_lo'=2,'x_lo'=2,'z'=4,'core'=2] {'x_hi','y_hi',..., dimensions={0} | all-to-all | bytes 1048576 | tf_op jit(solution)/shard_map/all_to_all | solution.py:263
  132.1 1.1 copy.13
  (104 shorter events, 8.0 us)
Async XLA Ops:
  0.0 19.9 %collective-permute-start.12 = (bf16[512,512]{1,0:T(8,128)(2,1)}, bf16[512,512]{1,0:T(8,128)(2,1)}, u32[]{:S(2)}, u32[]{:S(2)}) collective-permute-start(bf16[512,512]{1,0:T(8,128)(2,1)} %bitcast.38), channel_id=1, source_target_pairs={{0,8},{8,64},{64,72},{72,0},{1,9},{9,65},{65,73},{73,1},{2,10},{10... | collective-permute-start | bytes 1572872 | tf_op jit(solution)/shard_map/ppermute | solution.py:173
  2.0 14.3 %collective-permute-start.5 = (bf16[512,512]{1,0:T(8,128)(2,1)}, bf16[512,512]{1,0:T(8,128)(2,1)S(1)}, u32[]{:S(2)}, u32[]{:S(2)}) collective-permute-start(bf16[512,512]{1,0:T(8,128)(2,1)} %bitcast.39), channel_id=1, source_target_pairs={{0,6},{2,0},{4,2},{6,4},{1,7},{3,1},{5,3},{7,5},{8,14},{10,8},{12,... | collective-permute-start | bytes 1572872 | tf_op jit(solution)/shard_map/ppermute | solution.py:194
  5.8 15.5 %collective-permute-start.1 = (bf16[512,512]{1,0:T(8,128)(2,1)}, bf16[512,512]{1,0:T(8,128)(2,1)S(1)}, u32[]{:S(2)}, u32[]{:S(2)}) collective-permute-start(bf16[512,512]{1,0:T(8,128)(2,1)} %bitcast.40), channel_id=1, source_target_pairs={{0,2},{2,4},{4,6},{6,0},{1,3},{3,5},{5,7},{7,1},{8,10},{10,12},{12... | collective-permute-start | bytes 1572872 | tf_op jit(solution)/shard_map/ppermute | solution.py:193
  7.9 14.1 %collective-permute-start = (bf16[528,512]{1,0:T(8,128)(2,1)S(1)}, bf16[528,512]{1,0:T(8,128)(2,1)S(1)}, u32[]{:S(2)}, u32[]{:S(2)}) collective-permute-start(bf16[528,512]{1,0:T(8,128)(2,1)S(1)} %fusion.1), channel_id=1, source_target_pairs={{0,32},{32,0},{1,33},{33,1},{2,34},{34,2},{3,35},{35,3},{4,36},{36... | collective-permute-start | bytes 1622024 | tf_op jit(solution)/shard_map/ppermute | solution.py:192
  10.9 35.6 %collective-permute-start.9 = (bf16[1024,512]{1,0:T(8,128)(2,1)}, bf16[1024,512]{1,0:T(8,128)(2,1)S(1)}, u32[]{:S(2)}, u32[]{:S(2)}) collective-permute-start(bf16[1024,512]{1,0:T(8,128)(2,1)} %bitcast.9.refs_20_), channel_id=1, source_target_pairs={{0,32},{32,0},{1,33},{33,1},{2,34},{34,2},{3,35},{35,3},{4,36},{36... | collective-permute-start | bytes 3145736 | tf_op jit(solution)/shard_map/ppermute | solution.py:191
  16.4 9.5 %collective-permute-start.6 = (bf16[256,512]{1,0:T(8,128)(2,1)S(1)}, bf16[256,512]{1,0:T(8,128)(2,1)S(1)}, u32[]{:S(2)}, u32[]{:S(2)}) collective-permute-start(bf16[256,512]{1,0:T(8,128)(2,1)S(1)} %slice.29), channel_id=1, source_target_pairs={{0,6},{2,0},{4,2},{6,4},{1,7},{3,1},{5,3},{7,5},{8,14},{10,8},{12,... | collective-permute-start | bytes 786440 | tf_op jit(solution)/shard_map/ppermute | solution.py:197
  19.9 16.6 %collective-permute-start.14 = (bf16[512,512]{1,0:T(8,128)(2,1)S(1)}, bf16[512,512]{1,0:T(8,128)(2,1)}, u32[]{:S(2)}, u32[]{:S(2)}) collective-permute-start(bf16[512,512]{1,0:T(8,128)(2,1)S(1)} %collective-permute-done.5.refs_2_), channel_id=1, source_target_pairs={{0,72},{8,0},{64,8},{72,64},{1,73},{9,1},{65,9},{73,65},{2,74},{10... | collective-permute-start | bytes 1572872 | tf_op jit(solution)/shard_map/ppermute | solution.py:173
  21.3 15.2 %collective-permute-start.13 = (bf16[512,512]{1,0:T(8,128)(2,1)S(1)}, bf16[512,512]{1,0:T(8,128)(2,1)}, u32[]{:S(2)}, u32[]{:S(2)}) collective-permute-start(bf16[512,512]{1,0:T(8,128)(2,1)S(1)} %collective-permute-done.1.refs_1_), channel_id=1, source_target_pairs={{0,8},{8,64},{64,72},{72,0},{1,9},{9,65},{65,73},{73,1},{2,10},{10... | collective-permute-start | bytes 1572872 | tf_op jit(solution)/shard_map/ppermute | solution.py:173
  22.0 24.6 %collective-permute-start.11 = (bf16[528,512]{1,0:T(8,128)(2,1)S(1)}, bf16[528,512]{1,0:T(8,128)(2,1)S(1)}, u32[]{:S(2)}, u32[]{:S(2)}) collective-permute-start(bf16[528,512]{1,0:T(8,128)(2,1)S(1)} %collective-permute-done.refs_25_), channel_id=1, source_target_pairs={{0,1},{1,0},{2,3},{3,2},{4,5},{5,4},{6,7},{7,6},{8,9},{9,8},{10,11... | collective-permute-start | bytes 1622024 | tf_op jit(solution)/shard_map/ppermute | solution.py:177
  25.9 8.9 %collective-permute-start.2 = (bf16[256,512]{1,0:T(8,128)(2,1)S(1)}, bf16[256,512]{1,0:T(8,128)(2,1)S(1)}, u32[]{:S(2)}, u32[]{:S(2)}) collective-permute-start(bf16[256,512]{1,0:T(8,128)(2,1)S(1)} %slice.28), channel_id=1, source_target_pairs={{0,2},{2,4},{4,6},{6,0},{1,3},{3,5},{5,7},{7,1},{8,10},{10,12},{12... | collective-permute-start | bytes 786440 | tf_op jit(solution)/shard_map/ppermute | solution.py:196
  34.9 6.5 %collective-permute-start.7 = (bf16[256,512]{1,0:T(8,128)(2,1)S(1)}, bf16[256,512]{1,0:T(8,128)(2,1)S(1)}, u32[]{:S(2)}, u32[]{:S(2)}) collective-permute-start(bf16[256,512]{1,0:T(8,128)(2,1)S(1)} %collective-permute-done.6.refs_4_), channel_id=1, source_target_pairs={{0,72},{8,0},{64,8},{72,64},{1,73},{9,1},{65,9},{73,65},{2,74},{10... | collective-permute-start | bytes 786440 | tf_op jit(solution)/shard_map/ppermute | solution.py:173
  36.5 7.5 %collective-permute-start.3 = (bf16[256,512]{1,0:T(8,128)(2,1)S(1)}, bf16[256,512]{1,0:T(8,128)(2,1)S(1)}, u32[]{:S(2)}, u32[]{:S(2)}) collective-permute-start(bf16[256,512]{1,0:T(8,128)(2,1)S(1)} %collective-permute-done.2.refs_3_), channel_id=1, source_target_pairs={{0,8},{8,64},{64,72},{72,0},{1,9},{9,65},{65,73},{73,1},{2,10},{10... | collective-permute-start | bytes 786440 | tf_op jit(solution)/shard_map/ppermute | solution.py:173
  36.5 12.2 %collective-permute-start.15 = (bf16[512,512]{1,0:T(8,128)(2,1)S(1)}, bf16[512,512]{1,0:T(8,128)(2,1)S(1)}, u32[]{:S(2)}, u32[]{:S(2)}) collective-permute-start(bf16[512,512]{1,0:T(8,128)(2,1)S(1)} %bitcast.42), channel_id=1, source_target_pairs={{0,1},{1,0},{2,3},{3,2},{4,5},{5,4},{6,7},{7,6},{8,9},{9,8},{10,11... | collective-permute-start | bytes 1572872 | tf_op jit(solution)/shard_map/ppermute | solution.py:177
  41.3 5.6 %collective-permute-start.8 = (bf16[256,512]{1,0:T(8,128)(2,1)S(1)}, bf16[256,512]{1,0:T(8,128)(2,1)}, u32[]{:S(2)}, u32[]{:S(2)}) collective-permute-start(bf16[256,512]{1,0:T(8,128)(2,1)S(1)} %collective-permute-done.7.refs_9_), channel_id=1, source_target_pairs={{0,1},{1,0},{2,3},{3,2},{4,5},{5,4},{6,7},{7,6},{8,9},{9,8},{10,11... | collective-permute-start | bytes 786440 | tf_op jit(solution)/shard_map/ppermute | solution.py:177
  44.0 3.7 %collective-permute-start.4 = (bf16[256,512]{1,0:T(8,128)(2,1)S(1)}, bf16[256,512]{1,0:T(8,128)(2,1)}, u32[]{:S(2)}, u32[]{:S(2)}) collective-permute-start(bf16[256,512]{1,0:T(8,128)(2,1)S(1)} %collective-permute-done.3.refs_8_), channel_id=1, source_target_pairs={{0,1},{1,0},{2,3},{3,2},{4,5},{5,4},{6,7},{7,6},{8,9},{9,8},{10,11... | collective-permute-start | bytes 786440 | tf_op jit(solution)/shard_map/ppermute | solution.py:177
  46.6 1.8 %collective-permute-start.19 = (bf16[256,512]{1,0:T(8,128)(2,1)S(1)}, bf16[256,512]{1,0:T(8,128)(2,1)S(1)}, u32[]{:S(2)}, u32[]{:S(2)}) collective-permute-start(bf16[256,512]{1,0:T(8,128)(2,1)S(1)} %collective-permute-done.6.refs_4_), channel_id=1, source_target_pairs={{0,1},{1,0},{2,3},{3,2},{4,5},{5,4},{6,7},{7,6},{8,9},{9,8},{10,11... | collective-permute-start | bytes 786440 | tf_op jit(solution)/shard_map/ppermute | solution.py:177
  46.9 2.1 %collective-permute-start.16 = (bf16[512,512]{1,0:T(8,128)(2,1)S(1)}, bf16[512,512]{1,0:T(8,128)(2,1)S(1)}, u32[]{:S(2)}, u32[]{:S(2)}) collective-permute-start(bf16[512,512]{1,0:T(8,128)(2,1)S(1)} %collective-permute-done.1.refs_1_), channel_id=1, source_target_pairs={{0,1},{1,0},{2,3},{3,2},{4,5},{5,4},{6,7},{7,6},{8,9},{9,8},{10,11... | collective-permute-start | bytes 1572872 | tf_op jit(solution)/shard_map/ppermute | solution.py:177
  47.7 2.1 %collective-permute-start.17 = (bf16[512,512]{1,0:T(8,128)(2,1)S(1)}, bf16[512,512]{1,0:T(8,128)(2,1)S(1)}, u32[]{:S(2)}, u32[]{:S(2)}) collective-permute-start(bf16[512,512]{1,0:T(8,128)(2,1)S(1)} %collective-permute-done.5.refs_2_), channel_id=1, source_target_pairs={{0,1},{1,0},{2,3},{3,2},{4,5},{5,4},{6,7},{7,6},{8,9},{9,8},{10,11... | collective-permute-start | bytes 1572872 | tf_op jit(solution)/shard_map/ppermute | solution.py:177
  48.1 4.2 %collective-permute-start.20 = (bf16[512,512]{1,0:T(8,128)(2,1)}, bf16[512,512]{1,0:T(8,128)(2,1)S(1)}, u32[]{:S(2)}, u32[]{:S(2)}) collective-permute-start(bf16[512,512]{1,0:T(8,128)(2,1)} %collective-permute-done.12.refs_5_), channel_id=1, source_target_pairs={{0,1},{1,0},{2,3},{3,2},{4,5},{5,4},{6,7},{7,6},{8,9},{9,8},{10,11... | collective-permute-start | bytes 1572872 | tf_op jit(solution)/shard_map/ppermute | solution.py:177
  48.5 7.7 %collective-permute-start.23 = (bf16[1024,512]{1,0:T(8,128)(2,1)}, bf16[1024,512]{1,0:T(8,128)(2,1)}, u32[]{:S(2)}, u32[]{:S(2)}) collective-permute-start(bf16[1024,512]{1,0:T(8,128)(2,1)} %bitcast.9.refs_20_), channel_id=1, source_target_pairs={{0,1},{1,0},{2,3},{3,2},{4,5},{5,4},{6,7},{7,6},{8,9},{9,8},{10,11... | collective-permute-start | bytes 3145736 | tf_op jit(solution)/shard_map/ppermute | solution.py:177
  48.7 7.5 %collective-permute-start.10 = (bf16[1024,512]{1,0:T(8,128)(2,1)S(1)}, bf16[1024,512]{1,0:T(8,128)(2,1)}, u32[]{:S(2)}, u32[]{:S(2)}) collective-permute-start(bf16[1024,512]{1,0:T(8,128)(2,1)S(1)} %collective-permute-done.9.refs_24_), channel_id=1, source_target_pairs={{0,1},{1,0},{2,3},{3,2},{4,5},{5,4},{6,7},{7,6},{8,9},{9,8},{10,11... | collective-permute-start | bytes 3145736 | tf_op jit(solution)/shard_map/ppermute | solution.py:177
  49.1 6.3 %collective-permute-start.22 = (bf16[512,512]{1,0:T(8,128)(2,1)}, bf16[512,512]{1,0:T(8,128)(2,1)}, u32[]{:S(2)}, u32[]{:S(2)}) collective-permute-start(bf16[512,512]{1,0:T(8,128)(2,1)} %collective-permute-done.14.refs_7_), channel_id=1, source_target_pairs={{0,1},{1,0},{2,3},{3,2},{4,5},{5,4},{6,7},{7,6},{8,9},{9,8},{10,11... | collective-permute-start | bytes 1572872 | tf_op jit(solution)/shard_map/ppermute | solution.py:177
  49.8 6.1 %collective-permute-start.24 = (bf16[512,512]{1,0:T(8,128)(2,1)S(1)}, bf16[512,512]{1,0:T(8,128)(2,1)}, u32[]{:S(2)}, u32[]{:S(2)}) collective-permute-start(bf16[512,512]{1,0:T(8,128)(2,1)S(1)} %get-tuple-element.40.refs_21_), channel_id=1, source_target_pairs={{0,1},{1,0},{2,3},{3,2},{4,5},{5,4},{6,7},{7,6},{8,9},{9,8},{10,11... | collective-permute-start | bytes 1572872 | tf_op jit(solution)/shard_map/ppermute | solution.py:177
  53.1 3.1 %collective-permute-start.21 = (bf16[512,512]{1,0:T(8,128)(2,1)}, bf16[512,512]{1,0:T(8,128)(2,1)}, u32[]{:S(2)}, u32[]{:S(2)}) collective-permute-start(bf16[512,512]{1,0:T(8,128)(2,1)} %collective-permute-done.13.refs_6_), channel_id=1, source_target_pairs={{0,1},{1,0},{2,3},{3,2},{4,5},{5,4},{6,7},{7,6},{8,9},{9,8},{10,11... | collective-permute-start | bytes 1572872 | tf_op jit(solution)/shard_map/ppermute | solution.py:177
  (23 other events, 324.3 us)

commit v10 on v9

--- a/solution.py
+++ b/solution.py
@@ -188,6 +188,7 @@
     sent_rows = lax.dynamic_index_in_dim(rows, 1 - y, 0, keepdims=False)
     near_right = right_ops.reshape(ops * width, width)
     lists = jnp.pad(meta.astype(jnp.bfloat16), ((0, 16 - meta.shape[0]), (0, width - meta.shape[1])))
+    near_rows = jnp.concatenate([near_rows, lists])
     far_right = lax.ppermute(near_right, "y_hi", SWAP)
     far_rows = lax.ppermute(jnp.concatenate([sent_rows, lists]), "y_hi", SWAP)
     before = lax.ppermute(block, "z", UP)
@@ -204,13 +205,12 @@
     mate_early = [to_mate(part) for part in held]
     late = (corner_low, corner_high, far_right, far_rows)
     mate_late = [to_mate(part) for part in late]
-    mate_meta = to_mate(lax.optimization_barrier((meta, held[6]))[0])
     mate_late, mate_early = lax.optimization_barrier((mate_late, mate_early))
 
     def listed(buffer):
         return lax.slice(buffer, (size, 0), (size + meta.shape[0], meta.shape[1])).astype(jnp.int32)
 
-    metas = jnp.stack([meta, listed(lax.optimization_barrier((far_rows, mate_late[3]))[0]), mate_meta, listed(mate_late[3])])
+    metas = jnp.stack([meta, listed(lax.optimization_barrier((far_rows, mate_late[3]))[0]), listed(mate_early[9]), listed(mate_late[3])])
     waves = early + (corner_low, corner_high) + tuple(mate_early[:8] + mate_late[:2])
     operators = (near_right, near_rows, mate_early[8], mate_early[9], far_right, far_rows, mate_late[2], mate_late[3])
     return waves + operators, metas

time: 133 us -> 133 us (level); the launches traced: 133 us -> 132 us
  starting transfers between devices: 29.3 us -> 35.2 us
  waiting for transfers between devices: 23.6 us -> 17.7 us
  Pallas kernels: 20.7 us -> 18.6 us
    ppermute x1, waiting for transfers between devices: 8.86 us -> 2.46 us  [share(): across_low = lax.ppermute(before[:half], 'z', UP)]
    ppermute x15 -> x14, starting transfers between devices: 13.8 us -> 18 us  [to_mate(): return lax.ppermute(part, 'core', SWAP)]
    pallas_call x1, Pallas kernels: 20.7 us -> 18.6 us  [body(): pl.pallas_call(couplings_kernel, out_shape=jax.ShapeDtypeStruct((LEVELS,...]
    ppermute x5, waiting for transfers between devices: 3.46 us -> 1.69 us  [along_x(): return lax.ppermute(part, ('x_hi', 'x_lo'), steps)]
    ppermute x1, waiting for transfers between devices: 0.01 us -> 1.69 us  [share(): across_high = lax.ppermute(after[half:], 'z', DOWN)]
    ppermute x5, starting transfers between devices: 5.1 us -> 6.52 us  [along_x(): return lax.ppermute(part, ('x_hi', 'x_lo'), steps)]
    ppermute x15 -> x14, waiting for transfers between devices: 5.24 us -> 5.72 us  [to_mate(): return lax.ppermute(part, 'core', SWAP)]
  transfers between devices with their start and end apart: 26 -> 25, of which waited for: 12 -> 13; matrix products, arithmetic and copies ran while one was open for 2% -> 1% of each run, Pallas kernels for 0% -> 0%
where the time goes in v10:
time: 133 us; the launch traced here: 132 us
  blocking collectives  53 us (40%)
  starting transfers between devices  35.2 us (26%)
  Pallas kernels  18.6 us (14%)
  waiting for transfers between devices  17.7 us (13%)
  local copies, waits for them, and re-layouts  4.36 us (3%)
  other arithmetic  2.5 us (2%)
    all_to_all x1, blocking collectives, body(): lax.all_to_all(partial.reshape(-1, 2, SLICE, width), REDUCE, 0, 0, tiled=...  33.4 us
    all_to_all x1, blocking collectives, body(): whole = lax.all_to_all(spread, SPREAD, 0, 0, tiled=True)  19.6 us
    pallas_call x1, Pallas kernels, body(): pl.pallas_call(couplings_kernel, out_shape=jax.ShapeDtypeStruct((LEVELS,...  18.6 us
    ppermute x14, starting transfers between devices, to_mate(): return lax.ppermute(part, 'core', SWAP)  18 us
    ppermute x5, starting transfers between devices, along_x(): return lax.ppermute(part, ('x_hi', 'x_lo'), steps)  6.52 us
    ppermute x14, waiting for transfers between devices, to_mate(): return lax.ppermute(part, 'core', SWAP)  5.72 us
    ppermute x1, waiting for transfers between devices, share(): after = lax.ppermute(block, 'z', DOWN)  5.02 us
    ppermute x1, starting transfers between devices, share(): after = lax.ppermute(block, 'z', DOWN)  3.76 us
  transfers between devices with their start and end apart: 25, of which 13 were waited for; matrix products, arithmetic and copies ran while one was open for 1% of the time, Pallas kernels for 0%

profile of v10, /device:TPU:1, one launch (start us, length us, event | category | flops | bytes accessed | tf_op | source)
XLA Modules:
  0.0 131.6 jit_solution(10492672879870222145)
XLA Ops:
  0.0 2.0 %collective-permute-start.12 = (bf16[512,512]{1,0:T(8,128)(2,1)}, bf16[512,512]{1,0:T(8,128)(2,1)}, u32[]{:S(2)}, u32[]{:S(2)}) collective-permute-start(bf16[512,512]{1,0:T(8,128)(2,1)} %bitcast.43), channel_id=1, source_target_pairs={{0,8},{8,64},{64,72},{72,0},{1,9},{9,65},{65,73},{73,1},{2,10},{10... | collective-permute-start | bytes 1572872 | tf_op jit(solution)/shard_map/ppermute | solution.py:173
  2.0 3.8 %collective-permute-start.5 = (bf16[512,512]{1,0:T(8,128)(2,1)}, bf16[512,512]{1,0:T(8,128)(2,1)S(1)}, u32[]{:S(2)}, u32[]{:S(2)}) collective-permute-start(bf16[512,512]{1,0:T(8,128)(2,1)} %bitcast.44), channel_id=1, source_target_pairs={{0,6},{2,0},{4,2},{6,4},{1,7},{3,1},{5,3},{7,5},{8,14},{10,8},{12,... | collective-permute-start | bytes 1572872 | tf_op jit(solution)/shard_map/ppermute | solution.py:195
  5.8 1.3 copy.12
  7.9 3.0 %collective-permute-start = (bf16[528,512]{1,0:T(8,128)(2,1)S(1)}, bf16[528,512]{1,0:T(8,128)(2,1)S(1)}, u32[]{:S(2)}, u32[]{:S(2)}) collective-permute-start(bf16[528,512]{1,0:T(8,128)(2,1)S(1)} %get-tuple-element.65), channel_id=1, source_target_pairs={{0,32},{32,0},{1,33},{33,1},{2,34},{34,2},{3,35},{35,3},{4,36},{36... | collective-permute-start | bytes 1622024 | tf_op jit(solution)/shard_map/ppermute | solution.py:193
  11.4 5.0 %collective-permute-done.5.refs_2_ = bf16[512,512]{1,0:T(8,128)(2,1)S(1)} collective-permute-done((bf16[512,512]{1,0:T(8,128)(2,1)}, bf16[512,512]{1,0:T(8,128)(2,1)S(1)}, u32[]{:S(2)}, u32[]{:S(2)}) %collective-permute-start.5) | collective-permute-done | bytes 524320 | tf_op jit(solution)/shard_map/ppermute | solution.py:195
  16.4 3.5 %collective-permute-start.6 = (bf16[256,512]{1,0:T(8,128)(2,1)S(1)}, bf16[256,512]{1,0:T(8,128)(2,1)S(1)}, u32[]{:S(2)}, u32[]{:S(2)}) collective-permute-start(bf16[256,512]{1,0:T(8,128)(2,1)S(1)} %slice.33), channel_id=1, source_target_pairs={{0,6},{2,0},{4,2},{6,4},{1,7},{3,1},{5,3},{7,5},{8,14},{10,8},{12,... | collective-permute-start | bytes 786440 | tf_op jit(solution)/shard_map/ppermute | solution.py:198
  19.9 1.4 %collective-permute-start.14 = (bf16[512,512]{1,0:T(8,128)(2,1)S(1)}, bf16[512,512]{1,0:T(8,128)(2,1)}, u32[]{:S(2)}, u32[]{:S(2)}) collective-permute-start(bf16[512,512]{1,0:T(8,128)(2,1)S(1)} %collective-permute-done.5.refs_2_), channel_id=1, source_target_pairs={{0,72},{8,0},{64,8},{72,64},{1,73},{9,1},{65,9},{73,65},{2,74},{10... | collective-permute-start | bytes 1572872 | tf_op jit(solution)/shard_map/ppermute | solution.py:173
  22.0 1.7 %collective-permute-done.6.refs_4_ = bf16[256,512]{1,0:T(8,128)(2,1)S(1)} collective-permute-done((bf16[256,512]{1,0:T(8,128)(2,1)S(1)}, bf16[256,512]{1,0:T(8,128)(2,1)S(1)}, u32[]{:S(2)}, u32[]{:S(2)}) %collective-permute-start.6) | collective-permute-done | bytes 262176 | tf_op jit(solution)/shard_map/ppermute | solution.py:198
  23.7 2.7 %collective-permute-start.11 = (bf16[528,512]{1,0:T(8,128)(2,1)S(1)}, bf16[528,512]{1,0:T(8,128)(2,1)S(1)}, u32[]{:S(2)}, u32[]{:S(2)}) collective-permute-start(bf16[528,512]{1,0:T(8,128)(2,1)S(1)} %collective-permute-done.refs_25_), channel_id=1, source_target_pairs={{0,1},{1,0},{2,3},{3,2},{4,5},{5,4},{6,7},{7,6},{8,9},{9,8},{10,11... | collective-permute-start | bytes 1622024 | tf_op jit(solution)/shard_map/ppermute | solution.py:177
  26.4 2.5 %collective-permute-done.2.refs_3_ = bf16[256,512]{1,0:T(8,128)(2,1)S(1)} collective-permute-done((bf16[256,512]{1,0:T(8,128)(2,1)S(1)}, bf16[256,512]{1,0:T(8,128)(2,1)S(1)}, u32[]{:S(2)}, u32[]{:S(2)}) %collective-permute-start.2) | collective-permute-done | bytes 262176 | tf_op jit(solution)/shard_map/ppermute | solution.py:197
  28.9 2.0 %collective-permute-start.7 = (bf16[256,512]{1,0:T(8,128)(2,1)S(1)}, bf16[256,512]{1,0:T(8,128)(2,1)S(1)}, u32[]{:S(2)}, u32[]{:S(2)}) collective-permute-start(bf16[256,512]{1,0:T(8,128)(2,1)S(1)} %collective-permute-done.6.refs_4_), channel_id=1, source_target_pairs={{0,72},{8,0},{64,8},{72,64},{1,73},{9,1},{65,9},{73,65},{2,74},{10... | collective-permute-start | bytes 786440 | tf_op jit(solution)/shard_map/ppermute | solution.py:173
  31.4 1.0 collective-permute-start.3
  32.4 1.2 collective-permute-done.13.refs_6_
  33.6 4.4 %collective-permute-start.15 = (bf16[512,512]{1,0:T(8,128)(2,1)S(1)}, bf16[512,512]{1,0:T(8,128)(2,1)S(1)}, u32[]{:S(2)}, u32[]{:S(2)}) collective-permute-start(bf16[512,512]{1,0:T(8,128)(2,1)S(1)} %bitcast.47), channel_id=1, source_target_pairs={{0,1},{1,0},{2,3},{3,2},{4,5},{5,4},{6,7},{7,6},{8,9},{9,8},{10,11... | collective-permute-start | bytes 1572872 | tf_op jit(solution)/shard_map/ppermute | solution.py:177
  38.0 1.9 %collective-permute-start.8 = (bf16[256,512]{1,0:T(8,128)(2,1)S(1)}, bf16[256,512]{1,0:T(8,128)(2,1)}, u32[]{:S(2)}, u32[]{:S(2)}) collective-permute-start(bf16[256,512]{1,0:T(8,128)(2,1)S(1)} %collective-permute-done.7.refs_9_), channel_id=1, source_target_pairs={{0,1},{1,0},{2,3},{3,2},{4,5},{5,4},{6,7},{7,6},{8,9},{9,8},{10,11... | collective-permute-start | bytes 786440 | tf_op jit(solution)/shard_map/ppermute | solution.py:177
  39.9 4.2 %collective-permute-start.4 = (bf16[256,512]{1,0:T(8,128)(2,1)S(1)}, bf16[256,512]{1,0:T(8,128)(2,1)}, u32[]{:S(2)}, u32[]{:S(2)}) collective-permute-start(bf16[256,512]{1,0:T(8,128)(2,1)S(1)} %collective-permute-done.3.refs_8_), channel_id=1, source_target_pairs={{0,1},{1,0},{2,3},{3,2},{4,5},{5,4},{6,7},{7,6},{8,9},{9,8},{10,11... | collective-permute-start | bytes 786440 | tf_op jit(solution)/shard_map/ppermute | solution.py:177
  44.6 2.2 %collective-permute-start.18 = (bf16[256,512]{1,0:T(8,128)(2,1)S(1)}, bf16[256,512]{1,0:T(8,128)(2,1)}, u32[]{:S(2)}, u32[]{:S(2)}) collective-permute-start(bf16[256,512]{1,0:T(8,128)(2,1)S(1)} %collective-permute-done.2.refs_3_), channel_id=1, source_target_pairs={{0,1},{1,0},{2,3},{3,2},{4,5},{5,4},{6,7},{7,6},{8,9},{9,8},{10,11... | collective-permute-start | bytes 786440 | tf_op jit(solution)/shard_map/ppermute | solution.py:177
  50.2 2.1 %collective-permute-done.20.refs_15_ = bf16[512,512]{1,0:T(8,128)(2,1)S(1)} collective-permute-done((bf16[512,512]{1,0:T(8,128)(2,1)}, bf16[512,512]{1,0:T(8,128)(2,1)S(1)}, u32[]{:S(2)}, u32[]{:S(2)}) %collective-permute-start.20) | collective-permute-done | bytes 524320 | tf_op jit(solution)/shard_map/ppermute | solution.py:177
  52.3 0.8 copy-done.10
  53.7 1.7 %collective-permute-done.21.refs_16_ = bf16[512,512]{1,0:T(8,128)(2,1)} collective-permute-done((bf16[512,512]{1,0:T(8,128)(2,1)}, bf16[512,512]{1,0:T(8,128)(2,1)}, u32[]{:S(2)}, u32[]{:S(2)}) %collective-permute-start.21) | collective-permute-done | bytes 524320 | tf_op jit(solution)/shard_map/ppermute | solution.py:177
  58.4 18.6 %couplings.1 = bf16[4,16,32,512]{3,2,1,0:T(8,128)(2,1)} custom-call(s32[120]{0:T(128)} %broadcast_add_fusion.table, s32[4]{0:T(128)} %copy-done.17, s32[16]{0:T(128)} %dims.1, bf16[512,512]{1,0:T(8,128)(2,1)} %bitcast.46, bf16[512,512]{1,0:T(8,128)(2,1)} %copy-done.2, bf16[512,512]{1,0:T(8,128)(2,1)} %copy-done.1, bf16[256,512]{1,0:T(8,128)(2,1)} %copy-done.12, ...), custom_call_target="tpu_custom_call" | custom-call | tf_op jit(solution)/shard_map/couplings/pallas_call | solution.py:241
  77.0 33.4 %all_to_all.10 = bf16[32,2,32,512]{3,2,1,0:T(8,128)(2,1)S(1)} all-to-all(bf16[32,2,32,512]{3,2,1,0:T(8,128)(2,1)} %bitcast.35), channel_id=1, replica_groups=mesh['x_hi'=2,'y_hi'=2,'y_lo'=2,'x_lo'=2,'z'=4,'core'=2] {'x_hi','y_lo',..., dimensions={0} | all-to-all | bytes 4194304 | tf_op jit(solution)/shard_map/all_to_all | solution.py:260
  110.8 19.6 %all_to_all.11 = bf16[16,32,512]{2,1,0:T(8,128)(2,1)S(1)} all-to-all(bf16[16,32,512]{2,1,0:T(8,128)(2,1)S(1)} %bitcast.38), channel_id=1, replica_groups=mesh['x_hi'=2,'y_hi'=2,'y_lo'=2,'x_lo'=2,'z'=4,'core'=2] {'x_hi','y_hi',..., dimensions={0} | all-to-all | bytes 1048576 | tf_op jit(solution)/shard_map/all_to_all | solution.py:263
  130.6 1.1 copy.13
  (103 shorter events, 10.4 us)
Async XLA Ops:
  0.0 19.9 %collective-permute-start.12 = (bf16[512,512]{1,0:T(8,128)(2,1)}, bf16[512,512]{1,0:T(8,128)(2,1)}, u32[]{:S(2)}, u32[]{:S(2)}) collective-permute-start(bf16[512,512]{1,0:T(8,128)(2,1)} %bitcast.43), channel_id=1, source_target_pairs={{0,8},{8,64},{64,72},{72,0},{1,9},{9,65},{65,73},{73,1},{2,10},{10... | collective-permute-start | bytes 1572872 | tf_op jit(solution)/shard_map/ppermute | solution.py:173
  2.0 14.3 %collective-permute-start.5 = (bf16[512,512]{1,0:T(8,128)(2,1)}, bf16[512,512]{1,0:T(8,128)(2,1)S(1)}, u32[]{:S(2)}, u32[]{:S(2)}) collective-permute-start(bf16[512,512]{1,0:T(8,128)(2,1)} %bitcast.44), channel_id=1, source_target_pairs={{0,6},{2,0},{4,2},{6,4},{1,7},{3,1},{5,3},{7,5},{8,14},{10,8},{12,... | collective-permute-start | bytes 1572872 | tf_op jit(solution)/shard_map/ppermute | solution.py:195
  5.8 15.5 %collective-permute-start.1 = (bf16[512,512]{1,0:T(8,128)(2,1)}, bf16[512,512]{1,0:T(8,128)(2,1)S(1)}, u32[]{:S(2)}, u32[]{:S(2)}) collective-permute-start(bf16[512,512]{1,0:T(8,128)(2,1)} %bitcast.45), channel_id=1, source_target_pairs={{0,2},{2,4},{4,6},{6,0},{1,3},{3,5},{5,7},{7,1},{8,10},{10,12},{12... | collective-permute-start | bytes 1572872 | tf_op jit(solution)/shard_map/ppermute | solution.py:194
  7.9 14.1 %collective-permute-start = (bf16[528,512]{1,0:T(8,128)(2,1)S(1)}, bf16[528,512]{1,0:T(8,128)(2,1)S(1)}, u32[]{:S(2)}, u32[]{:S(2)}) collective-permute-start(bf16[528,512]{1,0:T(8,128)(2,1)S(1)} %get-tuple-element.65), channel_id=1, source_target_pairs={{0,32},{32,0},{1,33},{33,1},{2,34},{34,2},{3,35},{35,3},{4,36},{36... | collective-permute-start | bytes 1622024 | tf_op jit(solution)/shard_map/ppermute | solution.py:193
  10.9 33.7 %collective-permute-start.9 = (bf16[1024,512]{1,0:T(8,128)(2,1)S(1)}, bf16[1024,512]{1,0:T(8,128)(2,1)}, u32[]{:S(2)}, u32[]{:S(2)}) collective-permute-start(bf16[1024,512]{1,0:T(8,128)(2,1)S(1)} %bitcast.40), channel_id=1, source_target_pairs={{0,32},{32,0},{1,33},{33,1},{2,34},{34,2},{3,35},{35,3},{4,36},{36... | collective-permute-start | bytes 3145736 | tf_op jit(solution)/shard_map/ppermute | solution.py:192
  16.4 7.3 %collective-permute-start.6 = (bf16[256,512]{1,0:T(8,128)(2,1)S(1)}, bf16[256,512]{1,0:T(8,128)(2,1)S(1)}, u32[]{:S(2)}, u32[]{:S(2)}) collective-permute-start(bf16[256,512]{1,0:T(8,128)(2,1)S(1)} %slice.33), channel_id=1, source_target_pairs={{0,6},{2,0},{4,2},{6,4},{1,7},{3,1},{5,3},{7,5},{8,14},{10,8},{12,... | collective-permute-start | bytes 786440 | tf_op jit(solution)/shard_map/ppermute | solution.py:198
  19.9 11.5 %collective-permute-start.14 = (bf16[512,512]{1,0:T(8,128)(2,1)S(1)}, bf16[512,512]{1,0:T(8,128)(2,1)}, u32[]{:S(2)}, u32[]{:S(2)}) collective-permute-start(bf16[512,512]{1,0:T(8,128)(2,1)S(1)} %collective-permute-done.5.refs_2_), channel_id=1, source_target_pairs={{0,72},{8,0},{64,8},{72,64},{1,73},{9,1},{65,9},{73,65},{2,74},{10... | collective-permute-start | bytes 1572872 | tf_op jit(solution)/shard_map/ppermute | solution.py:173
  21.3 12.3 %collective-permute-start.13 = (bf16[512,512]{1,0:T(8,128)(2,1)S(1)}, bf16[512,512]{1,0:T(8,128)(2,1)}, u32[]{:S(2)}, u32[]{:S(2)}) collective-permute-start(bf16[512,512]{1,0:T(8,128)(2,1)S(1)} %collective-permute-done.1.refs_1_), channel_id=1, source_target_pairs={{0,8},{8,64},{64,72},{72,0},{1,9},{9,65},{65,73},{73,1},{2,10},{10... | collective-permute-start | bytes 1572872 | tf_op jit(solution)/shard_map/ppermute | solution.py:173
  22.0 6.8 %collective-permute-start.2 = (bf16[256,512]{1,0:T(8,128)(2,1)S(1)}, bf16[256,512]{1,0:T(8,128)(2,1)S(1)}, u32[]{:S(2)}, u32[]{:S(2)}) collective-permute-start(bf16[256,512]{1,0:T(8,128)(2,1)S(1)} %slice.32), channel_id=1, source_target_pairs={{0,2},{2,4},{4,6},{6,0},{1,3},{3,5},{5,7},{7,1},{8,10},{10,12},{12... | collective-permute-start | bytes 786440 | tf_op jit(solution)/shard_map/ppermute | solution.py:197
  23.7 23.0 %collective-permute-start.11 = (bf16[528,512]{1,0:T(8,128)(2,1)S(1)}, bf16[528,512]{1,0:T(8,128)(2,1)S(1)}, u32[]{:S(2)}, u32[]{:S(2)}) collective-permute-start(bf16[528,512]{1,0:T(8,128)(2,1)S(1)} %collective-permute-done.refs_25_), channel_id=1, source_target_pairs={{0,1},{1,0},{2,3},{3,2},{4,5},{5,4},{6,7},{7,6},{8,9},{9,8},{10,11... | collective-permute-start | bytes 1622024 | tf_op jit(solution)/shard_map/ppermute | solution.py:177
  28.9 9.1 %collective-permute-start.7 = (bf16[256,512]{1,0:T(8,128)(2,1)S(1)}, bf16[256,512]{1,0:T(8,128)(2,1)S(1)}, u32[]{:S(2)}, u32[]{:S(2)}) collective-permute-start(bf16[256,512]{1,0:T(8,128)(2,1)S(1)} %collective-permute-done.6.refs_4_), channel_id=1, source_target_pairs={{0,72},{8,0},{64,8},{72,64},{1,73},{9,1},{65,9},{73,65},{2,74},{10... | collective-permute-start | bytes 786440 | tf_op jit(solution)/shard_map/ppermute | solution.py:173
  31.4 8.5 %collective-permute-start.3 = (bf16[256,512]{1,0:T(8,128)(2,1)S(1)}, bf16[256,512]{1,0:T(8,128)(2,1)S(1)}, u32[]{:S(2)}, u32[]{:S(2)}) collective-permute-start(bf16[256,512]{1,0:T(8,128)(2,1)S(1)} %collective-permute-done.2.refs_3_), channel_id=1, source_target_pairs={{0,8},{8,64},{64,72},{72,0},{1,9},{9,65},{65,73},{73,1},{2,10},{10... | collective-permute-start | bytes 786440 | tf_op jit(solution)/shard_map/ppermute | solution.py:173
  33.6 15.1 %collective-permute-start.15 = (bf16[512,512]{1,0:T(8,128)(2,1)S(1)}, bf16[512,512]{1,0:T(8,128)(2,1)S(1)}, u32[]{:S(2)}, u32[]{:S(2)}) collective-permute-start(bf16[512,512]{1,0:T(8,128)(2,1)S(1)} %bitcast.47), channel_id=1, source_target_pairs={{0,1},{1,0},{2,3},{3,2},{4,5},{5,4},{6,7},{7,6},{8,9},{9,8},{10,11... | collective-permute-start | bytes 1572872 | tf_op jit(solution)/shard_map/ppermute | solution.py:177
  38.0 8.9 %collective-permute-start.8 = (bf16[256,512]{1,0:T(8,128)(2,1)S(1)}, bf16[256,512]{1,0:T(8,128)(2,1)}, u32[]{:S(2)}, u32[]{:S(2)}) collective-permute-start(bf16[256,512]{1,0:T(8,128)(2,1)S(1)} %collective-permute-done.7.refs_9_), channel_id=1, source_target_pairs={{0,1},{1,0},{2,3},{3,2},{4,5},{5,4},{6,7},{7,6},{8,9},{9,8},{10,11... | collective-permute-start | bytes 786440 | tf_op jit(solution)/shard_map/ppermute | solution.py:177
  39.9 7.4 %collective-permute-start.4 = (bf16[256,512]{1,0:T(8,128)(2,1)S(1)}, bf16[256,512]{1,0:T(8,128)(2,1)}, u32[]{:S(2)}, u32[]{:S(2)}) collective-permute-start(bf16[256,512]{1,0:T(8,128)(2,1)S(1)} %collective-permute-done.3.refs_8_), channel_id=1, source_target_pairs={{0,1},{1,0},{2,3},{3,2},{4,5},{5,4},{6,7},{7,6},{8,9},{9,8},{10,11... | collective-permute-start | bytes 786440 | tf_op jit(solution)/shard_map/ppermute | solution.py:177
  44.6 3.5 %collective-permute-start.18 = (bf16[256,512]{1,0:T(8,128)(2,1)S(1)}, bf16[256,512]{1,0:T(8,128)(2,1)}, u32[]{:S(2)}, u32[]{:S(2)}) collective-permute-start(bf16[256,512]{1,0:T(8,128)(2,1)S(1)} %collective-permute-done.2.refs_3_), channel_id=1, source_target_pairs={{0,1},{1,0},{2,3},{3,2},{4,5},{5,4},{6,7},{7,6},{8,9},{9,8},{10,11... | collective-permute-start | bytes 786440 | tf_op jit(solution)/shard_map/ppermute | solution.py:177
  46.9 2.2 %collective-permute-start.16 = (bf16[512,512]{1,0:T(8,128)(2,1)S(1)}, bf16[512,512]{1,0:T(8,128)(2,1)S(1)}, u32[]{:S(2)}, u32[]{:S(2)}) collective-permute-start(bf16[512,512]{1,0:T(8,128)(2,1)S(1)} %collective-permute-done.1.refs_1_), channel_id=1, source_target_pairs={{0,1},{1,0},{2,3},{3,2},{4,5},{5,4},{6,7},{7,6},{8,9},{9,8},{10,11... | collective-permute-start | bytes 1572872 | tf_op jit(solution)/shard_map/ppermute | solution.py:177
  47.3 2.5 %collective-permute-start.17 = (bf16[512,512]{1,0:T(8,128)(2,1)S(1)}, bf16[512,512]{1,0:T(8,128)(2,1)S(1)}, u32[]{:S(2)}, u32[]{:S(2)}) collective-permute-start(bf16[512,512]{1,0:T(8,128)(2,1)S(1)} %collective-permute-done.5.refs_2_), channel_id=1, source_target_pairs={{0,1},{1,0},{2,3},{3,2},{4,5},{5,4},{6,7},{7,6},{8,9},{9,8},{10,11... | collective-permute-start | bytes 1572872 | tf_op jit(solution)/shard_map/ppermute | solution.py:177
  48.1 4.2 %collective-permute-start.20 = (bf16[512,512]{1,0:T(8,128)(2,1)}, bf16[512,512]{1,0:T(8,128)(2,1)S(1)}, u32[]{:S(2)}, u32[]{:S(2)}) collective-permute-start(bf16[512,512]{1,0:T(8,128)(2,1)} %collective-permute-done.12.refs_5_), channel_id=1, source_target_pairs={{0,1},{1,0},{2,3},{3,2},{4,5},{5,4},{6,7},{7,6},{8,9},{9,8},{10,11... | collective-permute-start | bytes 1572872 | tf_op jit(solution)/shard_map/ppermute | solution.py:177
  48.4 7.7 %collective-permute-start.23 = (bf16[1024,512]{1,0:T(8,128)(2,1)S(1)}, bf16[1024,512]{1,0:T(8,128)(2,1)}, u32[]{:S(2)}, u32[]{:S(2)}) collective-permute-start(bf16[1024,512]{1,0:T(8,128)(2,1)S(1)} %bitcast.41), channel_id=1, source_target_pairs={{0,1},{1,0},{2,3},{3,2},{4,5},{5,4},{6,7},{7,6},{8,9},{9,8},{10,11... | collective-permute-start | bytes 3145736 | tf_op jit(solution)/shard_map/ppermute | solution.py:177
  48.7 7.5 %collective-permute-start.10 = (bf16[1024,512]{1,0:T(8,128)(2,1)}, bf16[1024,512]{1,0:T(8,128)(2,1)}, u32[]{:S(2)}, u32[]{:S(2)}) collective-permute-start(bf16[1024,512]{1,0:T(8,128)(2,1)} %collective-permute-done.9.refs_24_), channel_id=1, source_target_pairs={{0,1},{1,0},{2,3},{3,2},{4,5},{5,4},{6,7},{7,6},{8,9},{9,8},{10,11... | collective-permute-start | bytes 3145736 | tf_op jit(solution)/shard_map/ppermute | solution.py:177
  49.1 7.1 %collective-permute-start.24 = (bf16[528,512]{1,0:T(8,128)(2,1)S(1)}, bf16[528,512]{1,0:T(8,128)(2,1)}, u32[]{:S(2)}, u32[]{:S(2)}) collective-permute-start(bf16[528,512]{1,0:T(8,128)(2,1)S(1)} %get-tuple-element.39.refs_21_), channel_id=1, source_target_pairs={{0,1},{1,0},{2,3},{3,2},{4,5},{5,4},{6,7},{7,6},{8,9},{9,8},{10,11... | collective-permute-start | bytes 1622024 | tf_op jit(solution)/shard_map/ppermute | solution.py:177
  49.8 5.6 %collective-permute-start.21 = (bf16[512,512]{1,0:T(8,128)(2,1)}, bf16[512,512]{1,0:T(8,128)(2,1)}, u32[]{:S(2)}, u32[]{:S(2)}) collective-permute-start(bf16[512,512]{1,0:T(8,128)(2,1)} %collective-permute-done.13.refs_6_), channel_id=1, source_target_pairs={{0,1},{1,0},{2,3},{3,2},{4,5},{5,4},{6,7},{7,6},{8,9},{9,8},{10,11... | collective-permute-start | bytes 1572872 | tf_op jit(solution)/shard_map/ppermute | solution.py:177
  53.1 3.1 %collective-permute-start.22 = (bf16[512,512]{1,0:T(8,128)(2,1)}, bf16[512,512]{1,0:T(8,128)(2,1)}, u32[]{:S(2)}, u32[]{:S(2)}) collective-permute-start(bf16[512,512]{1,0:T(8,128)(2,1)} %collective-permute-done.14.refs_7_), channel_id=1, source_target_pairs={{0,1},{1,0},{2,3},{3,2},{4,5},{5,4},{6,7},{7,6},{8,9},{9,8},{10,11... | collective-permute-start | bytes 1572872 | tf_op jit(solution)/shard_map/ppermute | solution.py:177
  (22 other events, 329.8 us)

commit v11 on v10

--- a/solution.py
+++ b/solution.py
@@ -161,7 +161,7 @@
             rounded[part, s] = total.astype(jnp.bfloat16)
             return carry
 
-        lax.fori_loop(0, sectors, finish, 0)
+        lax.fori_loop(0, sectors, finish, 0, unroll=True)
         copy = pltpu.make_async_copy(rounded.at[part], out.at[part], out_sems.at[part])
         copy.start()
         copies.append(copy)

time: 133 us -> 135 us (1.015); the launches traced: 132 us -> 135 us
  Pallas kernels: 18.6 us -> 22.7 us
    pallas_call x1, Pallas kernels: 18.6 us -> 22.7 us  [body(): pl.pallas_call(couplings_kernel, out_shape=jax.ShapeDtypeStruct((LEVELS,...]
where the time goes in v11:
time: 135 us
  blocking collectives  52.8 us (39%)
  starting transfers between devices  35.2 us (26%)
  Pallas kernels  22.7 us (17%)
  waiting for transfers between devices  17.7 us (13%)
  local copies, waits for them, and re-layouts  4.36 us (3%)
  other arithmetic  2.5 us (2%)
    all_to_all x1, blocking collectives, body(): lax.all_to_all(partial.reshape(-1, 2, SLICE, width), REDUCE, 0, 0, tiled=...  33.2 us
    pallas_call x1, Pallas kernels, body(): pl.pallas_call(couplings_kernel, out_shape=jax.ShapeDtypeStruct((LEVELS,...  22.7 us
    all_to_all x1, blocking collectives, body(): whole = lax.all_to_all(spread, SPREAD, 0, 0, tiled=True)  19.6 us
    ppermute x14, starting transfers between devices, to_mate(): return lax.ppermute(part, 'core', SWAP)  18 us
    ppermute x5, starting transfers between devices, along_x(): return lax.ppermute(part, ('x_hi', 'x_lo'), steps)  6.52 us
    ppermute x14, waiting for transfers between devices, to_mate(): return lax.ppermute(part, 'core', SWAP)  5.72 us
    ppermute x1, waiting for transfers between devices, share(): after = lax.ppermute(block, 'z', DOWN)  5.02 us
    ppermute x1, starting transfers between devices, share(): after = lax.ppermute(block, 'z', DOWN)  3.76 us
  transfers between devices with their start and end apart: 25, of which 13 were waited for; matrix products, arithmetic and copies ran while one was open for 1% of the time, Pallas kernels for 0%

profile of v11, /device:TPU:1, one launch (start us, length us, event | category | flops | bytes accessed | tf_op | source)
XLA Modules:
  0.0 135.4 jit_solution(7386106564770861896)
XLA Ops:
  0.0 2.0 %collective-permute-start.12 = (bf16[512,512]{1,0:T(8,128)(2,1)}, bf16[512,512]{1,0:T(8,128)(2,1)}, u32[]{:S(2)}, u32[]{:S(2)}) collective-permute-start(bf16[512,512]{1,0:T(8,128)(2,1)} %bitcast.43), channel_id=1, source_target_pairs={{0,8},{8,64},{64,72},{72,0},{1,9},{9,65},{65,73},{73,1},{2,10},{10... | collective-permute-start | bytes 1572872 | tf_op jit(solution)/shard_map/ppermute | solution.py:173
  2.0 3.8 %collective-permute-start.5 = (bf16[512,512]{1,0:T(8,128)(2,1)}, bf16[512,512]{1,0:T(8,128)(2,1)S(1)}, u32[]{:S(2)}, u32[]{:S(2)}) collective-permute-start(bf16[512,512]{1,0:T(8,128)(2,1)} %bitcast.44), channel_id=1, source_target_pairs={{0,6},{2,0},{4,2},{6,4},{1,7},{3,1},{5,3},{7,5},{8,14},{10,8},{12,... | collective-permute-start | bytes 1572872 | tf_op jit(solution)/shard_map/ppermute | solution.py:195
  5.8 1.3 copy.12
  7.9 3.0 %collective-permute-start = (bf16[528,512]{1,0:T(8,128)(2,1)S(1)}, bf16[528,512]{1,0:T(8,128)(2,1)S(1)}, u32[]{:S(2)}, u32[]{:S(2)}) collective-permute-start(bf16[528,512]{1,0:T(8,128)(2,1)S(1)} %get-tuple-element.65), channel_id=1, source_target_pairs={{0,32},{32,0},{1,33},{33,1},{2,34},{34,2},{3,35},{35,3},{4,36},{36... | collective-permute-start | bytes 1622024 | tf_op jit(solution)/shard_map/ppermute | solution.py:193
  11.4 5.0 %collective-permute-done.5.refs_2_ = bf16[512,512]{1,0:T(8,128)(2,1)S(1)} collective-permute-done((bf16[512,512]{1,0:T(8,128)(2,1)}, bf16[512,512]{1,0:T(8,128)(2,1)S(1)}, u32[]{:S(2)}, u32[]{:S(2)}) %collective-permute-start.5) | collective-permute-done | bytes 524320 | tf_op jit(solution)/shard_map/ppermute | solution.py:195
  16.4 3.5 %collective-permute-start.6 = (bf16[256,512]{1,0:T(8,128)(2,1)S(1)}, bf16[256,512]{1,0:T(8,128)(2,1)S(1)}, u32[]{:S(2)}, u32[]{:S(2)}) collective-permute-start(bf16[256,512]{1,0:T(8,128)(2,1)S(1)} %slice.33), channel_id=1, source_target_pairs={{0,6},{2,0},{4,2},{6,4},{1,7},{3,1},{5,3},{7,5},{8,14},{10,8},{12,... | collective-permute-start | bytes 786440 | tf_op jit(solution)/shard_map/ppermute | solution.py:198
  19.9 1.4 %collective-permute-start.14 = (bf16[512,512]{1,0:T(8,128)(2,1)S(1)}, bf16[512,512]{1,0:T(8,128)(2,1)}, u32[]{:S(2)}, u32[]{:S(2)}) collective-permute-start(bf16[512,512]{1,0:T(8,128)(2,1)S(1)} %collective-permute-done.5.refs_2_), channel_id=1, source_target_pairs={{0,72},{8,0},{64,8},{72,64},{1,73},{9,1},{65,9},{73,65},{2,74},{10... | collective-permute-start | bytes 1572872 | tf_op jit(solution)/shard_map/ppermute | solution.py:173
  22.0 1.7 %collective-permute-done.6.refs_4_ = bf16[256,512]{1,0:T(8,128)(2,1)S(1)} collective-permute-done((bf16[256,512]{1,0:T(8,128)(2,1)S(1)}, bf16[256,512]{1,0:T(8,128)(2,1)S(1)}, u32[]{:S(2)}, u32[]{:S(2)}) %collective-permute-start.6) | collective-permute-done | bytes 262176 | tf_op jit(solution)/shard_map/ppermute | solution.py:198
  23.7 2.7 %collective-permute-start.11 = (bf16[528,512]{1,0:T(8,128)(2,1)S(1)}, bf16[528,512]{1,0:T(8,128)(2,1)S(1)}, u32[]{:S(2)}, u32[]{:S(2)}) collective-permute-start(bf16[528,512]{1,0:T(8,128)(2,1)S(1)} %collective-permute-done.refs_25_), channel_id=1, source_target_pairs={{0,1},{1,0},{2,3},{3,2},{4,5},{5,4},{6,7},{7,6},{8,9},{9,8},{10,11... | collective-permute-start | bytes 1622024 | tf_op jit(solution)/shard_map/ppermute | solution.py:177
  26.4 2.5 %collective-permute-done.2.refs_3_ = bf16[256,512]{1,0:T(8,128)(2,1)S(1)} collective-permute-done((bf16[256,512]{1,0:T(8,128)(2,1)S(1)}, bf16[256,512]{1,0:T(8,128)(2,1)S(1)}, u32[]{:S(2)}, u32[]{:S(2)}) %collective-permute-start.2) | collective-permute-done | bytes 262176 | tf_op jit(solution)/shard_map/ppermute | solution.py:197
  28.9 2.0 %collective-permute-start.7 = (bf16[256,512]{1,0:T(8,128)(2,1)S(1)}, bf16[256,512]{1,0:T(8,128)(2,1)S(1)}, u32[]{:S(2)}, u32[]{:S(2)}) collective-permute-start(bf16[256,512]{1,0:T(8,128)(2,1)S(1)} %collective-permute-done.6.refs_4_), channel_id=1, source_target_pairs={{0,72},{8,0},{64,8},{72,64},{1,73},{9,1},{65,9},{73,65},{2,74},{10... | collective-permute-start | bytes 786440 | tf_op jit(solution)/shard_map/ppermute | solution.py:173
  31.4 1.0 collective-permute-start.3
  32.4 1.2 collective-permute-done.13.refs_6_
  33.6 4.4 %collective-permute-start.15 = (bf16[512,512]{1,0:T(8,128)(2,1)S(1)}, bf16[512,512]{1,0:T(8,128)(2,1)S(1)}, u32[]{:S(2)}, u32[]{:S(2)}) collective-permute-start(bf16[512,512]{1,0:T(8,128)(2,1)S(1)} %bitcast.47), channel_id=1, source_target_pairs={{0,1},{1,0},{2,3},{3,2},{4,5},{5,4},{6,7},{7,6},{8,9},{9,8},{10,11... | collective-permute-start | bytes 1572872 | tf_op jit(solution)/shard_map/ppermute | solution.py:177
  38.0 1.9 %collective-permute-start.8 = (bf16[256,512]{1,0:T(8,128)(2,1)S(1)}, bf16[256,512]{1,0:T(8,128)(2,1)}, u32[]{:S(2)}, u32[]{:S(2)}) collective-permute-start(bf16[256,512]{1,0:T(8,128)(2,1)S(1)} %collective-permute-done.7.refs_9_), channel_id=1, source_target_pairs={{0,1},{1,0},{2,3},{3,2},{4,5},{5,4},{6,7},{7,6},{8,9},{9,8},{10,11... | collective-permute-start | bytes 786440 | tf_op jit(solution)/shard_map/ppermute | solution.py:177
  39.9 4.2 %collective-permute-start.4 = (bf16[256,512]{1,0:T(8,128)(2,1)S(1)}, bf16[256,512]{1,0:T(8,128)(2,1)}, u32[]{:S(2)}, u32[]{:S(2)}) collective-permute-start(bf16[256,512]{1,0:T(8,128)(2,1)S(1)} %collective-permute-done.3.refs_8_), channel_id=1, source_target_pairs={{0,1},{1,0},{2,3},{3,2},{4,5},{5,4},{6,7},{7,6},{8,9},{9,8},{10,11... | collective-permute-start | bytes 786440 | tf_op jit(solution)/shard_map/ppermute | solution.py:177
  44.6 2.2 %collective-permute-start.18 = (bf16[256,512]{1,0:T(8,128)(2,1)S(1)}, bf16[256,512]{1,0:T(8,128)(2,1)}, u32[]{:S(2)}, u32[]{:S(2)}) collective-permute-start(bf16[256,512]{1,0:T(8,128)(2,1)S(1)} %collective-permute-done.2.refs_3_), channel_id=1, source_target_pairs={{0,1},{1,0},{2,3},{3,2},{4,5},{5,4},{6,7},{7,6},{8,9},{9,8},{10,11... | collective-permute-start | bytes 786440 | tf_op jit(solution)/shard_map/ppermute | solution.py:177
  50.2 2.1 %collective-permute-done.20.refs_15_ = bf16[512,512]{1,0:T(8,128)(2,1)S(1)} collective-permute-done((bf16[512,512]{1,0:T(8,128)(2,1)}, bf16[512,512]{1,0:T(8,128)(2,1)S(1)}, u32[]{:S(2)}, u32[]{:S(2)}) %collective-permute-start.20) | collective-permute-done | bytes 524320 | tf_op jit(solution)/shard_map/ppermute | solution.py:177
  52.3 0.8 copy-done.10
  53.7 1.7 %collective-permute-done.21.refs_16_ = bf16[512,512]{1,0:T(8,128)(2,1)} collective-permute-done((bf16[512,512]{1,0:T(8,128)(2,1)}, bf16[512,512]{1,0:T(8,128)(2,1)}, u32[]{:S(2)}, u32[]{:S(2)}) %collective-permute-start.21) | collective-permute-done | bytes 524320 | tf_op jit(solution)/shard_map/ppermute | solution.py:177
  58.4 22.7 %couplings.1 = bf16[4,16,32,512]{3,2,1,0:T(8,128)(2,1)} custom-call(s32[120]{0:T(128)} %broadcast_add_fusion.table, s32[4]{0:T(128)} %copy-done.17, s32[16]{0:T(128)} %dims.1, bf16[512,512]{1,0:T(8,128)(2,1)} %bitcast.46, bf16[512,512]{1,0:T(8,128)(2,1)} %copy-done.2, bf16[512,512]{1,0:T(8,128)(2,1)} %copy-done.1, bf16[256,512]{1,0:T(8,128)(2,1)} %copy-done.12, ...), custom_call_target="tpu_custom_call" | custom-call | tf_op jit(solution)/shard_map/couplings/pallas_call | solution.py:241
  81.0 33.2 %all_to_all.10 = bf16[32,2,32,512]{3,2,1,0:T(8,128)(2,1)S(1)} all-to-all(bf16[32,2,32,512]{3,2,1,0:T(8,128)(2,1)} %bitcast.35), channel_id=1, replica_groups=mesh['x_hi'=2,'y_hi'=2,'y_lo'=2,'x_lo'=2,'z'=4,'core'=2] {'x_hi','y_lo',..., dimensions={0} | all-to-all | bytes 4194304 | tf_op jit(solution)/shard_map/all_to_all | solution.py:260
  114.6 19.6 %all_to_all.11 = bf16[16,32,512]{2,1,0:T(8,128)(2,1)S(1)} all-to-all(bf16[16,32,512]{2,1,0:T(8,128)(2,1)S(1)} %bitcast.38), channel_id=1, replica_groups=mesh['x_hi'=2,'y_hi'=2,'y_lo'=2,'x_lo'=2,'z'=4,'core'=2] {'x_hi','y_hi',..., dimensions={0} | all-to-all | bytes 1048576 | tf_op jit(solution)/shard_map/all_to_all | solution.py:263
  134.4 1.1 copy.13
  (103 shorter events, 10.4 us)
Async XLA Ops:
  0.0 19.9 %collective-permute-start.12 = (bf16[512,512]{1,0:T(8,128)(2,1)}, bf16[512,512]{1,0:T(8,128)(2,1)}, u32[]{:S(2)}, u32[]{:S(2)}) collective-permute-start(bf16[512,512]{1,0:T(8,128)(2,1)} %bitcast.43), channel_id=1, source_target_pairs={{0,8},{8,64},{64,72},{72,0},{1,9},{9,65},{65,73},{73,1},{2,10},{10... | collective-permute-start | bytes 1572872 | tf_op jit(solution)/shard_map/ppermute | solution.py:173
  2.0 14.3 %collective-permute-start.5 = (bf16[512,512]{1,0:T(8,128)(2,1)}, bf16[512,512]{1,0:T(8,128)(2,1)S(1)}, u32[]{:S(2)}, u32[]{:S(2)}) collective-permute-start(bf16[512,512]{1,0:T(8,128)(2,1)} %bitcast.44), channel_id=1, source_target_pairs={{0,6},{2,0},{4,2},{6,4},{1,7},{3,1},{5,3},{7,5},{8,14},{10,8},{12,... | collective-permute-start | bytes 1572872 | tf_op jit(solution)/shard_map/ppermute | solution.py:195
  5.8 15.5 %collective-permute-start.1 = (bf16[512,512]{1,0:T(8,128)(2,1)}, bf16[512,512]{1,0:T(8,128)(2,1)S(1)}, u32[]{:S(2)}, u32[]{:S(2)}) collective-permute-start(bf16[512,512]{1,0:T(8,128)(2,1)} %bitcast.45), channel_id=1, source_target_pairs={{0,2},{2,4},{4,6},{6,0},{1,3},{3,5},{5,7},{7,1},{8,10},{10,12},{12... | collective-permute-start | bytes 1572872 | tf_op jit(solution)/shard_map/ppermute | solution.py:194
  7.9 14.1 %collective-permute-start = (bf16[528,512]{1,0:T(8,128)(2,1)S(1)}, bf16[528,512]{1,0:T(8,128)(2,1)S(1)}, u32[]{:S(2)}, u32[]{:S(2)}) collective-permute-start(bf16[528,512]{1,0:T(8,128)(2,1)S(1)} %get-tuple-element.65), channel_id=1, source_target_pairs={{0,32},{32,0},{1,33},{33,1},{2,34},{34,2},{3,35},{35,3},{4,36},{36... | collective-permute-start | bytes 1622024 | tf_op jit(solution)/shard_map/ppermute | solution.py:193
  10.9 33.7 %collective-permute-start.9 = (bf16[1024,512]{1,0:T(8,128)(2,1)S(1)}, bf16[1024,512]{1,0:T(8,128)(2,1)}, u32[]{:S(2)}, u32[]{:S(2)}) collective-permute-start(bf16[1024,512]{1,0:T(8,128)(2,1)S(1)} %bitcast.40), channel_id=1, source_target_pairs={{0,32},{32,0},{1,33},{33,1},{2,34},{34,2},{3,35},{35,3},{4,36},{36... | collective-permute-start | bytes 3145736 | tf_op jit(solution)/shard_map/ppermute | solution.py:192
  16.4 7.3 %collective-permute-start.6 = (bf16[256,512]{1,0:T(8,128)(2,1)S(1)}, bf16[256,512]{1,0:T(8,128)(2,1)S(1)}, u32[]{:S(2)}, u32[]{:S(2)}) collective-permute-start(bf16[256,512]{1,0:T(8,128)(2,1)S(1)} %slice.33), channel_id=1, source_target_pairs={{0,6},{2,0},{4,2},{6,4},{1,7},{3,1},{5,3},{7,5},{8,14},{10,8},{12,... | collective-permute-start | bytes 786440 | tf_op jit(solution)/shard_map/ppermute | solution.py:198
  19.9 11.5 %collective-permute-start.14 = (bf16[512,512]{1,0:T(8,128)(2,1)S(1)}, bf16[512,512]{1,0:T(8,128)(2,1)}, u32[]{:S(2)}, u32[]{:S(2)}) collective-permute-start(bf16[512,512]{1,0:T(8,128)(2,1)S(1)} %collective-permute-done.5.refs_2_), channel_id=1, source_target_pairs={{0,72},{8,0},{64,8},{72,64},{1,73},{9,1},{65,9},{73,65},{2,74},{10... | collective-permute-start | bytes 1572872 | tf_op jit(solution)/shard_map/ppermute | solution.py:173
  21.3 12.3 %collective-permute-start.13 = (bf16[512,512]{1,0:T(8,128)(2,1)S(1)}, bf16[512,512]{1,0:T(8,128)(2,1)}, u32[]{:S(2)}, u32[]{:S(2)}) collective-permute-start(bf16[512,512]{1,0:T(8,128)(2,1)S(1)} %collective-permute-done.1.refs_1_), channel_id=1, source_target_pairs={{0,8},{8,64},{64,72},{72,0},{1,9},{9,65},{65,73},{73,1},{2,10},{10... | collective-permute-start | bytes 1572872 | tf_op jit(solution)/shard_map/ppermute | solution.py:173
  22.0 6.8 %collective-permute-start.2 = (bf16[256,512]{1,0:T(8,128)(2,1)S(1)}, bf16[256,512]{1,0:T(8,128)(2,1)S(1)}, u32[]{:S(2)}, u32[]{:S(2)}) collective-permute-start(bf16[256,512]{1,0:T(8,128)(2,1)S(1)} %slice.32), channel_id=1, source_target_pairs={{0,2},{2,4},{4,6},{6,0},{1,3},{3,5},{5,7},{7,1},{8,10},{10,12},{12... | collective-permute-start | bytes 786440 | tf_op jit(solution)/shard_map/ppermute | solution.py:197
  23.7 23.0 %collective-permute-start.11 = (bf16[528,512]{1,0:T(8,128)(2,1)S(1)}, bf16[528,512]{1,0:T(8,128)(2,1)S(1)}, u32[]{:S(2)}, u32[]{:S(2)}) collective-permute-start(bf16[528,512]{1,0:T(8,128)(2,1)S(1)} %collective-permute-done.refs_25_), channel_id=1, source_target_pairs={{0,1},{1,0},{2,3},{3,2},{4,5},{5,4},{6,7},{7,6},{8,9},{9,8},{10,11... | collective-permute-start | bytes 1622024 | tf_op jit(solution)/shard_map/ppermute | solution.py:177
  28.9 9.1 %collective-permute-start.7 = (bf16[256,512]{1,0:T(8,128)(2,1)S(1)}, bf16[256,512]{1,0:T(8,128)(2,1)S(1)}, u32[]{:S(2)}, u32[]{:S(2)}) collective-permute-start(bf16[256,512]{1,0:T(8,128)(2,1)S(1)} %collective-permute-done.6.refs_4_), channel_id=1, source_target_pairs={{0,72},{8,0},{64,8},{72,64},{1,73},{9,1},{65,9},{73,65},{2,74},{10... | collective-permute-start | bytes 786440 | tf_op jit(solution)/shard_map/ppermute | solution.py:173
  31.4 8.5 %collective-permute-start.3 = (bf16[256,512]{1,0:T(8,128)(2,1)S(1)}, bf16[256,512]{1,0:T(8,128)(2,1)S(1)}, u32[]{:S(2)}, u32[]{:S(2)}) collective-permute-start(bf16[256,512]{1,0:T(8,128)(2,1)S(1)} %collective-permute-done.2.refs_3_), channel_id=1, source_target_pairs={{0,8},{8,64},{64,72},{72,0},{1,9},{9,65},{65,73},{73,1},{2,10},{10... | collective-permute-start | bytes 786440 | tf_op jit(solution)/shard_map/ppermute | solution.py:173
  33.6 15.1 %collective-permute-start.15 = (bf16[512,512]{1,0:T(8,128)(2,1)S(1)}, bf16[512,512]{1,0:T(8,128)(2,1)S(1)}, u32[]{:S(2)}, u32[]{:S(2)}) collective-permute-start(bf16[512,512]{1,0:T(8,128)(2,1)S(1)} %bitcast.47), channel_id=1, source_target_pairs={{0,1},{1,0},{2,3},{3,2},{4,5},{5,4},{6,7},{7,6},{8,9},{9,8},{10,11... | collective-permute-start | bytes 1572872 | tf_op jit(solution)/shard_map/ppermute | solution.py:177
  38.0 8.9 %collective-permute-start.8 = (bf16[256,512]{1,0:T(8,128)(2,1)S(1)}, bf16[256,512]{1,0:T(8,128)(2,1)}, u32[]{:S(2)}, u32[]{:S(2)}) collective-permute-start(bf16[256,512]{1,0:T(8,128)(2,1)S(1)} %collective-permute-done.7.refs_9_), channel_id=1, source_target_pairs={{0,1},{1,0},{2,3},{3,2},{4,5},{5,4},{6,7},{7,6},{8,9},{9,8},{10,11... | collective-permute-start | bytes 786440 | tf_op jit(solution)/shard_map/ppermute | solution.py:177
  39.9 7.4 %collective-permute-start.4 = (bf16[256,512]{1,0:T(8,128)(2,1)S(1)}, bf16[256,512]{1,0:T(8,128)(2,1)}, u32[]{:S(2)}, u32[]{:S(2)}) collective-permute-start(bf16[256,512]{1,0:T(8,128)(2,1)S(1)} %collective-permute-done.3.refs_8_), channel_id=1, source_target_pairs={{0,1},{1,0},{2,3},{3,2},{4,5},{5,4},{6,7},{7,6},{8,9},{9,8},{10,11... | collective-permute-start | bytes 786440 | tf_op jit(solution)/shard_map/ppermute | solution.py:177
  44.6 3.5 %collective-permute-start.18 = (bf16[256,512]{1,0:T(8,128)(2,1)S(1)}, bf16[256,512]{1,0:T(8,128)(2,1)}, u32[]{:S(2)}, u32[]{:S(2)}) collective-permute-start(bf16[256,512]{1,0:T(8,128)(2,1)S(1)} %collective-permute-done.2.refs_3_), channel_id=1, source_target_pairs={{0,1},{1,0},{2,3},{3,2},{4,5},{5,4},{6,7},{7,6},{8,9},{9,8},{10,11... | collective-permute-start | bytes 786440 | tf_op jit(solution)/shard_map/ppermute | solution.py:177
  46.9 2.2 %collective-permute-start.16 = (bf16[512,512]{1,0:T(8,128)(2,1)S(1)}, bf16[512,512]{1,0:T(8,128)(2,1)S(1)}, u32[]{:S(2)}, u32[]{:S(2)}) collective-permute-start(bf16[512,512]{1,0:T(8,128)(2,1)S(1)} %collective-permute-done.1.refs_1_), channel_id=1, source_target_pairs={{0,1},{1,0},{2,3},{3,2},{4,5},{5,4},{6,7},{7,6},{8,9},{9,8},{10,11... | collective-permute-start | bytes 1572872 | tf_op jit(solution)/shard_map/ppermute | solution.py:177
  47.3 2.5 %collective-permute-start.17 = (bf16[512,512]{1,0:T(8,128)(2,1)S(1)}, bf16[512,512]{1,0:T(8,128)(2,1)S(1)}, u32[]{:S(2)}, u32[]{:S(2)}) collective-permute-start(bf16[512,512]{1,0:T(8,128)(2,1)S(1)} %collective-permute-done.5.refs_2_), channel_id=1, source_target_pairs={{0,1},{1,0},{2,3},{3,2},{4,5},{5,4},{6,7},{7,6},{8,9},{9,8},{10,11... | collective-permute-start | bytes 1572872 | tf_op jit(solution)/shard_map/ppermute | solution.py:177
  48.1 4.2 %collective-permute-start.20 = (bf16[512,512]{1,0:T(8,128)(2,1)}, bf16[512,512]{1,0:T(8,128)(2,1)S(1)}, u32[]{:S(2)}, u32[]{:S(2)}) collective-permute-start(bf16[512,512]{1,0:T(8,128)(2,1)} %collective-permute-done.12.refs_5_), channel_id=1, source_target_pairs={{0,1},{1,0},{2,3},{3,2},{4,5},{5,4},{6,7},{7,6},{8,9},{9,8},{10,11... | collective-permute-start | bytes 1572872 | tf_op jit(solution)/shard_map/ppermute | solution.py:177
  48.4 7.7 %collective-permute-start.23 = (bf16[1024,512]{1,0:T(8,128)(2,1)S(1)}, bf16[1024,512]{1,0:T(8,128)(2,1)}, u32[]{:S(2)}, u32[]{:S(2)}) collective-permute-start(bf16[1024,512]{1,0:T(8,128)(2,1)S(1)} %bitcast.41), channel_id=1, source_target_pairs={{0,1},{1,0},{2,3},{3,2},{4,5},{5,4},{6,7},{7,6},{8,9},{9,8},{10,11... | collective-permute-start | bytes 3145736 | tf_op jit(solution)/shard_map/ppermute | solution.py:177
  48.7 7.5 %collective-permute-start.10 = (bf16[1024,512]{1,0:T(8,128)(2,1)}, bf16[1024,512]{1,0:T(8,128)(2,1)}, u32[]{:S(2)}, u32[]{:S(2)}) collective-permute-start(bf16[1024,512]{1,0:T(8,128)(2,1)} %collective-permute-done.9.refs_24_), channel_id=1, source_target_pairs={{0,1},{1,0},{2,3},{3,2},{4,5},{5,4},{6,7},{7,6},{8,9},{9,8},{10,11... | collective-permute-start | bytes 3145736 | tf_op jit(solution)/shard_map/ppermute | solution.py:177
  49.1 7.1 %collective-permute-start.24 = (bf16[528,512]{1,0:T(8,128)(2,1)S(1)}, bf16[528,512]{1,0:T(8,128)(2,1)}, u32[]{:S(2)}, u32[]{:S(2)}) collective-permute-start(bf16[528,512]{1,0:T(8,128)(2,1)S(1)} %get-tuple-element.39.refs_21_), channel_id=1, source_target_pairs={{0,1},{1,0},{2,3},{3,2},{4,5},{5,4},{6,7},{7,6},{8,9},{9,8},{10,11... | collective-permute-start | bytes 1622024 | tf_op jit(solution)/shard_map/ppermute | solution.py:177
  49.8 5.6 %collective-permute-start.21 = (bf16[512,512]{1,0:T(8,128)(2,1)}, bf16[512,512]{1,0:T(8,128)(2,1)}, u32[]{:S(2)}, u32[]{:S(2)}) collective-permute-start(bf16[512,512]{1,0:T(8,128)(2,1)} %collective-permute-done.13.refs_6_), channel_id=1, source_target_pairs={{0,1},{1,0},{2,3},{3,2},{4,5},{5,4},{6,7},{7,6},{8,9},{9,8},{10,11... | collective-permute-start | bytes 1572872 | tf_op jit(solution)/shard_map/ppermute | solution.py:177
  53.1 3.1 %collective-permute-start.22 = (bf16[512,512]{1,0:T(8,128)(2,1)}, bf16[512,512]{1,0:T(8,128)(2,1)}, u32[]{:S(2)}, u32[]{:S(2)}) collective-permute-start(bf16[512,512]{1,0:T(8,128)(2,1)} %collective-permute-done.14.refs_7_), channel_id=1, source_target_pairs={{0,1},{1,0},{2,3},{3,2},{4,5},{5,4},{6,7},{7,6},{8,9},{9,8},{10,11... | collective-permute-start | bytes 1572872 | tf_op jit(solution)/shard_map/ppermute | solution.py:177
  (22 other events, 329.8 us)
